TPU v7x, 32 devices: a whole 2x2x4 slice. The times are simulated.
32 devices in a mesh: rows: 4 (over y, core), feat: 8 (over z, x).
Axes of the slice: x: 2, y: 2, z: 4, core: 2. Of those that a mesh axis runs over, the one named last changes fastest.
Arguments:
- samples: float32 [6144, 8192], P('rows', 'feat'), may hold values from -6 to 6
- whitening: float32 [8192, 1024], P('feat', 'rows'), may hold values from -0.09375 to 0.09375
- components: float32 [1024, 1024], P('rows', 'feat'), may hold values from -0.25 to 0.25
Outputs:
- moment: float32 [1024, 1024], P('rows', 'feat')
All inputs are finite; a program needn't handle non-finite values.
Results may differ from a plain program's by a relative error of at most 0.00017.
Values sent between devices are 32-bit elements; how exact they have to be, the bound alone decides.
No kernel may reach another device: no remote copies, remote signals or barrier semaphores. Data moves between devices by JAX's collectives and lax.ppermute only.
A program may use at most 64 MiB of HBM per device.

v0:
```python
import jax
import jax.numpy as jnp
from jax import lax
from jax.sharding import PartitionSpec as P


def on_device(samples, whitening, components):
    partial_y = jnp.dot(
        samples,
        lax.all_gather(whitening, "rows", axis=1, tiled=True),
        precision=lax.Precision.HIGHEST,
        preferred_element_type=jnp.float32,
    )
    whitened = lax.psum(partial_y, "feat")
    local_rows = whitened.shape[0]
    columns = whitened
    projected = jnp.dot(
        columns,
        lax.all_gather(components, "rows", axis=0, tiled=True),
        precision=lax.Precision.HIGHEST,
        preferred_element_type=jnp.float32,
    )
    squared = projected * projected
    scale_inv = 1.0 / jnp.sqrt(jnp.float32(local_rows * lax.axis_size("rows")))
    columns = whitened
    product = lax.dot_general(
        columns,
        squared,
        (((0,), (0,)), ((), ())),
        precision=lax.Precision.HIGHEST,
        preferred_element_type=jnp.float32,
    )
    return lax.psum_scatter(product * scale_inv, "rows", scatter_dimension=0, tiled=True)


def solution(mesh):
    placed = (P("rows", "feat"), P("feat", "rows"), P("rows", "feat"))
    return jax.shard_map(
        on_device, mesh=mesh, in_specs=placed, out_specs=P("rows", "feat"), check_vma=False
    )
```

profile of v0, /device:TPU:0, one launch (start us, length us, event | category | flops | bytes accessed | tf_op | source)
XLA Modules:
  0.0 328.8 jit_solution(7723023947166043347)
XLA Ops:
  6.5 0.0 all-gather.2.cloned.1.call-start
  6.5 0.7 all-gather.2.cloned.1.call-update
  7.3 0.0 all-reduce.2.cloned.1.call-start
  7.3 38.8 %all-gather.2.cloned.1.call-done = f32[1024,1024]{1,0:T(8,128)} async-done(((f32[1024,256]{1,0:T(8,128)}), f32[1024,1024]{1,0:T(8,128)}) %all-gather.2.cloned.1.call-update) | async-done | bytes 4194320 | tf_op jit(solution)/shard_map/all_gather | solution.py:10
  46.1 24.8 %fusion = f32[1536,1024]{1,0:T(8,128)} fusion(f32[1536,1024]{1,0:T(8,128)} %param.3, f32[1024,1024]{1,0:T(8,128)} %all-gather.2.cloned.1.call-done), kind=kOutput, calls=%fused_computation.2 | convolution fusion | flops 19327352832 | bytes 16777216 | tf_op jit(solution)/shard_map/dot_general | solution.py:8
  71.0 0.0 copy-start.1
  71.0 0.0 all-reduce.2.cloned.1.call-update
  71.0 0.0 reduce-scatter.2.cloned.1.call-start
  71.0 0.8 copy-done.1
  71.9 7.2 %all_gather.7 = f32[1024,128]{1,0:T(8,128)S(1)} all-gather(f32[256,128]{1,0:T(8,128)S(1)} %copy-done.1), channel_id=1, replica_groups=mesh['rows'=4,'feat'=8] {'rows'}, dimensions={0}, use_global_device_ids=true | all-gather | bytes 655360 | tf_op jit(solution)/shard_map/all_gather | solution.py:19
  79.0 203.6 %all-reduce.2.cloned.1.call-done = f32[1536,1024]{1,0:T(8,128)} async-done(((f32[1536,1024]{1,0:T(8,128)}), f32[1536,1024]{1,0:T(8,128)}) %all-reduce.2.cloned.1.call-update) | async-done | bytes 6291472 | tf_op jit(solution)/shard_map/psum | solution.py:14
  282.7 0.0 copy-start
  282.7 7.9 %convolution_multiply_fusion = f32[1536,128]{1,0:T(8,128)S(1)} fusion(f32[1536,1024]{1,0:T(8,128)} %all-reduce.2.cloned.1.call-done, f32[1024,128]{1,0:T(8,128)S(1)} %all_gather.7), kind=kOutput, calls=%fused_computation | convolution fusion | flops 2416115712 | bytes 7602176 | tf_op jit(solution)/shard_map/dot_general | solution.py:17
  290.6 0.0 copy-done
  290.6 10.9 %convolution_multiply_fusion.1 = f32[1024,128]{1,0:T(8,128)} fusion(f32[1536,1024]{1,0:T(8,128)S(1)} %copy-done, f32[1536,128]{1,0:T(8,128)S(1)} %convolution_multiply_fusion), kind=kOutput, calls=%fused_computation.1 | convolution fusion | flops 2416050176 | bytes 7602176 | tf_op jit(solution)/shard_map/dot_general | solution.py:26
  301.5 0.0 reduce-scatter.2.cloned.1.call-update
  301.5 20.8 %reduce-scatter.2.cloned.1.call-done = f32[256,128]{1,0:T(8,128)} async-done(((f32[1024,128]{1,0:T(8,128)}), f32[256,128]{1,0:T(8,128)}) %reduce-scatter.2.cloned.1.call-update) | async-done | bytes 131088 | tf_op jit(solution)/shard_map/reduce_scatter | solution.py:33
Async XLA Ops:
  6.5 39.6 %all-gather.2.cloned.1.call-start = ((), (), s32[]{:S(2)}) async-start(), calls=%async_computation.1 | async-start | bytes 5242880 | tf_op jit(solution)/shard_map/all_gather | solution.py:10
  7.3 275.4 %all-reduce.2.cloned.1.call-start = ((), (), s32[]{:S(2)}) async-start(), calls=%async_computation.2 | async-start | bytes 12582912 | tf_op jit(solution)/shard_map/psum | solution.py:14
  71.0 0.9 copy-start.1
  71.0 251.3 %reduce-scatter.2.cloned.1.call-start = ((), (), s32[]{:S(2)}) async-start(), calls=%async_computation.3 | async-start | bytes 655360 | tf_op jit(solution)/shard_map/reduce_scatter | solution.py:33
  282.7 7.9 %copy-start = (f32[1536,1024]{1,0:T(8,128)S(1)}, f32[1536,1024]{1,0:T(8,128)}, u32[]{:S(2)}) copy-start(f32[1536,1024]{1,0:T(8,128)} %all-reduce.2.cloned.1.call-done) | copy-start | bytes 18874372
Sparse Core Ops, SparseCore 0:
  8.9 37.1 all-gather.1
  71.1 211.5 all-reduce.1
  301.6 20.6 reduce-scatter.1
where the time goes:
time: 329 us
  waiting for transfers between devices  264 us (80%)
  matrix products  43.6 us (13%)
  between operations  13.1 us (4%)
  blocking collectives  7.18 us (2%)
    psum x1, waiting for transfers between devices, on_device(): whitened = lax.psum(partial_y, 'feat')  204 us
    all_gather x1, waiting for transfers between devices, on_device(): lax.all_gather(whitening, 'rows', axis=1, tiled=True)  38.8 us
    dot_general x1, matrix products, on_device(): jnp.dot(samples, lax.all_gather(whitening, 'rows', axis=1, tiled=True), p...  24.8 us
    reduce_scatter x1, waiting for transfers between devices, on_device(): lax.psum_scatter(product * scale_inv, 'rows', scatter_dimension=0, tiled=...  20.8 us
    dot_general x1, matrix products, on_device(): lax.dot_general(columns, squared, (((0,), (0,)), ((), ())), precision=lax...  10.9 us
    dot_general x1, matrix products, on_device(): jnp.dot(columns, lax.all_gather(components, 'rows', axis=0, tiled=True),...  7.89 us
    all_gather x1, blocking collectives, on_device(): lax.all_gather(components, 'rows', axis=0, tiled=True)  7.18 us
  transfers between devices with their start and end apart: 3, of which 3 were waited for; matrix products, arithmetic and copies ran while one was open for 0% of the time, Pallas kernels for 0%

commit v1 on v0

v1 whole, which is shorter than its diff:
```python
import functools

import jax
import jax.numpy as jnp
from jax import lax
from jax.experimental import pallas as pl
from jax.experimental.pallas import tpu as pltpu
from jax.sharding import PartitionSpec as P

VMEM_BYTES = 56 * 2**20


def cycle_of(mesh):
    line = list(mesh.devices[0])
    points = [tuple(d.coords) for d in line]
    moving = [a for a in range(len(points[0])) if len({p[a] for p in points}) > 1]
    if len(moving) != 2:
        return list(range(len(line)))
    inner = min(moving, key=lambda a: len({p[a] for p in points}))
    outer = moving[0] if inner == moving[1] else moving[1]
    at = {(p[outer], p[inner]): i for i, p in enumerate(points)}
    outers, inners = sorted({p[outer] for p in points}), sorted({p[inner] for p in points})
    walk = [at[o, inners[0]] for o in outers]
    for turn, o in enumerate(reversed(outers)):
        walk += [at[o, i] for i in (inners[1:] if turn % 2 == 0 else inners[:0:-1])]
    return walk


def split(a):
    high = a.astype(jnp.bfloat16)
    return high, (a - high.astype(jnp.float32)).astype(jnp.bfloat16)


def dot3(a, b, over=((1,), (0,))):
    def one(x, y):
        return lax.dot_general(x, y, (over, ((), ())), preferred_element_type=jnp.float32)

    return one(a[0], b[0]) + (one(a[0], b[1]) + one(a[1], b[0]))


def fill(high_ref, low_ref, refs):
    at = 0
    for ref in refs:
        width = ref.shape[1]
        high_ref[:, at : at + width], low_ref[:, at : at + width] = split(ref[...])
        at += width


def partial_kernel(samples_ref, *refs):
    *blocks, out_ref, high_ref, low_ref = refs

    @pl.when(pl.program_id(0) == 0)
    def _():
        fill(high_ref, low_ref, blocks)

    out_ref[...] = dot3(split(samples_ref[...]), (high_ref[...], low_ref[...]))


def partial_sums(samples, blocks, cost):
    rows, depth = samples.shape
    width = sum(b.shape[1] for b in blocks)
    tile = rows // 4 if rows % 32 == 0 else rows
    return pl.pallas_call(
        partial_kernel,
        out_shape=jax.ShapeDtypeStruct((rows, width), jnp.float32),
        grid=(rows // tile,),
        in_specs=[pl.BlockSpec((tile, depth), lambda i: (i, 0))]
        + [pl.BlockSpec(b.shape, lambda i: (0, 0)) for b in blocks],
        out_specs=pl.BlockSpec((tile, width), lambda i: (i, 0)),
        scratch_shapes=[pltpu.VMEM((depth, width), jnp.bfloat16)] * 2,
        compiler_params=pltpu.CompilerParams(vmem_limit_bytes=VMEM_BYTES),
        cost_estimate=pl.CostEstimate(
            flops=cost * 2 * rows * depth * width, bytes_accessed=4 * rows * (depth + width), transcendentals=0
        ),
    )(samples, *blocks)


def near_kernel(near_ref, *refs):
    *blocks, projected_ref, high_ref, low_ref, turned_high_ref, turned_low_ref = refs
    height = blocks[0].shape[0]
    near = split(near_ref[...])
    turned_high_ref[...], turned_low_ref[...] = near[0].T, near[1].T
    total = 0.0
    for k, block in enumerate(blocks):
        parts = split(block[...])
        if k < 2:
            mine = slice(k * height, (k + 1) * height)
            total = total + dot3((near[0][:, mine], near[1][:, mine]), parts)
        else:
            at = (k - 2) * height
            high_ref[at : at + height, :], low_ref[at : at + height, :] = parts
    projected_ref[...] = total


def near_terms(near, blocks):
    rows, depth = near.shape
    height, width = blocks[0].shape
    rest = height * (len(blocks) - 2)
    tile = width // 4 if width % 512 == 0 else width
    whole = lambda j: (0, 0)
    column = lambda j: (0, j)
    return pl.pallas_call(
        near_kernel,
        out_shape=[jax.ShapeDtypeStruct((rows, width), jnp.float32)]
        + [jax.ShapeDtypeStruct((rest, width), jnp.bfloat16)] * 2
        + [jax.ShapeDtypeStruct((depth, rows), jnp.bfloat16)] * 2,
        grid=(width // tile,),
        in_specs=[pl.BlockSpec(near.shape, whole)] + [pl.BlockSpec((height, tile), column) for _ in blocks],
        out_specs=[pl.BlockSpec((rows, tile), column)]
        + [pl.BlockSpec((rest, tile), column)] * 2
        + [pl.BlockSpec((depth, rows), whole)] * 2,
        compiler_params=pltpu.CompilerParams(vmem_limit_bytes=VMEM_BYTES),
        cost_estimate=pl.CostEstimate(
            flops=6 * rows * depth * width, bytes_accessed=12 * rest * width, transcendentals=0
        ),
    )(near, *blocks)


def moment_kernel(
    scale_inv, far_ref, projected_ref, comp_high_ref, comp_low_ref, near_high_ref, near_low_ref,
    kept_ref, sent_ref, high_ref, low_ref, turned_high_ref, turned_low_ref,
):
    @pl.when(pl.program_id(0) == 0)
    def _():
        high, low = split(far_ref[...])
        high_ref[...], low_ref[...] = high, low
        turned_high_ref[...], turned_low_ref[...] = high.T, low.T

    projected = projected_ref[...] + dot3(
        (high_ref[...], low_ref[...]), (comp_high_ref[...], comp_low_ref[...])
    )
    squared = split(projected * projected)
    pairs = ((near_high_ref, near_low_ref), (turned_high_ref, turned_low_ref))
    for out_ref, first in ((sent_ref, 1), (kept_ref, 0)):
        at = 0
        for high, low in pairs:
            width = high.shape[0] // 2
            mine = slice(first * width, (first + 1) * width)
            out_ref[at : at + width, :] = scale_inv * dot3((high[mine, :], low[mine, :]), squared)
            at += width


def moments(far, near_side, scale_inv):
    projected, comp_high, comp_low, near_high, near_low = near_side
    rows, width = projected.shape
    depth = near_high.shape[0] + far.shape[1]
    tile = width // 4 if width % 512 == 0 else width
    whole = lambda j: (0, 0)
    column = lambda j: (0, j)
    return pl.pallas_call(
        functools.partial(moment_kernel, scale_inv),
        out_shape=[jax.ShapeDtypeStruct((depth // 2, width), jnp.float32)] * 2,
        grid=(width // tile,),
        in_specs=[
            pl.BlockSpec(far.shape, whole),
            pl.BlockSpec((rows, tile), column),
            pl.BlockSpec((comp_high.shape[0], tile), column),
            pl.BlockSpec((comp_low.shape[0], tile), column),
            pl.BlockSpec(near_high.shape, whole),
            pl.BlockSpec(near_low.shape, whole),
        ],
        out_specs=[pl.BlockSpec((depth // 2, tile), column)] * 2,
        scratch_shapes=[pltpu.VMEM(far.shape, jnp.bfloat16)] * 2
        + [pltpu.VMEM(far.shape[::-1], jnp.bfloat16)] * 2,
        compiler_params=pltpu.CompilerParams(vmem_limit_bytes=VMEM_BYTES),
        cost_estimate=pl.CostEstimate(
            flops=12 * rows * depth * width, bytes_accessed=12 * depth * width, transcendentals=0
        ),
    )(far, *near_side)


def solution(mesh):
    n_rows, n_feat = mesh.shape["rows"], mesh.shape["feat"]
    cycle = cycle_of(mesh)
    place = [cycle.index(i) for i in range(n_feat)]
    onward = [(cycle[i], cycle[(i + 1) % n_feat]) for i in range(n_feat)]
    backward = [(b, a) for a, b in onward]
    high_bits = [1 << b for b in range(1, n_rows.bit_length() - 1)]

    def swap(a, bit):
        return lax.ppermute(a, "rows", [(i, i ^ bit) for i in range(n_rows)])

    def total_over_feat(a, dim):
        return lax.psum_scatter(
            a, "feat", scatter_dimension=dim, tiled=True, axis_index_groups=[cycle]
        )

    def ring_components(own, far):
        ahead, behind = [own], [own]
        for step in range(1, n_feat):
            if step == 3:
                far, ahead, behind = lax.optimization_barrier((far, ahead, behind))
            if step % 2:
                ahead.append(lax.ppermute(ahead[-1], "feat", onward))
            else:
                behind.append(lax.ppermute(behind[-1], "feat", backward))
        line = jnp.concatenate(ahead[::-1] + behind[1:], axis=1)
        first = (jnp.asarray(place)[lax.axis_index("feat")] - (len(ahead) - 1)) % n_feat
        return jnp.roll(line, first * own.shape[1], axis=1), far

    def over_high_bits(own):
        blocks = [own]
        for bit in high_bits:
            blocks += [swap(block, bit) for block in blocks]
        return blocks

    def on_device(samples, whitening, components):
        far = over_high_bits(whitening)[1:]
        near_part = partial_sums(samples, [whitening, swap(whitening, 1)], 40)
        near_sum = total_over_feat(near_part, 0)
        line, far = ring_components(components, far)
        far_part = partial_sums(samples, far + [swap(block, 1) for block in far], 15)
        far_sum = total_over_feat(far_part, 0)
        lines = over_high_bits(line)
        others = [swap(block, 1) for block in lines]
        blocks = [lines[0], others[0]] + lines[1:] + others[1:]
        scale_inv = float((samples.shape[0] * n_rows) ** -0.5)
        kept, sent = moments(far_sum, near_terms(near_sum, blocks), scale_inv)
        total = total_over_feat(kept + swap(sent, 1), 1)
        total = total.reshape(n_rows // 2, -1, total.shape[1])
        for bit in high_bits[::-1]:
            half = total.shape[0] // 2
            total = total[:half] + swap(total[half:], bit)
        return total[0]

    placed = (P("rows", "feat"), P("feat", "rows"), P("rows", "feat"))
    return jax.shard_map(
        on_device, mesh=mesh, in_specs=placed, out_specs=P("rows", "feat"), check_vma=False
    )
```

time: 329 us -> 176 us (0.53)
  waiting for transfers between devices: 264 us -> 106 us
  matrix products: 43.6 us -> 0 us
  Pallas kernels: 0 us -> 31.1 us
  starting transfers between devices: 0.08 us -> 14.6 us
  blocking collectives: 7.18 us -> 0 us
  other arithmetic: 0 us -> 4.85 us
  local copies, waits for them, and re-layouts: 0.83 us -> 5.04 us
    psum x1 -> x0, waiting for transfers between devices: 204 us -> none  [on_device(): whitened = lax.psum(partial_y, 'feat')]
    ppermute x0 -> x15, waiting for transfers between devices: none -> 72.2 us  [the longest x8 51.2 us: swap(): return lax.ppermute(a, 'rows', [(i, i ^ bit) for i in range(n_rows)])]
    dot_general x3 -> x0, matrix products: 43.6 us -> none  [the longest x1 24.8 us: on_device(): jnp.dot(samples, lax.all_gather(whitening, 'rows', axis=1, tiled=True), p...]
    all_gather x1 -> x0, waiting for transfers between devices: 38.8 us -> none  [on_device(): lax.all_gather(whitening, 'rows', axis=1, tiled=True)]
    pallas_call x0 -> x4, Pallas kernels: none -> 31.1 us  [the longest x2 18.4 us: partial_sums(): pl.pallas_call(partial_kernel, out_shape=jax.ShapeDtypeStruct((rows, widt...]
    ppermute x0 -> x15, starting transfers between devices: none -> 14.5 us  [the longest x4 7.64 us: ring_components(): ahead.append(lax.ppermute(ahead[-1], 'feat', onward))]
    reduce_scatter x1 -> x3, waiting for transfers between devices: 20.8 us -> 33.3 us  [total_over_feat(): lax.psum_scatter(a, 'feat', scatter_dimension=dim, tiled=True, axis_index...]
    all_gather x1 -> x0, blocking collectives: 7.18 us -> none  [on_device(): lax.all_gather(components, 'rows', axis=0, tiled=True)]
  transfers between devices with their start and end apart: 3 -> 18, of which waited for: 3 -> 14; matrix products, arithmetic and copies ran while one was open for 0% -> 0% of each run, Pallas kernels for 0% -> 8%
where the time goes in v1:
time: 176 us; the launch traced here: 175 us
  waiting for transfers between devices  106 us (60%)
  Pallas kernels  31.1 us (18%)
  starting transfers between devices  14.6 us (8%)
  between operations  14 us (8%)
  local copies, waits for them, and re-layouts  5.04 us (3%)
  other arithmetic  4.85 us (3%)
    ppermute x8, waiting for transfers between devices, swap(): return lax.ppermute(a, 'rows', [(i, i ^ bit) for i in range(n_rows)])  51.2 us
    reduce_scatter x3, waiting for transfers between devices, total_over_feat(): lax.psum_scatter(a, 'feat', scatter_dimension=dim, tiled=True, axis_index...  33.3 us
    pallas_call x2, Pallas kernels, partial_sums(): pl.pallas_call(partial_kernel, out_shape=jax.ShapeDtypeStruct((rows, widt...  18.4 us
    ppermute x4, waiting for transfers between devices, ring_components(): ahead.append(lax.ppermute(ahead[-1], 'feat', onward))  16 us
    ppermute x4, starting transfers between devices, ring_components(): ahead.append(lax.ppermute(ahead[-1], 'feat', onward))  7.64 us
    pallas_call x1, Pallas kernels, moments(): pl.pallas_call(functools.partial(moment_kernel, scale_inv), out_shape=[ja...  7.47 us
    ppermute x8, starting transfers between devices, swap(): return lax.ppermute(a, 'rows', [(i, i ^ bit) for i in range(n_rows)])  6.07 us
    pallas_call x1, Pallas kernels, near_terms(): pl.pallas_call(near_kernel, out_shape=[jax.ShapeDtypeStruct((rows, width)...  5.31 us
  transfers between devices with their start and end apart: 18, of which 14 were waited for; matrix products, arithmetic and copies ran while one was open for 0% of the time, Pallas kernels for 8%

profile of v1, /device:TPU:0, one launch (start us, length us, event | category | flops | bytes accessed | tf_op | source)
XLA Modules:
  0.0 175.2 jit_solution(18216320677982514342)
XLA Ops:
  6.5 0.5 collective-permute-start.4
  7.0 2.5 %collective-permute-done.4.refs_1_ = f32[1024,256]{1,0:T(8,128)S(1)} collective-permute-done((f32[1024,256]{1,0:T(8,128)}, f32[1024,256]{1,0:T(8,128)S(1)}, u32[]{:S(2)}, u32[]{:S(2)}) %collective-permute-start.4) | collective-permute-done | bytes 1048608 | tf_op jit(solution)/shard_map/ppermute | solution.py:181
  9.5 1.0 copy-done.7
  10.5 9.2 %shard_map.47 = f32[1536,512]{1,0:T(8,128)} custom-call(f32[1536,1024]{1,0:T(8,128)} %samples_ref.3, f32[1024,256]{1,0:T(8,128)} %refs_0_.1, f32[1024,256]{1,0:T(8,128)} %copy-done.7), custom_call_target="tpu_custom_call" | custom-call | flops 64424509440 | bytes 9437184 | tf_op jit(solution)/shard_map/pallas_call | solution.py:63
  19.7 0.0 reduce-scatter.6.cloned.1.call-update
  19.7 0.0 reduce-scatter.4.cloned.1.call-start
  19.7 1.1 copy-done.4
  20.9 2.9 %collective-permute-start = (f32[1024,256]{1,0:T(8,128)S(1)}, f32[1024,256]{1,0:T(8,128)S(1)}, u32[]{:S(2)}, u32[]{:S(2)}) collective-permute-start(f32[1024,256]{1,0:T(8,128)S(1)} %copy-done.4), channel_id=1, source_target_pairs={{0,16},{8,24},{16,0},{24,8},{1,17},{9,25},{17,1},{25,9},{2,18},{10... | collective-permute-start | bytes 3145736 | tf_op jit(solution)/shard_map/ppermute | solution.py:181
  23.8 1.5 collective-permute-start.1
  25.4 0.5 collective-permute-start.2
  25.8 3.2 %collective-permute-done.1 = f32[256,128]{1,0:T(8,128)S(1)} collective-permute-done((f32[256,128]{1,0:T(8,128)S(1)}, f32[256,128]{1,0:T(8,128)S(1)}, u32[]{:S(2)}, u32[]{:S(2)}) %collective-permute-start.1) | collective-permute-done | bytes 131104 | tf_op jit(solution)/shard_map/ppermute | solution.py:194
  29.0 1.3 collective-permute-done.2
  30.3 16.9 %collective-permute-done.refs_0_ = f32[1024,256]{1,0:T(8,128)S(1)} collective-permute-done((f32[1024,256]{1,0:T(8,128)S(1)}, f32[1024,256]{1,0:T(8,128)S(1)}, u32[]{:S(2)}, u32[]{:S(2)}) %collective-permute-start) | collective-permute-done | bytes 1048608 | tf_op jit(solution)/shard_map/ppermute | solution.py:181
  47.2 0.0 collective-permute-start.3
  47.2 2.7 %collective-permute-done.3.refs_1_ = f32[1024,256]{1,0:T(8,128)S(1)} collective-permute-done((f32[1024,256]{1,0:T(8,128)S(1)}, f32[1024,256]{1,0:T(8,128)S(1)}, u32[]{:S(2)}, u32[]{:S(2)}) %collective-permute-start.3) | collective-permute-done | bytes 1048608 | tf_op jit(solution)/shard_map/ppermute | solution.py:181
  49.9 1.1 copy-done.6
  51.0 9.2 %shard_map.46 = f32[1536,512]{1,0:T(8,128)} custom-call(f32[1536,1024]{1,0:T(8,128)} %samples_ref.3, f32[1024,256]{1,0:T(8,128)} %copy-done.5, f32[1024,256]{1,0:T(8,128)} %copy-done.6), custom_call_target="tpu_custom_call" | custom-call | flops 24159191040 | bytes 9437184 | tf_op jit(solution)/shard_map/pallas_call | solution.py:63
  60.2 0.0 reduce-scatter.4.cloned.1.call-update
  60.2 0.0 reduce-scatter.8.cloned.1.call-start
  60.3 1.8 %collective-permute-start.5 = (f32[256,128]{1,0:T(8,128)S(1)}, f32[256,128]{1,0:T(8,128)S(1)}, u32[]{:S(2)}, u32[]{:S(2)}) collective-permute-start(f32[256,128]{1,0:T(8,128)S(1)} %collective-permute-done.1), channel_id=1, source_target_pairs={{0,2},{2,4},{4,6},{6,7},{7,5},{5,3},{3,1},{1,0},{8,10},{10,12},{12... | collective-permute-start | bytes 393224 | tf_op jit(solution)/shard_map/ppermute | solution.py:194
  62.1 3.8 %collective-permute-done.5 = f32[256,128]{1,0:T(8,128)S(1)} collective-permute-done((f32[256,128]{1,0:T(8,128)S(1)}, f32[256,128]{1,0:T(8,128)S(1)}, u32[]{:S(2)}, u32[]{:S(2)}) %collective-permute-start.5) | collective-permute-done | bytes 131104 | tf_op jit(solution)/shard_map/ppermute | solution.py:194
  65.9 1.8 %collective-permute-start.6 = (f32[256,128]{1,0:T(8,128)S(1)}, f32[256,128]{1,0:T(8,128)S(1)}, u32[]{:S(2)}, u32[]{:S(2)}) collective-permute-start(f32[256,128]{1,0:T(8,128)S(1)} %collective-permute-done.5), channel_id=1, source_target_pairs={{0,2},{2,4},{4,6},{6,7},{7,5},{5,3},{3,1},{1,0},{8,10},{10,12},{12... | collective-permute-start | bytes 393224 | tf_op jit(solution)/shard_map/ppermute | solution.py:194
  67.7 0.2 collective-permute-start.8
  67.9 4.9 %collective-permute-done.6 = f32[256,128]{1,0:T(8,128)S(1)} collective-permute-done((f32[256,128]{1,0:T(8,128)S(1)}, f32[256,128]{1,0:T(8,128)S(1)}, u32[]{:S(2)}, u32[]{:S(2)}) %collective-permute-start.6) | collective-permute-done | bytes 131104 | tf_op jit(solution)/shard_map/ppermute | solution.py:194
  72.8 2.5 %collective-permute-start.7 = (f32[256,128]{1,0:T(8,128)S(1)}, f32[256,128]{1,0:T(8,128)S(1)}, u32[]{:S(2)}, u32[]{:S(2)}) collective-permute-start(f32[256,128]{1,0:T(8,128)S(1)} %collective-permute-done.6), channel_id=1, source_target_pairs={{0,2},{2,4},{4,6},{6,7},{7,5},{5,3},{3,1},{1,0},{8,10},{10,12},{12... | collective-permute-start | bytes 393224 | tf_op jit(solution)/shard_map/ppermute | solution.py:194
  75.3 0.6 dynamic_slice.7
  76.6 0.0 collective-permute-done.8
  76.6 0.1 collective-permute-start.9
  76.7 4.1 %collective-permute-done.7 = f32[256,128]{1,0:T(8,128)S(1)} collective-permute-done((f32[256,128]{1,0:T(8,128)S(1)}, f32[256,128]{1,0:T(8,128)S(1)}, u32[]{:S(2)}, u32[]{:S(2)}) %collective-permute-start.7) | collective-permute-done | bytes 131104 | tf_op jit(solution)/shard_map/ppermute | solution.py:194
  80.9 3.7 %collective-permute-done.9 = f32[256,128]{1,0:T(8,128)S(1)} collective-permute-done((f32[256,128]{1,0:T(8,128)S(1)}, f32[256,128]{1,0:T(8,128)S(1)}, u32[]{:S(2)}, u32[]{:S(2)}) %collective-permute-start.9) | collective-permute-done | bytes 131104 | tf_op jit(solution)/shard_map/ppermute | solution.py:196
  84.8 0.1 constant_dynamic-slice_fusion.refs_0_
  84.9 1.0 collective-permute-start.11
  85.9 18.6 %collective-permute-done.11.refs_2_ = f32[256,1024]{1,0:T(8,128)S(1)} collective-permute-done((f32[256,1024]{1,0:T(8,128)S(1)}, f32[256,1024]{1,0:T(8,128)S(1)}, u32[]{:S(2)}, u32[]{:S(2)}) %collective-permute-start.11) | collective-permute-done | bytes 1048608 | tf_op jit(solution)/shard_map/ppermute | solution.py:181
  104.5 0.0 collective-permute-start.12
  104.5 0.0 collective-permute-done.10.refs_1_
  104.5 2.8 %collective-permute-done.12.refs_3_ = f32[256,1024]{1,0:T(8,128)} collective-permute-done((f32[256,1024]{1,0:T(8,128)S(1)}, f32[256,1024]{1,0:T(8,128)}, u32[]{:S(2)}, u32[]{:S(2)}) %collective-permute-start.12) | collective-permute-done | bytes 1048608 | tf_op jit(solution)/shard_map/ppermute | solution.py:181
  107.3 5.3 %shard_map.48 = (f32[192,1024]{1,0:T(8,128)}, bf16[512,1024]{1,0:T(8,128)(2,1)}, bf16[512,1024]{1,0:T(8,128)(2,1)}, bf16[512,192]{1,0:T(8,128)(2,1)}, bf16[512,192]{1,0:T(8,128)(2,1)}) custom-call(f32[192,512]{1,0:T(8,128)} %reduce-scatter.6.cloned.1.call-done.near_ref, f32[256,1024]{1,0:T(8,128)} %copy-done, f32[256,1024]{1,0:T(8,128)} %copy-done.2, ...), custom_call_target="tpu_custom_call" | custom-call | flops 603979776 | bytes 6291456 | tf_op jit(solution)/shard_map/pallas_call | solution.py:102
  112.6 0.0 reduce-scatter.4.cloned.1.call-done.far_ref
  112.7 7.5 %shard_map.49 = (f32[512,1024]{1,0:T(8,128)}, f32[512,1024]{1,0:T(8,128)}) custom-call(f32[192,512]{1,0:T(8,128)} %reduce-scatter.4.cloned.1.call-done.far_ref, f32[192,1024]{1,0:T(8,128)} %get-tuple-element.20.projected_ref, bf16[512,1024]{1,0:T(8,128)(2,1)} %get-tuple-element.21.comp_high_ref, bf16[512,1024]{1,0:T(8,128)(2,1)} %get-tuple-element.22.comp_low_ref, ...), custom_call_target="tpu_custom_call" | custom-call | flops 2415919104 | bytes 12582912 | tf_op jit(solution)/shard_map/pallas_call | solution.py:150
  120.1 0.1 collective-permute-start.13
  120.3 4.2 %collective-permute-done.13 = f32[512,1024]{1,0:T(8,128)S(1)} collective-permute-done((f32[512,1024]{1,0:T(8,128)}, f32[512,1024]{1,0:T(8,128)S(1)}, u32[]{:S(2)}, u32[]{:S(2)}) %collective-permute-start.13) | collective-permute-done | bytes 2097184 | tf_op jit(solution)/shard_map/ppermute | solution.py:181
  124.5 3.3 %add.35 = f32[512,1024]{1,0:T(8,128)} add(f32[512,1024]{1,0:T(8,128)} %get-tuple-element.25, f32[512,1024]{1,0:T(8,128)S(1)} %collective-permute-done.13) | non-fusion elementwise | flops 524288 | bytes 6291456 | tf_op jit(solution)/shard_map/add | solution.py:219
  127.8 0.0 reduce-scatter.8.cloned.1.call-update
  127.8 33.3 %reduce-scatter.8.cloned.1.call-done = f32[512,128]{1,0:T(8,128)} async-done(((f32[512,1024]{1,0:T(8,128)}), f32[512,128]{1,0:T(8,128)}) %reduce-scatter.8.cloned.1.call-update) | async-done | bytes 262160 | tf_op jit(solution)/shard_map/reduce_scatter | solution.py:184
  161.1 0.9 slice_bitcast_fusion
  162.1 1.6 collective-permute-start.14
  163.6 3.5 %collective-permute-done.14 = f32[1,256,128]{2,1,0:T(8,128)S(1)} collective-permute-done((f32[1,256,128]{2,1,0:T(8,128)S(1)}, f32[1,256,128]{2,1,0:T(8,128)S(1)}, u32[]{:S(2)}, u32[]{:S(2)}) %collective-permute-start.14) | collective-permute-done | bytes 131104 | tf_op jit(solution)/shard_map/ppermute | solution.py:181
  167.1 1.6 fusion.1
  (34 shorter events, 0.2 us)
Async XLA Ops:
  6.5 100.8 %reduce-scatter.6.cloned.1.call-start = ((), (), s32[]{:S(2)}) async-start(), calls=%async_computation.4 | async-start | bytes 3538944 | tf_op jit(solution)/shard_map/reduce_scatter | solution.py:184
  6.5 3.0 %collective-permute-start.4 = (f32[1024,256]{1,0:T(8,128)}, f32[1024,256]{1,0:T(8,128)S(1)}, u32[]{:S(2)}, u32[]{:S(2)}) collective-permute-start(f32[1024,256]{1,0:T(8,128)} %refs_0_.1), channel_id=1, source_target_pairs={{0,8},{8,0},{16,24},{24,16},{1,9},{9,1},{17,25},{25,17},{2,10},{10... | collective-permute-start | bytes 3145736 | tf_op jit(solution)/shard_map/ppermute | solution.py:181
  9.5 1.0 copy-start.7
  19.7 1.2 copy-start.4
  19.7 4.1 %copy-start.3 = (f32[256,128]{1,0:T(8,128)S(1)}, f32[256,128]{1,0:T(8,128)}, u32[]{:S(2)}) copy-start(f32[256,128]{1,0:T(8,128)} %param.6) | copy-start | bytes 393220
  19.7 93.0 %reduce-scatter.4.cloned.1.call-start = ((), (), s32[]{:S(2)}) async-start(), calls=%async_computation.3 | async-start | bytes 3538944 | tf_op jit(solution)/shard_map/reduce_scatter | solution.py:184
  20.9 26.4 %collective-permute-start = (f32[1024,256]{1,0:T(8,128)S(1)}, f32[1024,256]{1,0:T(8,128)S(1)}, u32[]{:S(2)}, u32[]{:S(2)}) collective-permute-start(f32[1024,256]{1,0:T(8,128)S(1)} %copy-done.4), channel_id=1, source_target_pairs={{0,16},{8,24},{16,0},{24,8},{1,17},{9,25},{17,1},{25,9},{2,18},{10... | collective-permute-start | bytes 3145736 | tf_op jit(solution)/shard_map/ppermute | solution.py:181
  23.8 5.2 %collective-permute-start.1 = (f32[256,128]{1,0:T(8,128)S(1)}, f32[256,128]{1,0:T(8,128)S(1)}, u32[]{:S(2)}, u32[]{:S(2)}) collective-permute-start(f32[256,128]{1,0:T(8,128)S(1)} %copy-done.3), channel_id=1, source_target_pairs={{0,2},{2,4},{4,6},{6,7},{7,5},{5,3},{3,1},{1,0},{8,10},{10,12},{12... | collective-permute-start | bytes 393224 | tf_op jit(solution)/shard_map/ppermute | solution.py:194
  25.4 5.0 %collective-permute-start.2 = (f32[256,128]{1,0:T(8,128)S(1)}, f32[256,128]{1,0:T(8,128)S(1)}, u32[]{:S(2)}, u32[]{:S(2)}) collective-permute-start(f32[256,128]{1,0:T(8,128)S(1)} %copy-done.3), channel_id=1, source_target_pairs={{2,0},{4,2},{6,4},{7,6},{5,7},{3,5},{1,3},{0,1},{10,8},{12,10},{14... | collective-permute-start | bytes 393224 | tf_op jit(solution)/shard_map/ppermute | solution.py:196
  47.2 2.7 %copy-start.5 = (f32[1024,256]{1,0:T(8,128)}, f32[1024,256]{1,0:T(8,128)S(1)}, u32[]{:S(2)}) copy-start(f32[1024,256]{1,0:T(8,128)S(1)} %collective-permute-done.refs_0_) | copy-start | bytes 3145732
  47.2 2.7 %collective-permute-start.3 = (f32[1024,256]{1,0:T(8,128)S(1)}, f32[1024,256]{1,0:T(8,128)S(1)}, u32[]{:S(2)}, u32[]{:S(2)}) collective-permute-start(f32[1024,256]{1,0:T(8,128)S(1)} %collective-permute-done.refs_0_), channel_id=1, source_target_pairs={{0,8},{8,0},{16,24},{24,16},{1,9},{9,1},{17,25},{25,17},{2,10},{10... | collective-permute-start | bytes 3145736 | tf_op jit(solution)/shard_map/ppermute | solution.py:181
  49.9 1.1 copy-start.6
  60.2 15.1 %copy-start.8 = (s32[8]{0:T(128)S(1)}, s32[8]{0:T(128)}, u32[]{:S(2)}) copy-start(s32[8]{0:T(128)} %constant.47.clone) | copy-start | bytes 100
  60.2 100.9 %reduce-scatter.8.cloned.1.call-start = ((), (), s32[]{:S(2)}) async-start(), calls=%async_computation.5 | async-start | bytes 2359296 | tf_op jit(solution)/shard_map/reduce_scatter | solution.py:184
  60.3 5.6 %collective-permute-start.5 = (f32[256,128]{1,0:T(8,128)S(1)}, f32[256,128]{1,0:T(8,128)S(1)}, u32[]{:S(2)}, u32[]{:S(2)}) collective-permute-start(f32[256,128]{1,0:T(8,128)S(1)} %collective-permute-done.1), channel_id=1, source_target_pairs={{0,2},{2,4},{4,6},{6,7},{7,5},{5,3},{3,1},{1,0},{8,10},{10,12},{12... | collective-permute-start | bytes 393224 | tf_op jit(solution)/shard_map/ppermute | solution.py:194
  65.9 6.9 %collective-permute-start.6 = (f32[256,128]{1,0:T(8,128)S(1)}, f32[256,128]{1,0:T(8,128)S(1)}, u32[]{:S(2)}, u32[]{:S(2)}) collective-permute-start(f32[256,128]{1,0:T(8,128)S(1)} %collective-permute-done.5), channel_id=1, source_target_pairs={{0,2},{2,4},{4,6},{6,7},{7,5},{5,3},{3,1},{1,0},{8,10},{10,12},{12... | collective-permute-start | bytes 393224 | tf_op jit(solution)/shard_map/ppermute | solution.py:194
  67.7 8.9 %collective-permute-start.8 = (f32[256,128]{1,0:T(8,128)S(1)}, f32[256,128]{1,0:T(8,128)S(1)}, u32[]{:S(2)}, u32[]{:S(2)}) collective-permute-start(f32[256,128]{1,0:T(8,128)S(1)} %collective-permute-done.2), channel_id=1, source_target_pairs={{2,0},{4,2},{6,4},{7,6},{5,7},{3,5},{1,3},{0,1},{10,8},{12,10},{14... | collective-permute-start | bytes 393224 | tf_op jit(solution)/shard_map/ppermute | solution.py:196
  72.8 7.9 %collective-permute-start.7 = (f32[256,128]{1,0:T(8,128)S(1)}, f32[256,128]{1,0:T(8,128)S(1)}, u32[]{:S(2)}, u32[]{:S(2)}) collective-permute-start(f32[256,128]{1,0:T(8,128)S(1)} %collective-permute-done.6), channel_id=1, source_target_pairs={{0,2},{2,4},{4,6},{6,7},{7,5},{5,3},{3,1},{1,0},{8,10},{10,12},{12... | collective-permute-start | bytes 393224 | tf_op jit(solution)/shard_map/ppermute | solution.py:194
  76.6 8.0 %collective-permute-start.9 = (f32[256,128]{1,0:T(8,128)S(1)}, f32[256,128]{1,0:T(8,128)S(1)}, u32[]{:S(2)}, u32[]{:S(2)}) collective-permute-start(f32[256,128]{1,0:T(8,128)S(1)} %collective-permute-done.8), channel_id=1, source_target_pairs={{2,0},{4,2},{6,4},{7,6},{5,7},{3,5},{1,3},{0,1},{10,8},{12,10},{14... | collective-permute-start | bytes 393224 | tf_op jit(solution)/shard_map/ppermute | solution.py:196
  84.9 22.4 %copy-start = (f32[256,1024]{1,0:T(8,128)}, f32[256,1024]{1,0:T(8,128)S(1)}, u32[]{:S(2)}) copy-start(f32[256,1024]{1,0:T(8,128)S(1)} %constant_dynamic-slice_fusion.refs_0_) | copy-start | bytes 3145732
  84.9 19.6 %collective-permute-start.11 = (f32[256,1024]{1,0:T(8,128)S(1)}, f32[256,1024]{1,0:T(8,128)S(1)}, u32[]{:S(2)}, u32[]{:S(2)}) collective-permute-start(f32[256,1024]{1,0:T(8,128)S(1)} %constant_dynamic-slice_fusion.refs_0_), channel_id=1, source_target_pairs={{0,16},{8,24},{16,0},{24,8},{1,17},{9,25},{17,1},{25,9},{2,18},{10... | collective-permute-start | bytes 3145736 | tf_op jit(solution)/shard_map/ppermute | solution.py:181
  85.9 18.7 %collective-permute-start.10 = (f32[256,1024]{1,0:T(8,128)S(1)}, f32[256,1024]{1,0:T(8,128)S(1)}, u32[]{:S(2)}, u32[]{:S(2)}) collective-permute-start(f32[256,1024]{1,0:T(8,128)S(1)} %constant_dynamic-slice_fusion.refs_0_), channel_id=1, source_target_pairs={{0,8},{8,0},{16,24},{24,16},{1,9},{9,1},{17,25},{25,17},{2,10},{10... | collective-permute-start | bytes 3145736 | tf_op jit(solution)/shard_map/ppermute | solution.py:181
  104.5 2.8 %copy-start.1 = (f32[256,1024]{1,0:T(8,128)}, f32[256,1024]{1,0:T(8,128)S(1)}, u32[]{:S(2)}) copy-start(f32[256,1024]{1,0:T(8,128)S(1)} %collective-permute-done.11.refs_2_) | copy-start | bytes 3145732
  104.5 2.8 %collective-permute-start.12 = (f32[256,1024]{1,0:T(8,128)S(1)}, f32[256,1024]{1,0:T(8,128)}, u32[]{:S(2)}, u32[]{:S(2)}) collective-permute-start(f32[256,1024]{1,0:T(8,128)S(1)} %collective-permute-done.11.refs_2_), channel_id=1, source_target_pairs={{0,8},{8,0},{16,24},{24,16},{1,9},{9,1},{17,25},{25,17},{2,10},{10... | collective-permute-start | bytes 3145736 | tf_op jit(solution)/shard_map/ppermute | solution.py:181
  104.5 2.8 %copy-start.2 = (f32[256,1024]{1,0:T(8,128)}, f32[256,1024]{1,0:T(8,128)S(1)}, u32[]{:S(2)}) copy-start(f32[256,1024]{1,0:T(8,128)S(1)} %collective-permute-done.10.refs_1_) | copy-start | bytes 3145732
  120.1 4.4 %collective-permute-start.13 = (f32[512,1024]{1,0:T(8,128)}, f32[512,1024]{1,0:T(8,128)S(1)}, u32[]{:S(2)}, u32[]{:S(2)}) collective-permute-start(f32[512,1024]{1,0:T(8,128)} %get-tuple-element.26), channel_id=1, source_target_pairs={{0,8},{8,0},{16,24},{24,16},{1,9},{9,1},{17,25},{25,17},{2,10},{10... | collective-permute-start | bytes 6291464 | tf_op jit(solution)/shard_map/ppermute | solution.py:181
  162.1 5.0 %collective-permute-start.14 = (f32[1,256,128]{2,1,0:T(8,128)S(1)}, f32[1,256,128]{2,1,0:T(8,128)S(1)}, u32[]{:S(2)}, u32[]{:S(2)}) collective-permute-start(f32[1,256,128]{2,1,0:T(8,128)S(1)} %slice_bitcast_fusion), channel_id=1, source_target_pairs={{0,16},{8,24},{16,0},{24,8},{1,17},{9,25},{17,1},{25,9},{2,18},{10... | collective-permute-start | bytes 393224 | tf_op jit(solution)/shard_map/ppermute | solution.py:181
Sparse Core Ops, SparseCore 0:
  19.8 41.3 reduce-scatter.5
  63.5 42.4 reduce-scatter.3
  127.9 33.1 reduce-scatter.7

commit v2 on v0

v2 whole, which is shorter than its diff:
```python
import functools

import jax
import jax.numpy as jnp
import numpy as np
from jax import lax
from jax.experimental import pallas as pl
from jax.experimental.pallas import tpu as pltpu
from jax.sharding import PartitionSpec as P

VMEM_BYTES = 56 * 2**20
NEAR_COST, FAR_COST = 40, 0
EARLY, PINS = 2, 2
TIE1, TIE2 = 2, 3
ROWS_OVER_ROWS = ((0,), (0,))
LANES_OVER_LANES = ((1,), (1,))


def cycle_of(mesh):
    line = list(mesh.devices[0])
    points = [tuple(d.coords) for d in line]
    moving = [a for a in range(len(points[0])) if len({p[a] for p in points}) > 1]
    if len(moving) != 2:
        return list(range(len(line)))
    inner = min(moving, key=lambda a: len({p[a] for p in points}))
    outer = moving[0] if inner == moving[1] else moving[1]
    at = {(p[outer], p[inner]): i for i, p in enumerate(points)}
    outers, inners = sorted({p[outer] for p in points}), sorted({p[inner] for p in points})
    walk = [at[o, inners[0]] for o in outers]
    for turn, o in enumerate(reversed(outers)):
        walk += [at[o, i] for i in (inners[1:] if turn % 2 == 0 else inners[:0:-1])]
    return walk


def split(a):
    high = a.astype(jnp.bfloat16)
    return high, (a - high.astype(jnp.float32)).astype(jnp.bfloat16)


def dot3(a, b, over=((1,), (0,))):
    def one(x, y):
        return lax.dot_general(x, y, (over, ((), ())), preferred_element_type=jnp.float32)

    return one(a[0], b[0]) + (one(a[0], b[1]) + one(a[1], b[0]))


def call(kernel, out_shape, table, *args, grid=(), in_specs=None, out_specs=None, scratch_shapes=(), flops=0):
    whole = lambda a: pl.BlockSpec(a.shape, lambda *_: (0,) * len(a.shape))
    outs = list(out_shape)
    return pl.pallas_call(
        kernel,
        out_shape=outs,
        grid_spec=pltpu.PrefetchScalarGridSpec(
            num_scalar_prefetch=1,
            grid=grid or (1,),
            in_specs=in_specs or [whole(a) for a in args],
            out_specs=out_specs or [whole(a) for a in outs],
            scratch_shapes=list(scratch_shapes),
        ),
        compiler_params=pltpu.CompilerParams(vmem_limit_bytes=VMEM_BYTES),
        cost_estimate=pl.CostEstimate(flops=flops, bytes_accessed=sum(4 * a.size for a in args), transcendentals=0),
    )(table, *args)


def f32(*shape):
    return jax.ShapeDtypeStruct(shape, jnp.float32)


def bf16(*shape):
    return jax.ShapeDtypeStruct(shape, jnp.bfloat16)


def partial_kernel(core_at, n_tiles, table, *refs):
    tiles, blocks, (out_ref, high_ref, low_ref) = refs[:n_tiles], refs[n_tiles:-3], refs[-3:]
    width = blocks[0].shape[1]
    for core in (0, 1):

        @pl.when((pl.program_id(0) == 0) & (table[core_at] == core))
        def _():
            for k, ref in enumerate(blocks):
                at = (k // 2 * 2 + (k % 2 ^ core)) * width
                high_ref[:, at : at + width], low_ref[:, at : at + width] = split(ref[...])

    rows = jnp.concatenate([ref[...] for ref in tiles], axis=0)
    out_ref[...] = dot3(split(rows), (high_ref[...], low_ref[...]))


def partial_sums(samples, blocks, table, pieces, core_at, cost):
    rows, depth = samples.shape
    width = sum(b.shape[1] for b in blocks)
    height = rows // pieces
    together = max(k for k in (1, 2, 4) if pieces % k == 0 and (k == 1 or height * k <= 384))

    def part(first, steps):
        return call(
            functools.partial(partial_kernel, core_at, together),
            [f32(height * together * steps, width)],
            table,
            *[samples] * together,
            *blocks,
            grid=(steps,),
            in_specs=[
                pl.BlockSpec((height, depth), lambda i, t, k=k: (t[(i + first) * together + k], 0))
                for k in range(together)
            ]
            + [pl.BlockSpec(b.shape, lambda i, t: (0, 0)) for b in blocks],
            out_specs=[pl.BlockSpec((height * together, width), lambda i, t: (i, 0))],
            scratch_shapes=[pltpu.VMEM((depth, width), jnp.bfloat16)] * 2,
            flops=cost * 2 * height * together * steps * depth * width,
        )[0]

    return part(0, 1), part(1, pieces // together - 1)


def near_kernel(order_at, table, *refs):
    *pieces, near_ref, far_ref, projected_ref, high_ref, low_ref, near_high_ref, near_low_ref = refs
    height = pieces[0].shape[0]
    for k, ref in enumerate(pieces):
        rows = slice(k * height, (k + 1) * height)
        near_high_ref[rows, :], near_low_ref[rows, :] = split(ref[...])
    n, height, _ = near_ref.shape
    near = []
    for k in range(n):
        at = table[order_at + k]
        near.append(near_ref[at])
        rows = slice(k * height, (k + 1) * height)
        high_ref[rows, :], low_ref[rows, :] = split(far_ref[at])
    near = split(jnp.concatenate(near, axis=0))
    projected_ref[...] = dot3(near, (near_high_ref[...], near_low_ref[...]), LANES_OVER_LANES)


def moment_kernel(scale_inv, n_high, table, *refs):
    projected_ref, comp_high_ref, comp_low_ref, near_high_ref, near_low_ref, *refs = refs
    *pieces, out0_ref, out1_ref, high_ref, low_ref = refs

    @pl.when(pl.program_id(0) == 0)
    def _():
        height = pieces[0].shape[0]
        for k, ref in enumerate(pieces):
            rows = slice(k * height, (k + 1) * height)
            high_ref[rows, :], low_ref[rows, :] = split(ref[...])

    projected = projected_ref[...] + dot3(
        (comp_high_ref[...], comp_low_ref[...]), (high_ref[...], low_ref[...]), LANES_OVER_LANES
    )
    squared = split(projected * projected)
    near = dot3(squared, (near_high_ref[...], near_low_ref[...])) * scale_inv
    far = dot3(squared, (high_ref[...], low_ref[...])) * scale_inv
    width = near.shape[1] // 2
    for core, ref in enumerate((out0_ref, out1_ref)):
        ref[:, :width] = near[:, core * width : (core + 1) * width]
        for h in range(1, n_high):
            at = (2 * (h - 1) + core) * width
            ref[:, h * width : (h + 1) * width] = far[:, at : at + width]


def divide_kernel(core_at, table, own_ref, *refs):
    *others, kept_ref, sent_ref = refs
    total = own_ref[...]
    for ref in others:
        total = total + ref[...]
    width = kept_ref.shape[1]
    for core in (0, 1):

        @pl.when(table[core_at] == core)
        def _():
            kept_ref[...] = total[:, core * width : (core + 1) * width]
            sent_ref[...] = total[:, (1 - core) * width : (2 - core) * width]


def assemble_kernel(core_at, table, own_ref, other_ref, out_ref):
    for core in (0, 1):

        @pl.when(table[core_at] == core)
        def _():
            pair = (own_ref[...], other_ref[...])
            out_ref[...] = jnp.concatenate(pair[:: 1 - 2 * core], axis=0).T


def solution(mesh):
    n_rows, n_feat = mesh.shape["rows"], mesh.shape["feat"]
    cycle = cycle_of(mesh)
    place = [cycle.index(i) for i in range(n_feat)]
    n_high = n_rows // 2
    high_bits = [1 << b for b in range(1, n_rows.bit_length() - 1)]
    both = ("rows", "feat")
    streams = [
        [
            (r * n_feat + cycle[i], r * n_feat + cycle[(i + (1 if r % 2 == s else -1)) % n_feat])
            for r in range(n_rows)
            for i in range(n_feat)
        ]
        for s in (0, 1)
    ]
    order = [j for j in range(n_feat) if j % 2 == 0] + [j for j in range(n_feat) if j % 2]
    pieces, reach = n_feat, n_feat // 2
    core_at, order_at = pieces, pieces + 1
    cut = max(1, reach // 2)
    held_order = [0, *range(1, cut + 1), *(n_feat - k for k in range(1, min(cut, reach - 1) + 1))]
    held_order += [*range(cut + 1, reach + 1), *(n_feat - k for k in range(cut + 1, reach))]
    facts = np.zeros((2, n_feat, order_at + n_feat), np.int32)
    for core in (0, 1):
        for f in range(n_feat):
            p, way = place[f], 1 - 2 * core
            for t in range(reach):
                facts[core, f, 2 * t] = (p + way * (reach - t)) % n_feat
                facts[core, f, 2 * t + 1] = (p - way * (reach - 1 - t)) % n_feat
            facts[core, f, core_at] = core
            for k, j in enumerate(order):
                away = way * (p - place[f ^ j]) % n_feat
                facts[core, f, order_at + k] = held_order.index(away)

    def swap(a, bit):
        return lax.ppermute(a, "rows", [(i, i ^ bit) for i in range(n_rows)])

    def swap_feat(a, bit):
        return lax.ppermute(a, "feat", [(i, i ^ bit) for i in range(n_feat)])

    def over_high_bits(own):
        blocks = [own]
        for bit in high_bits:
            blocks += [swap(block, bit) for block in blocks]
        return blocks

    def on_device(samples, whitening, components):
        core = lax.axis_index("rows") % 2
        table = lax.dynamic_slice(
            jnp.asarray(facts), (core, lax.axis_index("feat"), 0), (1, 1, facts.shape[2])
        ).reshape(-1)
        height = samples.shape[0] // pieces

        def rounds(part, first, last, held):
            for t in range(first, last):
                for s in (0, 1):
                    at = 2 * t + s
                    cut_at = part[0].shape[0] // height
                    source, at_row = (part[0], at) if at < cut_at else (part[1], at - cut_at)
                    piece = source[at_row * height : (at_row + 1) * height]
                    if t == 0:
                        held[s] = piece
                    elif at < n_feat:
                        held[s] = lax.ppermute(held[s], both, streams[s]) + piece
            return held

        far = over_high_bits(whitening)[1:]
        near_part = partial_sums(samples, [whitening, swap(whitening, 1)], table, pieces, core_at, NEAR_COST)

        turned = components.T
        turned = turned.reshape(2, turned.shape[0] // 2, -1)
        mine, others = (
            lax.dynamic_index_in_dim(turned, c, keepdims=False) for c in (core, 1 - core)
        )
        others = swap(others, 1)
        first = core == 0
        own = jnp.concatenate([jnp.where(first, mine, others), jnp.where(first, others, mine)], axis=1)
        line, groups = {0: own}, []

        def pass_components(first, last):
            for step in range(first, last):
                line[step] = lax.ppermute(line[step - 1], both, streams[0])
                if step < reach:
                    line[n_feat - step] = lax.ppermute(line[(n_feat - step + 1) % n_feat], both, streams[1])
                if step in (cut, reach):
                    done = sum(g.shape[0] for g in groups)
                    groups.append(jnp.stack([line[away] for away in held_order[done : len(line)]]))

        pass_components(1, 2)
        first_near, line = lax.optimization_barrier((near_part[0], line))
        near_part = (first_near, near_part[1])
        near = rounds(near_part, 0, 1, [None, None])
        for t in range(1, reach):
            if t == EARLY:
                far, near = lax.optimization_barrier((far, near))
                far_blocks = []
                for block in far:
                    far_blocks += [block, swap(block, 1)]
                far_part = partial_sums(samples, far_blocks, table, pieces, core_at, FAR_COST)
            if t < PINS:
                pass_components(t + 1, t + 2)
            near = rounds(near_part, t, t + 1, near)
            if t < PINS:
                near, line = lax.optimization_barrier((near, line))
            if t == EARLY:
                first_far, line = lax.optimization_barrier((far_part[0], line))
                far_part = (first_far, far_part[1])
        near = lax.ppermute(near[0], both, streams[0]) + near[1]
        pass_components(min(PINS + 1, reach + 1), reach + 1)

        held = rounds(far_part, 0, min(TIE1, reach), [None, None])
        over = over_high_bits(groups[0])
        held, over = lax.optimization_barrier((held, over))
        held = rounds(far_part, min(TIE1, reach), min(TIE2, reach), held)
        over = [over] + [over_high_bits(g) for g in groups[1:]]
        held, over = lax.optimization_barrier((held, over))
        near_stack, *far_stacks = [jnp.concatenate(parts) for parts in zip(*over)]
        far_stack = jnp.concatenate(far_stacks, axis=2) if n_high > 2 else far_stacks[0]
        near_rows = [near, swap(near, 1)]
        n_wide, n_tall = near_stack.shape[2], n_feat * near_stack.shape[1]
        f_wide, n_deep = far_stack.shape[2], 2 * height
        near_side = call(
            functools.partial(near_kernel, order_at),
            [f32(n_tall, n_deep), bf16(n_tall, f_wide), bf16(n_tall, f_wide), bf16(n_deep, n_wide), bf16(n_deep, n_wide)],
            table,
            *near_rows,
            near_stack,
            far_stack,
            flops=6 * n_tall * n_deep * n_wide,
        )
        held = rounds(far_part, min(TIE2, reach), reach, held)
        arrived = lax.ppermute(held[0], both, streams[0])
        arrived, near_side = lax.optimization_barrier((arrived, near_side))
        far_sum = arrived + held[1]
        far_rows = [far_sum, swap(far_sum, 1)]
        scale_inv = float((samples.shape[0] * n_rows) ** -0.5)
        tile = n_tall // 2
        whole = lambda a: pl.BlockSpec(a.shape, lambda i, t: (0, 0))
        tiled = lambda a: pl.BlockSpec((tile, a.shape[1]), lambda i, t: (i, 0))
        half_wide = n_high * (n_wide // 2)
        a, b = call(
            functools.partial(moment_kernel, scale_inv, n_high),
            [f32(n_tall, half_wide)] * 2,
            table,
            *near_side,
            *far_rows,
            grid=(n_tall // tile,),
            in_specs=[tiled(x) for x in near_side[:3]] + [whole(x) for x in near_side[3:]] + [whole(x) for x in far_rows],
            out_specs=[pl.BlockSpec((tile, half_wide), lambda i, t: (i, 0))] * 2,
            scratch_shapes=[pltpu.VMEM((n_deep, f_wide), jnp.bfloat16)] * 2,
            flops=6 * n_tall * n_deep * (n_wide + 2 * f_wide),
        )

        def over_rows(x):
            for bit in high_bits[::-1]:
                half = x.shape[1] // 2
                x = x[:, :half] + swap(x[:, half:], bit)
            return x

        def over_first_bit(x):
            half = x.shape[0] // 2
            return x[:half] + swap_feat(x[half:], 1)

        a, b = over_first_bit(over_rows(a)), over_rows(over_first_bit(b))
        joint = jnp.concatenate([a, b], axis=1)
        step = joint.shape[0] // (n_feat // 2)
        parts = [joint[k * step : (k + 1) * step] for k in range(n_feat // 2)]
        parts = parts[:1] + [swap_feat(part, 2 * k) for k, part in enumerate(parts) if k]
        width = joint.shape[1] // 2
        kept, sent = call(
            functools.partial(divide_kernel, core_at), [f32(step, width)] * 2, table, *parts
        )
        return call(
            functools.partial(assemble_kernel, core_at), [f32(width, 2 * step)], table, kept, swap(sent, 1)
        )[0]

    placed = (P("rows", "feat"), P("feat", "rows"), P("rows", "feat"))
    return jax.shard_map(
        on_device, mesh=mesh, in_specs=placed, out_specs=P("rows", "feat"), check_vma=False
    )
```

time: 329 us -> 156 us (0.47)
  waiting for transfers between devices: 264 us -> 57.7 us
  matrix products: 43.6 us -> 0 us
  Pallas kernels: 0 us -> 43.4 us
  starting transfers between devices: 0.08 us -> 34.9 us
  between operations: 13.1 us -> 0.3 us
  local copies, waits for them, and re-layouts: 0.83 us -> 12.6 us
  blocking collectives: 7.18 us -> 0 us
  other arithmetic: 0 us -> 6.57 us
    psum x1 -> x0, waiting for transfers between devices: 204 us -> none  [on_device(): whitened = lax.psum(partial_y, 'feat')]
    ppermute x0 -> x37, waiting for transfers between devices: none -> 57.7 us  [the longest x5 21.1 us: swap_feat(): return lax.ppermute(a, 'feat', [(i, i ^ bit) for i in range(n_feat)])]
    dot_general x3 -> x0, matrix products: 43.6 us -> none  [the longest x1 24.8 us: on_device(): jnp.dot(samples, lax.all_gather(whitening, 'rows', axis=1, tiled=True), p...]
    pallas_call x0 -> x8, Pallas kernels: none -> 43.4 us  [call(): pl.pallas_call(kernel, out_shape=outs, grid_spec=pltpu.PrefetchScalarGrid...]
    all_gather x1 -> x0, waiting for transfers between devices: 38.8 us -> none  [on_device(): lax.all_gather(whitening, 'rows', axis=1, tiled=True)]
    ppermute x0 -> x37, starting transfers between devices: none -> 34.9 us  [the longest x12 14.2 us: rounds(): held[s] = lax.ppermute(held[s], both, streams[s]) + piece]
    reduce_scatter x1 -> x0, waiting for transfers between devices: 20.8 us -> none  [on_device(): lax.psum_scatter(product * scale_inv, 'rows', scatter_dimension=0, tiled=...]
    all_gather x1 -> x0, blocking collectives: 7.18 us -> none  [on_device(): lax.all_gather(components, 'rows', axis=0, tiled=True)]
  transfers between devices with their start and end apart: 3 -> 37, of which waited for: 3 -> 19; matrix products, arithmetic and copies ran while one was open for 0% -> 8% of each run, Pallas kernels for 0% -> 21%
where the time goes in v2:
time: 156 us; the launch traced here: 155 us
  waiting for transfers between devices  57.7 us (37%)
  Pallas kernels  43.4 us (28%)
  starting transfers between devices  34.9 us (22%)
  local copies, waits for them, and re-layouts  12.6 us (8%)
  other arithmetic  6.57 us (4%)
    pallas_call x8, Pallas kernels, call(): pl.pallas_call(kernel, out_shape=outs, grid_spec=pltpu.PrefetchScalarGrid...  43.4 us
    ppermute x5, waiting for transfers between devices, swap_feat(): return lax.ppermute(a, 'feat', [(i, i ^ bit) for i in range(n_feat)])  21.1 us
    ppermute x12, waiting for transfers between devices, rounds(): held[s] = lax.ppermute(held[s], both, streams[s]) + piece  14.9 us
    ppermute x12, starting transfers between devices, rounds(): held[s] = lax.ppermute(held[s], both, streams[s]) + piece  14.2 us
    ppermute x11, waiting for transfers between devices, swap(): return lax.ppermute(a, 'rows', [(i, i ^ bit) for i in range(n_rows)])  10.7 us
    ppermute x4, waiting for transfers between devices, pass_components(): line[step] = lax.ppermute(line[step - 1], both, streams[0])  7.65 us
    ppermute x5, starting transfers between devices, swap_feat(): return lax.ppermute(a, 'feat', [(i, i ^ bit) for i in range(n_feat)])  6.46 us
    unnamed x35, local copies, waits for them, and re-layouts  5.8 us
  transfers between devices with their start and end apart: 37, of which 19 were waited for; matrix products, arithmetic and copies ran while one was open for 8% of the time, Pallas kernels for 21%

profile of v2, /device:TPU:0, one launch (start us, length us, event | category | flops | bytes accessed | tf_op | source)
XLA Modules:
  0.0 155.4 jit_solution(5894584799813674773)
XLA Ops:
  0.5 2.5 %collective-permute-start = (f32[1024,256]{1,0:T(8,128)}, f32[1024,256]{1,0:T(8,128)S(1)}, u32[]{:S(2)}, u32[]{:S(2)}) collective-permute-start(f32[1024,256]{1,0:T(8,128)} %refs_2_.3), channel_id=1, source_target_pairs={{0,16},{8,24},{16,0},{24,8},{1,17},{9,25},{17,1},{25,9},{2,18},{10... | collective-permute-start | bytes 3145736 | tf_op jit(solution)/shard_map/ppermute | solution.py:214
  4.3 1.2 fusion.5.table
  5.6 1.5 collective-permute-start.4
  8.6 5.3 %shard_map.46 = f32[384,512]{1,0:T(8,128)} custom-call(s32[17]{0:T(128)} %fusion.5.table, f32[1536,1024]{1,0:T(8,128)} %refs_1_.7, f32[1536,1024]{1,0:T(8,128)} %refs_1_.7, f32[1024,256]{1,0:T(8,128)} %refs_2_.3, f32[1024,256]{1,0:T(8,128)} %copy-done.13), custom_call_target="tpu_custom_call" | custom-call | flops 16106127360 | bytes 14680064 | tf_op jit(solution)/shard_map/pallas_call | solution.py:50
  13.9 1.2 fusion.7
  15.1 1.6 %collective-permute-start.7 = (f32[64,512]{1,0:T(8,128)S(1)}, f32[64,512]{1,0:T(8,128)S(1)}, u32[]{:S(2)}, u32[]{:S(2)}) collective-permute-start(f32[64,512]{1,0:T(8,128)S(1)} %collective-permute-done.3), channel_id=1, source_target_pairs={{0,2},{2,4},{4,6},{6,7},{7,5},{5,3},{3,1},{1,0},{8,9},{10,8},{12,1... | collective-permute-start | bytes 393224 | tf_op jit(solution)/shard_map/ppermute | solution.py:260
  17.2 1.5 collective-permute-start.6
  19.2 8.4 %shard_map.47 = f32[1152,512]{1,0:T(8,128)} custom-call(s32[17]{0:T(128)} %fusion.5.table, f32[1536,1024]{1,0:T(8,128)} %refs_1_.7, f32[1536,1024]{1,0:T(8,128)} %refs_1_.7, f32[1024,256]{1,0:T(8,128)} %refs_2_.3, f32[1024,256]{1,0:T(8,128)} %copy-done.13), custom_call_target="tpu_custom_call" | custom-call | flops 48318382080 | bytes 14680064 | tf_op jit(solution)/shard_map/pallas_call | solution.py:50
  27.6 2.5 %collective-permute-done.6 = f32[192,512]{1,0:T(8,128)S(1)} collective-permute-done((f32[192,512]{1,0:T(8,128)S(1)}, f32[192,512]{1,0:T(8,128)S(1)}, u32[]{:S(2)}, u32[]{:S(2)}) %collective-permute-start.6) | collective-permute-done | bytes 393248 | tf_op jit(solution)/shard_map/ppermute | solution.py:242
  30.1 1.3 slice_add_fusion.12
  31.5 1.6 %collective-permute-start.21 = (f32[192,512]{1,0:T(8,128)S(1)}, f32[192,512]{1,0:T(8,128)S(1)}, u32[]{:S(2)}, u32[]{:S(2)}) collective-permute-start(f32[192,512]{1,0:T(8,128)S(1)} %get-tuple-element.61), channel_id=1, source_target_pairs={{0,2},{2,4},{4,6},{6,7},{7,5},{5,3},{3,1},{1,0},{8,9},{10,8},{12,1... | collective-permute-start | bytes 1179656 | tf_op jit(solution)/shard_map/ppermute | solution.py:242
  35.1 5.3 %shard_map.48 = f32[384,512]{1,0:T(8,128)} custom-call(s32[17]{0:T(128)} %fusion.5.table, f32[1536,1024]{1,0:T(8,128)} %refs_1_.7, f32[1536,1024]{1,0:T(8,128)} %refs_1_.7, f32[1024,256]{1,0:T(8,128)} %copy-done.1, f32[1024,256]{1,0:T(8,128)} %copy-done.2), custom_call_target="tpu_custom_call" | custom-call | bytes 14680064 | tf_op jit(solution)/shard_map/pallas_call | solution.py:50
  40.4 2.1 %fusion.6 = (f32[192,512]{1,0:T(8,128)}, f32[192,512]{1,0:T(8,128)}) fusion(f32[384,512]{1,0:T(8,128)} %shard_map.48), kind=kLoop, calls=%fused_computation.42 | loop fusion | bytes 1572864 | tf_op jit(solution)/shard_map/slice | solution.py:238
  42.4 1.4 collective-permute-start.11
  45.0 1.4 collective-permute-start.24
  47.1 8.4 %shard_map.49 = f32[1152,512]{1,0:T(8,128)} custom-call(s32[17]{0:T(128)} %fusion.5.table, f32[1536,1024]{1,0:T(8,128)} %refs_1_.7, f32[1536,1024]{1,0:T(8,128)} %refs_1_.7, f32[1024,256]{1,0:T(8,128)} %copy-done.1, f32[1024,256]{1,0:T(8,128)} %copy-done.2), custom_call_target="tpu_custom_call" | custom-call | bytes 14680064 | tf_op jit(solution)/shard_map/pallas_call | solution.py:50
  55.5 3.5 %collective-permute-done.15 = f32[64,512]{1,0:T(8,128)} collective-permute-done((f32[64,512]{1,0:T(8,128)S(1)}, f32[64,512]{1,0:T(8,128)}, u32[]{:S(2)}, u32[]{:S(2)}) %collective-permute-start.15) | collective-permute-done | bytes 131104 | tf_op jit(solution)/shard_map/ppermute | solution.py:260
  59.6 1.4 collective-permute-start.17
  61.6 1.3 slice_add_fusion.10
  62.9 1.6 %collective-permute-start.13 = (f32[192,512]{1,0:T(8,128)S(1)}, f32[192,512]{1,0:T(8,128)S(1)}, u32[]{:S(2)}, u32[]{:S(2)}) collective-permute-start(f32[192,512]{1,0:T(8,128)S(1)} %get-tuple-element.54), channel_id=1, source_target_pairs={{0,2},{2,4},{4,6},{6,7},{7,5},{5,3},{3,1},{1,0},{8,9},{10,8},{12,1... | collective-permute-start | bytes 1179656 | tf_op jit(solution)/shard_map/ppermute | solution.py:242
  64.6 1.5 collective-permute-done.17
  66.0 1.4 collective-permute-start.14
  67.5 4.1 %collective-permute-done.16 = f32[64,512]{1,0:T(8,128)S(1)} collective-permute-done((f32[64,512]{1,0:T(8,128)}, f32[64,512]{1,0:T(8,128)S(1)}, u32[]{:S(2)}, u32[]{:S(2)}) %collective-permute-start.16) | collective-permute-done | bytes 131104 | tf_op jit(solution)/shard_map/ppermute | solution.py:260
  73.3 1.7 %collective-permute-start.25 = (f32[192,512]{1,0:T(8,128)S(1)}, f32[192,512]{1,0:T(8,128)S(1)}, u32[]{:S(2)}, u32[]{:S(2)}) collective-permute-start(f32[192,512]{1,0:T(8,128)S(1)} %get-tuple-element.83), channel_id=1, source_target_pairs={{0,1},{2,0},{4,2},{6,4},{7,6},{5,7},{3,5},{1,3},{8,10},{10,12},{12... | collective-permute-start | bytes 1179656 | tf_op jit(solution)/shard_map/ppermute | solution.py:242
  75.3 4.7 %collective-permute-done.13 = f32[192,512]{1,0:T(8,128)S(1)} collective-permute-done((f32[192,512]{1,0:T(8,128)S(1)}, f32[192,512]{1,0:T(8,128)S(1)}, u32[]{:S(2)}, u32[]{:S(2)}) %collective-permute-start.13) | collective-permute-done | bytes 393248 | tf_op jit(solution)/shard_map/ppermute | solution.py:242
  81.4 5.2 %collective-permute-done.25 = f32[192,512]{1,0:T(8,128)S(1)} collective-permute-done((f32[192,512]{1,0:T(8,128)S(1)}, f32[192,512]{1,0:T(8,128)S(1)}, u32[]{:S(2)}, u32[]{:S(2)}) %collective-permute-start.25) | collective-permute-done | bytes 393248 | tf_op jit(solution)/shard_map/ppermute | solution.py:242
  86.7 2.5 %collective-permute-done.19 = f32[192,512]{1,0:T(8,128)S(1)} collective-permute-done((f32[192,512]{1,0:T(8,128)S(1)}, f32[192,512]{1,0:T(8,128)S(1)}, u32[]{:S(2)}, u32[]{:S(2)}) %collective-permute-start.19) | collective-permute-done | bytes 393248 | tf_op jit(solution)/shard_map/ppermute | solution.py:242
  89.3 1.3 collective-permute-start.20
  91.4 1.6 %pad_maximum_fusion = (f32[8,64,512]{2,1,0:T(8,128)}, f32[8,64,512]{2,1,0:T(8,128)}) fusion(f32[3,64,512]{2,1,0:T(8,128)S(1)} %pad_maximum_fusion.2, f32[5,64,512]{2,1,0:T(8,128)S(1)} %bitcast_dynamic-update-slice_fusion, f32[3,64,512]{2,1,0:T(8,128)S(1)} %collective-permute-done.18, f32[5,64,512]{2,1,0:T(8,128)S(1)} %collective-permute-done.12), kind=kLoop, calls=%fused_computation | loop fusion | flops 524288 | bytes 4194304 | tf_op jit(solution)/shard_map/concatenate | solution.py:295
  93.7 4.7 %shard_map.50 = (f32[512,384]{1,0:T(8,128)}, bf16[512,512]{1,0:T(8,128)(2,1)}, bf16[512,512]{1,0:T(8,128)(2,1)}, bf16[384,512]{1,0:T(8,128)(2,1)}, bf16[384,512]{1,0:T(8,128)(2,1)}) custom-call(s32[17]{0:T(128)} %fusion.5.table, f32[192,512]{1,0:T(8,128)} %copy-done.4, f32[192,512]{1,0:T(8,128)} %copy-done.7, f32[8,64,512]{2,1,0:T(8,128)} %get-tuple-element.101.refs_2_, ...), custom_call_target="tpu_custom_call" | custom-call | flops 603979776 | bytes 2883584 | tf_op jit(solution)/shard_map/pallas_call | solution.py:50
  98.4 1.8 %collective-permute-done.20 = f32[192,512]{1,0:T(8,128)S(1)} collective-permute-done((f32[192,512]{1,0:T(8,128)S(1)}, f32[192,512]{1,0:T(8,128)S(1)}, u32[]{:S(2)}, u32[]{:S(2)}) %collective-permute-start.20) | collective-permute-done | bytes 393248 | tf_op jit(solution)/shard_map/ppermute | solution.py:310
  100.4 1.7 %collective-permute-done.28.refs_6_ = f32[192,512]{1,0:T(8,128)S(1)} collective-permute-done((f32[192,512]{1,0:T(8,128)S(1)}, f32[192,512]{1,0:T(8,128)S(1)}, u32[]{:S(2)}, u32[]{:S(2)}) %collective-permute-start.28) | collective-permute-done | bytes 393248 | tf_op jit(solution)/shard_map/ppermute | solution.py:214
  102.9 6.6 %shard_map.51 = (f32[512,512]{1,0:T(8,128)}, f32[512,512]{1,0:T(8,128)}) custom-call(s32[17]{0:T(128)} %fusion.5.table, f32[512,384]{1,0:T(8,128)} %get-tuple-element.72.refs_0_, bf16[512,512]{1,0:T(8,128)(2,1)} %get-tuple-element.73.refs_1_, bf16[512,512]{1,0:T(8,128)(2,1)} %get-tuple-element.74.refs_2_, bf16[384,512]{1,0:T(8,128)(2,1)} %get-tuple-element.75.refs_3_, ...), custom_call_target="tpu_custom_call" | custom-call | flops 1811939328 | bytes 5242880 | tf_op jit(solution)/shard_map/pallas_call | solution.py:50
  109.5 1.2 slice.105
  110.7 1.4 collective-permute-start.31
  112.2 1.1 slice.101
  113.8 10.9 %collective-permute-done.31 = f32[256,512]{1,0:T(8,128)S(1)} collective-permute-done((f32[256,512]{1,0:T(8,128)S(1)}, f32[256,512]{1,0:T(8,128)S(1)}, u32[]{:S(2)}, u32[]{:S(2)}) %collective-permute-start.31) | collective-permute-done | bytes 524320 | tf_op jit(solution)/shard_map/ppermute | solution.py:217
  125.5 1.6 %collective-permute-done.29 = f32[512,256]{1,0:T(8,128)S(1)} collective-permute-done((f32[512,256]{1,0:T(8,128)S(1)}, f32[512,256]{1,0:T(8,128)S(1)}, u32[]{:S(2)}, u32[]{:S(2)}) %collective-permute-start.29) | collective-permute-done | bytes 524320 | tf_op jit(solution)/shard_map/ppermute | solution.py:214
  127.9 4.8 %collective-permute-done.32 = f32[256,256]{1,0:T(8,128)S(1)} collective-permute-done((f32[256,256]{1,0:T(8,128)S(1)}, f32[256,256]{1,0:T(8,128)S(1)}, u32[]{:S(2)}, u32[]{:S(2)}) %collective-permute-start.32) | collective-permute-done | bytes 262176 | tf_op jit(solution)/shard_map/ppermute | solution.py:214
  132.7 1.7 %collective-permute-done.30 = f32[256,256]{1,0:T(8,128)S(1)} collective-permute-done((f32[256,256]{1,0:T(8,128)S(1)}, f32[256,256]{1,0:T(8,128)S(1)}, u32[]{:S(2)}, u32[]{:S(2)}) %collective-permute-start.30) | collective-permute-done | bytes 262176 | tf_op jit(solution)/shard_map/ppermute | solution.py:217
  135.1 2.6 %collective-permute-start.35 = (f32[64,512]{1,0:T(8,128)S(1)}, f32[64,512]{1,0:T(8,128)S(1)}, u32[]{:S(2)}, u32[]{:S(2)}) collective-permute-start(f32[64,512]{1,0:T(8,128)S(1)} %get-tuple-element.95), channel_id=1, source_target_pairs={{0,6},{1,7},{2,4},{3,5},{4,2},{5,3},{6,0},{7,1},{8,14},{9,15},{10,... | collective-permute-start | bytes 393224 | tf_op jit(solution)/shard_map/ppermute | solution.py:217
  138.2 1.3 collective-permute-start.34
  139.5 3.8 %collective-permute-done.35.refs_2_ = f32[64,512]{1,0:T(8,128)S(1)} collective-permute-done((f32[64,512]{1,0:T(8,128)S(1)}, f32[64,512]{1,0:T(8,128)S(1)}, u32[]{:S(2)}, u32[]{:S(2)}) %collective-permute-start.35) | collective-permute-done | bytes 131104 | tf_op jit(solution)/shard_map/ppermute | solution.py:217
  143.3 1.1 collective-permute-done.33.refs_0_
  144.4 3.6 %collective-permute-done.34.refs_1_ = f32[64,512]{1,0:T(8,128)S(1)} collective-permute-done((f32[64,512]{1,0:T(8,128)S(1)}, f32[64,512]{1,0:T(8,128)S(1)}, u32[]{:S(2)}, u32[]{:S(2)}) %collective-permute-start.34) | collective-permute-done | bytes 131104 | tf_op jit(solution)/shard_map/ppermute | solution.py:217
  148.6 2.4 %shard_map.52 = (f32[64,256]{1,0:T(8,128)}, f32[64,256]{1,0:T(8,128)}) custom-call(s32[17]{0:T(128)} %fusion.5.table, f32[64,512]{1,0:T(8,128)} %get-tuple-element.96.own_ref, f32[64,512]{1,0:T(8,128)} %copy-done.10, f32[64,512]{1,0:T(8,128)} %copy-done.11, f32[64,512]{1,0:T(8,128)} %copy-done.9), custom_call_target="tpu_custom_call" | custom-call | bytes 524288 | tf_op jit(solution)/shard_map/pallas_call | solution.py:50
  151.1 1.5 collective-permute-done.36.other_ref
  153.1 2.3 %shard_map.53 = f32[256,128]{1,0:T(8,128)} custom-call(s32[17]{0:T(128)} %fusion.5.table, f32[64,256]{1,0:T(8,128)} %get-tuple-element.81.own_ref, f32[64,256]{1,0:T(8,128)} %copy-done.12), custom_call_target="tpu_custom_call" | custom-call | bytes 131072 | tf_op jit(solution)/shard_map/pallas_call | solution.py:50
  (95 shorter events, 20.1 us)
Async XLA Ops:
  0.0 7.6 %collective-permute-start.1 = (f32[1024,256]{1,0:T(8,128)}, f32[1024,256]{1,0:T(8,128)S(1)}, u32[]{:S(2)}, u32[]{:S(2)}) collective-permute-start(f32[1024,256]{1,0:T(8,128)} %refs_2_.3), channel_id=1, source_target_pairs={{0,8},{8,0},{16,24},{24,16},{1,9},{9,1},{17,25},{25,17},{2,10},{10... | collective-permute-start | bytes 3145736 | tf_op jit(solution)/shard_map/ppermute | solution.py:214
  0.5 30.9 %collective-permute-start = (f32[1024,256]{1,0:T(8,128)}, f32[1024,256]{1,0:T(8,128)S(1)}, u32[]{:S(2)}, u32[]{:S(2)}) collective-permute-start(f32[1024,256]{1,0:T(8,128)} %refs_2_.3), channel_id=1, source_target_pairs={{0,16},{8,24},{16,0},{24,8},{1,17},{9,25},{17,1},{25,9},{2,18},{10... | collective-permute-start | bytes 3145736 | tf_op jit(solution)/shard_map/ppermute | solution.py:214
  4.0 1.5 collective-permute-start.2
  5.6 8.4 %collective-permute-start.4 = (f32[64,512]{1,0:T(8,128)S(1)}, f32[64,512]{1,0:T(8,128)S(1)}, u32[]{:S(2)}, u32[]{:S(2)}) collective-permute-start(f32[64,512]{1,0:T(8,128)S(1)} %pad_maximum_fusion.4), channel_id=1, source_target_pairs={{0,1},{2,0},{4,2},{6,4},{7,6},{5,7},{3,5},{1,3},{8,10},{10,12},{12... | collective-permute-start | bytes 393224 | tf_op jit(solution)/shard_map/ppermute | solution.py:262
  7.1 6.8 %collective-permute-start.3 = (f32[64,512]{1,0:T(8,128)S(1)}, f32[64,512]{1,0:T(8,128)S(1)}, u32[]{:S(2)}, u32[]{:S(2)}) collective-permute-start(f32[64,512]{1,0:T(8,128)S(1)} %pad_maximum_fusion.4), channel_id=1, source_target_pairs={{0,2},{2,4},{4,6},{6,7},{7,5},{5,3},{3,1},{1,0},{8,9},{10,8},{12,1... | collective-permute-start | bytes 393224 | tf_op jit(solution)/shard_map/ppermute | solution.py:260
  7.6 1.0 copy-start.13
  15.1 16.2 %collective-permute-start.7 = (f32[64,512]{1,0:T(8,128)S(1)}, f32[64,512]{1,0:T(8,128)S(1)}, u32[]{:S(2)}, u32[]{:S(2)}) collective-permute-start(f32[64,512]{1,0:T(8,128)S(1)} %collective-permute-done.3), channel_id=1, source_target_pairs={{0,2},{2,4},{4,6},{6,7},{7,5},{5,3},{3,1},{1,0},{8,9},{10,8},{12,1... | collective-permute-start | bytes 393224 | tf_op jit(solution)/shard_map/ppermute | solution.py:260
  16.7 14.6 %collective-permute-start.8 = (f32[64,512]{1,0:T(8,128)S(1)}, f32[64,512]{1,0:T(8,128)S(1)}, u32[]{:S(2)}, u32[]{:S(2)}) collective-permute-start(f32[64,512]{1,0:T(8,128)S(1)} %collective-permute-done.4), channel_id=1, source_target_pairs={{0,1},{2,0},{4,2},{6,4},{7,6},{5,7},{3,5},{1,3},{8,10},{10,12},{12... | collective-permute-start | bytes 393224 | tf_op jit(solution)/shard_map/ppermute | solution.py:262
  17.2 12.9 %collective-permute-start.6 = (f32[192,512]{1,0:T(8,128)S(1)}, f32[192,512]{1,0:T(8,128)S(1)}, u32[]{:S(2)}, u32[]{:S(2)}) collective-permute-start(f32[192,512]{1,0:T(8,128)S(1)} %get-tuple-element.93), channel_id=1, source_target_pairs={{0,1},{2,0},{4,2},{6,4},{7,6},{5,7},{3,5},{1,3},{8,10},{10,12},{12... | collective-permute-start | bytes 1179656 | tf_op jit(solution)/shard_map/ppermute | solution.py:242
  18.7 11.4 %collective-permute-start.5 = (f32[192,512]{1,0:T(8,128)S(1)}, f32[192,512]{1,0:T(8,128)S(1)}, u32[]{:S(2)}, u32[]{:S(2)}) collective-permute-start(f32[192,512]{1,0:T(8,128)S(1)} %get-tuple-element.94), channel_id=1, source_target_pairs={{0,2},{2,4},{4,6},{6,7},{7,5},{5,3},{3,1},{1,0},{8,9},{10,8},{12,1... | collective-permute-start | bytes 1179656 | tf_op jit(solution)/shard_map/ppermute | solution.py:242
  31.4 2.7 %copy-start.1 = (f32[1024,256]{1,0:T(8,128)}, f32[1024,256]{1,0:T(8,128)S(1)}, u32[]{:S(2)}) copy-start(f32[1024,256]{1,0:T(8,128)S(1)} %collective-permute-done.refs_2_) | copy-start | bytes 3145732
  31.4 2.7 %collective-permute-start.9 = (f32[1024,256]{1,0:T(8,128)S(1)}, f32[1024,256]{1,0:T(8,128)S(1)}, u32[]{:S(2)}, u32[]{:S(2)}) collective-permute-start(f32[1024,256]{1,0:T(8,128)S(1)} %collective-permute-done.refs_2_), channel_id=1, source_target_pairs={{0,8},{8,0},{16,24},{24,16},{1,9},{9,1},{17,25},{25,17},{2,10},{10... | collective-permute-start | bytes 3145736 | tf_op jit(solution)/shard_map/ppermute | solution.py:214
  31.5 15.6 %copy-start.3 = (f32[1152,512]{1,0:T(8,128)S(1)}, f32[1152,512]{1,0:T(8,128)}, u32[]{:S(2)}) copy-start(f32[1152,512]{1,0:T(8,128)} %shard_map.47) | copy-start | bytes 7077892
  31.5 14.9 %collective-permute-start.21 = (f32[192,512]{1,0:T(8,128)S(1)}, f32[192,512]{1,0:T(8,128)S(1)}, u32[]{:S(2)}, u32[]{:S(2)}) collective-permute-start(f32[192,512]{1,0:T(8,128)S(1)} %get-tuple-element.61), channel_id=1, source_target_pairs={{0,2},{2,4},{4,6},{6,7},{7,5},{5,3},{3,1},{1,0},{8,9},{10,8},{12,1... | collective-permute-start | bytes 1179656 | tf_op jit(solution)/shard_map/ppermute | solution.py:242
  34.1 1.0 copy-start.2
  42.4 17.2 %collective-permute-start.11 = (f32[192,512]{1,0:T(8,128)}, f32[192,512]{1,0:T(8,128)S(1)}, u32[]{:S(2)}, u32[]{:S(2)}) collective-permute-start(f32[192,512]{1,0:T(8,128)} %get-tuple-element.91), channel_id=1, source_target_pairs={{0,1},{2,0},{4,2},{6,4},{7,6},{5,7},{3,5},{1,3},{8,10},{10,12},{12... | collective-permute-start | bytes 1179656 | tf_op jit(solution)/shard_map/ppermute | solution.py:242
  43.8 17.2 %collective-permute-start.10 = (f32[192,512]{1,0:T(8,128)}, f32[192,512]{1,0:T(8,128)S(1)}, u32[]{:S(2)}, u32[]{:S(2)}) collective-permute-start(f32[192,512]{1,0:T(8,128)} %get-tuple-element.92), channel_id=1, source_target_pairs={{0,2},{2,4},{4,6},{6,7},{7,5},{5,3},{3,1},{1,0},{8,9},{10,8},{12,1... | collective-permute-start | bytes 1179656 | tf_op jit(solution)/shard_map/ppermute | solution.py:242
  44.5 18.4 %collective-permute-start.12 = (f32[5,64,512]{2,1,0:T(8,128)S(1)}, f32[5,64,512]{2,1,0:T(8,128)S(1)}, u32[]{:S(2)}, u32[]{:S(2)}) collective-permute-start(f32[5,64,512]{2,1,0:T(8,128)S(1)} %bitcast_dynamic-update-slice_fusion), channel_id=1, source_target_pairs={{0,16},{8,24},{16,0},{24,8},{1,17},{9,25},{17,1},{25,9},{2,18},{10... | collective-permute-start | bytes 1966088 | tf_op jit(solution)/shard_map/ppermute | solution.py:214
  45.0 28.1 %collective-permute-start.24 = (f32[192,512]{1,0:T(8,128)S(1)}, f32[192,512]{1,0:T(8,128)S(1)}, u32[]{:S(2)}, u32[]{:S(2)}) collective-permute-start(f32[192,512]{1,0:T(8,128)S(1)} %get-tuple-element.62), channel_id=1, source_target_pairs={{0,1},{2,0},{4,2},{6,4},{7,6},{5,7},{3,5},{1,3},{8,10},{10,12},{12... | collective-permute-start | bytes 1179656 | tf_op jit(solution)/shard_map/ppermute | solution.py:242
  46.4 12.6 %collective-permute-start.15 = (f32[64,512]{1,0:T(8,128)S(1)}, f32[64,512]{1,0:T(8,128)}, u32[]{:S(2)}, u32[]{:S(2)}) collective-permute-start(f32[64,512]{1,0:T(8,128)S(1)} %collective-permute-done.7), channel_id=1, source_target_pairs={{0,2},{2,4},{4,6},{6,7},{7,5},{5,3},{3,1},{1,0},{8,9},{10,8},{12,1... | collective-permute-start | bytes 393224 | tf_op jit(solution)/shard_map/ppermute | solution.py:260
  55.5 24.5 %copy-start = (f32[1152,512]{1,0:T(8,128)S(1)}, f32[1152,512]{1,0:T(8,128)}, u32[]{:S(2)}) copy-start(f32[1152,512]{1,0:T(8,128)} %shard_map.49) | copy-start | bytes 7077892
  59.0 14.1 %collective-permute-start.22 = (f32[192,512]{1,0:T(8,128)S(1)}, f32[192,512]{1,0:T(8,128)S(1)}, u32[]{:S(2)}, u32[]{:S(2)}) collective-permute-start(f32[192,512]{1,0:T(8,128)S(1)} %slice_add_fusion.6), channel_id=1, source_target_pairs={{0,2},{2,4},{4,6},{6,7},{7,5},{5,3},{3,1},{1,0},{8,9},{10,8},{12,1... | collective-permute-start | bytes 1179656 | tf_op jit(solution)/shard_map/ppermute | solution.py:242
  59.6 6.4 %collective-permute-start.17 = (f32[64,512]{1,0:T(8,128)S(1)}, f32[64,512]{1,0:T(8,128)S(1)}, u32[]{:S(2)}, u32[]{:S(2)}) collective-permute-start(f32[64,512]{1,0:T(8,128)S(1)} %collective-permute-done.8), channel_id=1, source_target_pairs={{0,1},{2,0},{4,2},{6,4},{7,6},{5,7},{3,5},{1,3},{8,10},{10,12},{12... | collective-permute-start | bytes 393224 | tf_op jit(solution)/shard_map/ppermute | solution.py:262
  61.0 10.6 %collective-permute-start.16 = (f32[64,512]{1,0:T(8,128)}, f32[64,512]{1,0:T(8,128)S(1)}, u32[]{:S(2)}, u32[]{:S(2)}) collective-permute-start(f32[64,512]{1,0:T(8,128)} %collective-permute-done.15), channel_id=1, source_target_pairs={{0,2},{2,4},{4,6},{6,7},{7,5},{5,3},{3,1},{1,0},{8,9},{10,8},{12,1... | collective-permute-start | bytes 393224 | tf_op jit(solution)/shard_map/ppermute | solution.py:260
  62.9 17.1 %collective-permute-start.13 = (f32[192,512]{1,0:T(8,128)S(1)}, f32[192,512]{1,0:T(8,128)S(1)}, u32[]{:S(2)}, u32[]{:S(2)}) collective-permute-start(f32[192,512]{1,0:T(8,128)S(1)} %get-tuple-element.54), channel_id=1, source_target_pairs={{0,2},{2,4},{4,6},{6,7},{7,5},{5,3},{3,1},{1,0},{8,9},{10,8},{12,1... | collective-permute-start | bytes 1179656 | tf_op jit(solution)/shard_map/ppermute | solution.py:242
  66.0 14.0 %collective-permute-start.14 = (f32[192,512]{1,0:T(8,128)S(1)}, f32[192,512]{1,0:T(8,128)S(1)}, u32[]{:S(2)}, u32[]{:S(2)}) collective-permute-start(f32[192,512]{1,0:T(8,128)S(1)} %get-tuple-element.55), channel_id=1, source_target_pairs={{0,1},{2,0},{4,2},{6,4},{7,6},{5,7},{3,5},{1,3},{8,10},{10,12},{12... | collective-permute-start | bytes 1179656 | tf_op jit(solution)/shard_map/ppermute | solution.py:242
  72.5 7.8 %collective-permute-start.18 = (f32[3,64,512]{2,1,0:T(8,128)S(1)}, f32[3,64,512]{2,1,0:T(8,128)S(1)}, u32[]{:S(2)}, u32[]{:S(2)}) collective-permute-start(f32[3,64,512]{2,1,0:T(8,128)S(1)} %pad_maximum_fusion.2), channel_id=1, source_target_pairs={{0,16},{8,24},{16,0},{24,8},{1,17},{9,25},{17,1},{25,9},{2,18},{10... | collective-permute-start | bytes 1179656 | tf_op jit(solution)/shard_map/ppermute | solution.py:214
  73.3 13.3 %collective-permute-start.25 = (f32[192,512]{1,0:T(8,128)S(1)}, f32[192,512]{1,0:T(8,128)S(1)}, u32[]{:S(2)}, u32[]{:S(2)}) collective-permute-start(f32[192,512]{1,0:T(8,128)S(1)} %get-tuple-element.83), channel_id=1, source_target_pairs={{0,1},{2,0},{4,2},{6,4},{7,6},{5,7},{3,5},{1,3},{8,10},{10,12},{12... | collective-permute-start | bytes 1179656 | tf_op jit(solution)/shard_map/ppermute | solution.py:242
  74.9 11.6 %collective-permute-start.23 = (f32[192,512]{1,0:T(8,128)S(1)}, f32[192,512]{1,0:T(8,128)S(1)}, u32[]{:S(2)}, u32[]{:S(2)}) collective-permute-start(f32[192,512]{1,0:T(8,128)S(1)} %get-tuple-element.84), channel_id=1, source_target_pairs={{0,2},{2,4},{4,6},{6,7},{7,5},{5,3},{3,1},{1,0},{8,9},{10,8},{12,1... | collective-permute-start | bytes 1179656 | tf_op jit(solution)/shard_map/ppermute | solution.py:286
  80.4 8.9 %collective-permute-start.19 = (f32[192,512]{1,0:T(8,128)S(1)}, f32[192,512]{1,0:T(8,128)S(1)}, u32[]{:S(2)}, u32[]{:S(2)}) collective-permute-start(f32[192,512]{1,0:T(8,128)S(1)} %get-tuple-element.60), channel_id=1, source_target_pairs={{0,2},{2,4},{4,6},{6,7},{7,5},{5,3},{3,1},{1,0},{8,9},{10,8},{12,1... | collective-permute-start | bytes 1179656 | tf_op jit(solution)/shard_map/ppermute | solution.py:242
  86.6 6.3 %copy-start.4 = (f32[192,512]{1,0:T(8,128)}, f32[192,512]{1,0:T(8,128)S(1)}, u32[]{:S(2)}) copy-start(f32[192,512]{1,0:T(8,128)S(1)} %fusion.1.refs_0_) | copy-start | bytes 1179652
  86.6 6.3 %collective-permute-start.26 = (f32[192,512]{1,0:T(8,128)S(1)}, f32[192,512]{1,0:T(8,128)S(1)}, u32[]{:S(2)}, u32[]{:S(2)}) collective-permute-start(f32[192,512]{1,0:T(8,128)S(1)} %fusion.1.refs_0_), channel_id=1, source_target_pairs={{0,8},{8,0},{16,24},{24,16},{1,9},{9,1},{17,25},{25,17},{2,10},{10... | collective-permute-start | bytes 1179656 | tf_op jit(solution)/shard_map/ppermute | solution.py:214
  89.3 10.9 %collective-permute-start.20 = (f32[192,512]{1,0:T(8,128)S(1)}, f32[192,512]{1,0:T(8,128)S(1)}, u32[]{:S(2)}, u32[]{:S(2)}) collective-permute-start(f32[192,512]{1,0:T(8,128)S(1)} %slice_add_fusion.7), channel_id=1, source_target_pairs={{0,2},{2,4},{4,6},{6,7},{7,5},{5,3},{3,1},{1,0},{8,9},{10,8},{12,1... | collective-permute-start | bytes 1179656 | tf_op jit(solution)/shard_map/ppermute | solution.py:310
  90.6 9.6 %collective-permute-start.27 = (f32[192,512]{1,0:T(8,128)S(1)}, f32[192,512]{1,0:T(8,128)S(1)}, u32[]{:S(2)}, u32[]{:S(2)}) collective-permute-start(f32[192,512]{1,0:T(8,128)S(1)} %get-tuple-element.78), channel_id=1, source_target_pairs={{0,1},{2,0},{4,2},{6,4},{7,6},{5,7},{3,5},{1,3},{8,10},{10,12},{12... | collective-permute-start | bytes 1179656 | tf_op jit(solution)/shard_map/ppermute | solution.py:242
  100.3 1.8 %copy-start.8 = (f32[192,512]{1,0:T(8,128)}, f32[192,512]{1,0:T(8,128)S(1)}, u32[]{:S(2)}) copy-start(f32[192,512]{1,0:T(8,128)S(1)} %fusion.refs_5_) | copy-start | bytes 1179652
  100.3 1.8 %collective-permute-start.28 = (f32[192,512]{1,0:T(8,128)S(1)}, f32[192,512]{1,0:T(8,128)S(1)}, u32[]{:S(2)}, u32[]{:S(2)}) collective-permute-start(f32[192,512]{1,0:T(8,128)S(1)} %fusion.refs_5_), channel_id=1, source_target_pairs={{0,8},{8,0},{16,24},{24,16},{1,9},{9,1},{17,25},{25,17},{2,10},{10... | collective-permute-start | bytes 1179656 | tf_op jit(solution)/shard_map/ppermute | solution.py:214
  109.5 15.3 %copy-start.6 = (f32[512,512]{1,0:T(8,128)S(1)}, f32[512,512]{1,0:T(8,128)}, u32[]{:S(2)}) copy-start(f32[512,512]{1,0:T(8,128)} %get-tuple-element.80) | copy-start | bytes 3145732
  109.5 17.6 %copy-start.5 = (f32[512,512]{1,0:T(8,128)S(1)}, f32[512,512]{1,0:T(8,128)}, u32[]{:S(2)}) copy-start(f32[512,512]{1,0:T(8,128)} %get-tuple-element.79) | copy-start | bytes 3145732
  110.7 14.0 %collective-permute-start.31 = (f32[256,512]{1,0:T(8,128)S(1)}, f32[256,512]{1,0:T(8,128)S(1)}, u32[]{:S(2)}, u32[]{:S(2)}) collective-permute-start(f32[256,512]{1,0:T(8,128)S(1)} %slice.105), channel_id=1, source_target_pairs={{0,1},{1,0},{2,3},{3,2},{4,5},{5,4},{6,7},{7,6},{8,9},{9,8},{10,11... | collective-permute-start | bytes 1572872 | tf_op jit(solution)/shard_map/ppermute | solution.py:217
  113.3 13.8 %collective-permute-start.29 = (f32[512,256]{1,0:T(8,128)S(1)}, f32[512,256]{1,0:T(8,128)S(1)}, u32[]{:S(2)}, u32[]{:S(2)}) collective-permute-start(f32[512,256]{1,0:T(8,128)S(1)} %slice.101), channel_id=1, source_target_pairs={{0,16},{8,24},{16,0},{24,8},{1,17},{9,25},{17,1},{25,9},{2,18},{10... | collective-permute-start | bytes 1572872 | tf_op jit(solution)/shard_map/ppermute | solution.py:214
  124.9 7.7 %collective-permute-start.32 = (f32[256,256]{1,0:T(8,128)S(1)}, f32[256,256]{1,0:T(8,128)S(1)}, u32[]{:S(2)}, u32[]{:S(2)}) collective-permute-start(f32[256,256]{1,0:T(8,128)S(1)} %slice.127), channel_id=1, source_target_pairs={{0,16},{8,24},{16,0},{24,8},{1,17},{9,25},{17,1},{25,9},{2,18},{10... | collective-permute-start | bytes 786440 | tf_op jit(solution)/shard_map/ppermute | solution.py:214
  127.2 7.2 %collective-permute-start.30 = (f32[256,256]{1,0:T(8,128)S(1)}, f32[256,256]{1,0:T(8,128)S(1)}, u32[]{:S(2)}, u32[]{:S(2)}) collective-permute-start(f32[256,256]{1,0:T(8,128)S(1)} %slice.125), channel_id=1, source_target_pairs={{0,1},{1,0},{2,3},{3,2},{4,5},{5,4},{6,7},{7,6},{8,9},{9,8},{10,11... | collective-permute-start | bytes 786440 | tf_op jit(solution)/shard_map/ppermute | solution.py:217
  135.1 8.1 %collective-permute-start.35 = (f32[64,512]{1,0:T(8,128)S(1)}, f32[64,512]{1,0:T(8,128)S(1)}, u32[]{:S(2)}, u32[]{:S(2)}) collective-permute-start(f32[64,512]{1,0:T(8,128)S(1)} %get-tuple-element.95), channel_id=1, source_target_pairs={{0,6},{1,7},{2,4},{3,5},{4,2},{5,3},{6,0},{7,1},{8,14},{9,15},{10,... | collective-permute-start | bytes 393224 | tf_op jit(solution)/shard_map/ppermute | solution.py:217
  137.8 6.6 %collective-permute-start.33 = (f32[64,512]{1,0:T(8,128)S(1)}, f32[64,512]{1,0:T(8,128)S(1)}, u32[]{:S(2)}, u32[]{:S(2)}) collective-permute-start(f32[64,512]{1,0:T(8,128)S(1)} %get-tuple-element.97), channel_id=1, source_target_pairs={{0,2},{1,3},{2,0},{3,1},{4,6},{5,7},{6,4},{7,5},{8,10},{9,11},{10,... | collective-permute-start | bytes 393224 | tf_op jit(solution)/shard_map/ppermute | solution.py:217
  138.2 9.7 %collective-permute-start.34 = (f32[64,512]{1,0:T(8,128)S(1)}, f32[64,512]{1,0:T(8,128)S(1)}, u32[]{:S(2)}, u32[]{:S(2)}) collective-permute-start(f32[64,512]{1,0:T(8,128)S(1)} %get-tuple-element.98), channel_id=1, source_target_pairs={{0,4},{1,5},{2,6},{3,7},{4,0},{5,1},{6,2},{7,3},{8,12},{9,13},{10,... | collective-permute-start | bytes 393224 | tf_op jit(solution)/shard_map/ppermute | solution.py:217
  143.3 4.7 %copy-start.9 = (f32[64,512]{1,0:T(8,128)}, f32[64,512]{1,0:T(8,128)S(1)}, u32[]{:S(2)}) copy-start(f32[64,512]{1,0:T(8,128)S(1)} %collective-permute-done.35.refs_2_) | copy-start | bytes 393220
  144.4 3.6 %copy-start.10 = (f32[64,512]{1,0:T(8,128)}, f32[64,512]{1,0:T(8,128)S(1)}, u32[]{:S(2)}) copy-start(f32[64,512]{1,0:T(8,128)S(1)} %collective-permute-done.33.refs_0_) | copy-start | bytes 393220
  151.1 1.5 collective-permute-start.36
  (4 other events, 2.8 us)

commit v3 on v2

--- a/solution.py
+++ b/solution.py
@@ -8,7 +8,7 @@
 from jax.experimental.pallas import tpu as pltpu
 from jax.sharding import PartitionSpec as P
 
-VMEM_BYTES = 56 * 2**20
+VMEM_BYTES = 40 * 2**20
 NEAR_COST, FAR_COST = 40, 0
 EARLY, PINS = 2, 2
 TIE1, TIE2 = 2, 3
@@ -44,7 +44,7 @@
     return one(a[0], b[0]) + (one(a[0], b[1]) + one(a[1], b[0]))
 
 
-def call(kernel, out_shape, table, *args, grid=(), in_specs=None, out_specs=None, scratch_shapes=(), flops=0):
+def call(kernel, out_shape, table, *args, grid=(), in_specs=None, out_specs=None, scratch_shapes=(), flops=0, grant=VMEM_BYTES):
     whole = lambda a: pl.BlockSpec(a.shape, lambda *_: (0,) * len(a.shape))
     outs = list(out_shape)
     return pl.pallas_call(
@@ -57,7 +57,7 @@
             out_specs=out_specs or [whole(a) for a in outs],
             scratch_shapes=list(scratch_shapes),
         ),
-        compiler_params=pltpu.CompilerParams(vmem_limit_bytes=VMEM_BYTES),
+        compiler_params=pltpu.CompilerParams(vmem_limit_bytes=grant),
         cost_estimate=pl.CostEstimate(flops=flops, bytes_accessed=sum(4 * a.size for a in args), transcendentals=0),
     )(table, *args)
 
@@ -129,29 +129,69 @@
     projected_ref[...] = dot3(near, (near_high_ref[...], near_low_ref[...]), LANES_OVER_LANES)
 
 
-def moment_kernel(scale_inv, n_high, table, *refs):
+def columns_of(near, far, width, core, highs):
+    parts = []
+    for h in highs:
+        at = core * width if h == 0 else (2 * (h - 1) + core) * width
+        parts.append((near if h == 0 else far)[:, at : at + width])
+    return parts
+
+
+def store_moments(ref, squared, scale_inv, columns):
+    at = 0
+    for high, low in columns:
+        width = high.shape[1]
+        ref[:, at : at + width] = scale_inv * dot3(squared, (high, low))
+        at += width
+
+
+def sent_kernel(scale_inv, n_high, table, *refs):
     projected_ref, comp_high_ref, comp_low_ref, near_high_ref, near_low_ref, *refs = refs
-    *pieces, out0_ref, out1_ref, high_ref, low_ref = refs
+    *pieces, a_ref, b_ref, sq_high_ref, sq_low_ref, far_high_ref, far_low_ref = refs
 
     @pl.when(pl.program_id(0) == 0)
     def _():
         height = pieces[0].shape[0]
         for k, ref in enumerate(pieces):
             rows = slice(k * height, (k + 1) * height)
-            high_ref[rows, :], low_ref[rows, :] = split(ref[...])
+            far_high_ref[rows, :], far_low_ref[rows, :] = split(ref[...])
 
     projected = projected_ref[...] + dot3(
-        (comp_high_ref[...], comp_low_ref[...]), (high_ref[...], low_ref[...]), LANES_OVER_LANES
+        (comp_high_ref[...], comp_low_ref[...]), (far_high_ref[...], far_low_ref[...]), LANES_OVER_LANES
     )
     squared = split(projected * projected)
-    near = dot3(squared, (near_high_ref[...], near_low_ref[...])) * scale_inv
-    far = dot3(squared, (high_ref[...], low_ref[...])) * scale_inv
-    width = near.shape[1] // 2
-    for core, ref in enumerate((out0_ref, out1_ref)):
-        ref[:, :width] = near[:, core * width : (core + 1) * width]
-        for h in range(1, n_high):
-            at = (2 * (h - 1) + core) * width
-            ref[:, h * width : (h + 1) * width] = far[:, at : at + width]
+    sq_high_ref[...], sq_low_ref[...] = squared
+    width = near_high_ref.shape[1] // 2
+
+    def columns(core, highs):
+        return zip(
+            columns_of(near_high_ref, far_high_ref, width, core, highs),
+            columns_of(near_low_ref, far_low_ref, width, core, highs),
+        )
+
+    store_moments(a_ref, squared, scale_inv, columns(0, range(n_high // 2, n_high)))
+
+    @pl.when(pl.program_id(0) == 1)
+    def _():
+        store_moments(b_ref, squared, scale_inv, columns(1, range(n_high)))
+
+
+def kept_kernel(scale_inv, n_high, table, *refs):
+    sq_high_ref, sq_low_ref, near_high_ref, near_low_ref, far_high_ref, far_low_ref, a_ref, b_ref = refs
+    squared = sq_high_ref[...], sq_low_ref[...]
+    width = near_high_ref.shape[1] // 2
+
+    def columns(core, highs):
+        return zip(
+            columns_of(near_high_ref, far_high_ref, width, core, highs),
+            columns_of(near_low_ref, far_low_ref, width, core, highs),
+        )
+
+    store_moments(a_ref, squared, scale_inv, columns(0, range(n_high // 2)))
+
+    @pl.when(pl.program_id(0) == 0)
+    def _():
+        store_moments(b_ref, squared, scale_inv, columns(1, range(n_high)))
 
 
 def divide_kernel(core_at, table, own_ref, *refs):
@@ -312,34 +352,44 @@
         far_sum = arrived + held[1]
         far_rows = [far_sum, swap(far_sum, 1)]
         scale_inv = float((samples.shape[0] * n_rows) ** -0.5)
-        tile = n_tall // 2
+        tile, wide = n_tall // 2, n_wide // 2
         whole = lambda a: pl.BlockSpec(a.shape, lambda i, t: (0, 0))
         tiled = lambda a: pl.BlockSpec((tile, a.shape[1]), lambda i, t: (i, 0))
-        half_wide = n_high * (n_wide // 2)
-        a, b = call(
-            functools.partial(moment_kernel, scale_inv, n_high),
-            [f32(n_tall, half_wide)] * 2,
+        half_a, half_b = f32(n_tall, n_high // 2 * wide), f32(tile, n_high * wide)
+        squares, rows_split = [bf16(n_tall, n_deep)] * 2, [bf16(n_deep, f_wide)] * 2
+        a_sent, b_sent, *squared_and_far = call(
+            functools.partial(sent_kernel, scale_inv, n_high),
+            [half_a, half_b] + squares + rows_split,
             table,
             *near_side,
             *far_rows,
-            grid=(n_tall // tile,),
+            grid=(2,),
             in_specs=[tiled(x) for x in near_side[:3]] + [whole(x) for x in near_side[3:]] + [whole(x) for x in far_rows],
-            out_specs=[pl.BlockSpec((tile, half_wide), lambda i, t: (i, 0))] * 2,
-            scratch_shapes=[pltpu.VMEM((n_deep, f_wide), jnp.bfloat16)] * 2,
-            flops=6 * n_tall * n_deep * (n_wide + 2 * f_wide),
-        )
-
-        def over_rows(x):
-            for bit in high_bits[::-1]:
+            out_specs=[tiled(half_a), whole(half_b)] + [tiled(x) for x in squares] + [whole(x) for x in rows_split],
+            flops=6 * n_tall * n_deep * (f_wide + n_wide // 2 * n_high),
+        )
+        a_kept, b_kept = call(
+            functools.partial(kept_kernel, scale_inv, n_high),
+            [half_a, half_b],
+            table,
+            *squared_and_far[:2],
+            *near_side[3:],
+            *squared_and_far[2:],
+            grid=(2,),
+            in_specs=[tiled(x) for x in squares] + [whole(x) for x in near_side[3:]] + [whole(x) for x in rows_split],
+            out_specs=[tiled(half_a), whole(half_b)],
+            flops=6 * n_tall * n_deep * (n_wide // 2 * n_high),
+        )
+
+        def over_rows(x, bits):
+            for bit in bits:
                 half = x.shape[1] // 2
                 x = x[:, :half] + swap(x[:, half:], bit)
             return x
 
-        def over_first_bit(x):
-            half = x.shape[0] // 2
-            return x[:half] + swap_feat(x[half:], 1)
-
-        a, b = over_first_bit(over_rows(a)), over_rows(over_first_bit(b))
+        a = over_rows(a_kept + swap(a_sent, high_bits[-1]), high_bits[-2::-1])
+        a = a[:tile] + swap_feat(a[tile:], 1)
+        b = over_rows(b_kept + swap_feat(b_sent, 1), high_bits[::-1])
         joint = jnp.concatenate([a, b], axis=1)
         step = joint.shape[0] // (n_feat // 2)
         parts = [joint[k * step : (k + 1) * step] for k in range(n_feat // 2)]

time: 156 us -> 137 us (0.88)
  Pallas kernels: 43.4 us -> 23.8 us
  waiting for transfers between devices: 57.7 us -> 69.8 us
  local copies, waits for them, and re-layouts: 12.6 us -> 5.91 us
  other arithmetic: 6.57 us -> 1.44 us
    pallas_call x8 -> x9, Pallas kernels: 43.4 us -> 23.8 us  [call(): pl.pallas_call(kernel, out_shape=outs, grid_spec=pltpu.PrefetchScalarGrid...]
    ppermute x5, waiting for transfers between devices: 21.1 us -> 14 us  [swap_feat(): return lax.ppermute(a, 'feat', [(i, i ^ bit) for i in range(n_feat)])]
    ppermute x1, waiting for transfers between devices: 1.8 us -> 7.04 us  [on_device(): arrived = lax.ppermute(held[0], both, streams[0])]
    ppermute x12, waiting for transfers between devices: 14.9 us -> 19.9 us  [rounds(): held[s] = lax.ppermute(held[s], both, streams[s]) + piece]
    ppermute x11, waiting for transfers between devices: 10.7 us -> 15.7 us  [swap(): return lax.ppermute(a, 'rows', [(i, i ^ bit) for i in range(n_rows)])]
    slice x2, local copies, waits for them, and re-layouts: 3.22 us -> 0.11 us  [rounds(): piece = source[at_row * height:(at_row + 1) * height]]
    ppermute x4, waiting for transfers between devices: 7.65 us -> 10.6 us  [pass_components(): line[step] = lax.ppermute(line[step - 1], both, streams[0])]
    add x6, other arithmetic: 2.9 us -> 0.67 us  [rounds(): held[s] = lax.ppermute(held[s], both, streams[s]) + piece]
  transfers between devices with their start and end apart: 37 -> 37, of which waited for: 19 -> 18; matrix products, arithmetic and copies ran while one was open for 8% -> 2% of each run, Pallas kernels for 21% -> 13%
where the time goes in v3:
time: 137 us
  waiting for transfers between devices  69.8 us (51%)
  starting transfers between devices  35.1 us (26%)
  Pallas kernels  23.8 us (17%)
  local copies, waits for them, and re-layouts  5.91 us (4%)
  other arithmetic  1.44 us (1%)
    pallas_call x9, Pallas kernels, call(): pl.pallas_call(kernel, out_shape=outs, grid_spec=pltpu.PrefetchScalarGrid...  23.8 us
    ppermute x12, waiting for transfers between devices, rounds(): held[s] = lax.ppermute(held[s], both, streams[s]) + piece  19.9 us
    ppermute x11, waiting for transfers between devices, swap(): return lax.ppermute(a, 'rows', [(i, i ^ bit) for i in range(n_rows)])  15.7 us
    ppermute x5, waiting for transfers between devices, swap_feat(): return lax.ppermute(a, 'feat', [(i, i ^ bit) for i in range(n_feat)])  14 us
    ppermute x12, starting transfers between devices, rounds(): held[s] = lax.ppermute(held[s], both, streams[s]) + piece  13.9 us
    ppermute x4, waiting for transfers between devices, pass_components(): line[step] = lax.ppermute(line[step - 1], both, streams[0])  10.6 us
    ppermute x5, starting transfers between devices, swap_feat(): return lax.ppermute(a, 'feat', [(i, i ^ bit) for i in range(n_feat)])  7.34 us
    ppermute x1, waiting for transfers between devices, on_device(): arrived = lax.ppermute(held[0], both, streams[0])  7.04 us
  transfers between devices with their start and end apart: 37, of which 18 were waited for; matrix products, arithmetic and copies ran while one was open for 2% of the time, Pallas kernels for 13%

profile of v3, /device:TPU:0, one launch (start us, length us, event | category | flops | bytes accessed | tf_op | source)
XLA Modules:
  0.0 136.5 jit_solution(4302707802379080867)
XLA Ops:
  0.5 2.5 %collective-permute-start = (f32[1024,256]{1,0:T(8,128)}, f32[1024,256]{1,0:T(8,128)S(1)}, u32[]{:S(2)}, u32[]{:S(2)}) collective-permute-start(f32[1024,256]{1,0:T(8,128)} %refs_2_.3), channel_id=1, source_target_pairs={{0,16},{8,24},{16,0},{24,8},{1,17},{9,25},{17,1},{25,9},{2,18},{10... | collective-permute-start | bytes 3145736 | tf_op jit(solution)/shard_map/ppermute | solution.py:254
  3.0 1.0 copy.7
  4.3 0.7 fusion.5.table
  5.4 1.5 %collective-permute-start.4 = (f32[64,512]{1,0:T(8,128)S(1)}, f32[64,512]{1,0:T(8,128)S(1)}, u32[]{:S(2)}, u32[]{:S(2)}) collective-permute-start(f32[64,512]{1,0:T(8,128)S(1)} %pad_maximum_fusion.4), channel_id=1, source_target_pairs={{0,1},{2,0},{4,2},{6,4},{7,6},{5,7},{3,5},{1,3},{8,10},{10,12},{12... | collective-permute-start | bytes 393224 | tf_op jit(solution)/shard_map/ppermute | solution.py:302
  7.4 2.8 %copy-done = f32[1536,1024]{1,0:T(8,128)S(1)} copy-done((f32[1536,1024]{1,0:T(8,128)S(1)}, f32[1536,1024]{1,0:T(8,128)}, u32[]{:S(2)}) %copy-start) | copy-done | bytes 6291480
  10.2 1.2 copy-done.1
  11.5 2.2 %shard_map.46 = f32[384,512]{1,0:T(8,128)S(1)} custom-call(s32[17]{0:T(128)S(1)} %fusion.5.table, f32[1536,1024]{1,0:T(8,128)S(1)} %copy-done, f32[1536,1024]{1,0:T(8,128)S(1)} %copy-done, f32[1024,256]{1,0:T(8,128)S(1)} %copy-done.1, f32[1024,256]{1,0:T(8,128)S(1)} %collective-permute-done.1.refs_3_), custom_call_target="tpu_custom_call" | custom-call | flops 16106127360 | bytes 14680064 | tf_op jit(solution)/shard_map/pallas_call | solution.py:50
  13.8 1.6 %collective-permute-start.7 = (f32[64,512]{1,0:T(8,128)S(1)}, f32[64,512]{1,0:T(8,128)S(1)}, u32[]{:S(2)}, u32[]{:S(2)}) collective-permute-start(f32[64,512]{1,0:T(8,128)S(1)} %collective-permute-done.3), channel_id=1, source_target_pairs={{0,2},{2,4},{4,6},{6,7},{7,5},{5,3},{3,1},{1,0},{8,9},{10,8},{12,1... | collective-permute-start | bytes 393224 | tf_op jit(solution)/shard_map/ppermute | solution.py:300
  15.9 1.5 %collective-permute-start.6 = (f32[192,512]{1,0:T(8,128)S(1)}, f32[192,512]{1,0:T(8,128)S(1)}, u32[]{:S(2)}, u32[]{:S(2)}) collective-permute-start(f32[192,512]{1,0:T(8,128)S(1)} %get-tuple-element.105), channel_id=1, source_target_pairs={{0,1},{2,0},{4,2},{6,4},{7,6},{5,7},{3,5},{1,3},{8,10},{10,12},{12... | collective-permute-start | bytes 1179656 | tf_op jit(solution)/shard_map/ppermute | solution.py:282
  17.9 5.1 %shard_map.47 = f32[1152,512]{1,0:T(8,128)S(1)} custom-call(s32[17]{0:T(128)S(1)} %fusion.5.table, f32[1536,1024]{1,0:T(8,128)S(1)} %copy-done, f32[1536,1024]{1,0:T(8,128)S(1)} %copy-done, f32[1024,256]{1,0:T(8,128)S(1)} %copy-done.1, f32[1024,256]{1,0:T(8,128)S(1)} %collective-permute-done.1.refs_3_), custom_call_target="tpu_custom_call" | custom-call | flops 48318382080 | bytes 14680064 | tf_op jit(solution)/shard_map/pallas_call | solution.py:50
  23.0 5.7 %collective-permute-done.6 = f32[192,512]{1,0:T(8,128)S(1)} collective-permute-done((f32[192,512]{1,0:T(8,128)S(1)}, f32[192,512]{1,0:T(8,128)S(1)}, u32[]{:S(2)}, u32[]{:S(2)}) %collective-permute-start.6) | collective-permute-done | bytes 393248 | tf_op jit(solution)/shard_map/ppermute | solution.py:282
  29.1 1.6 %collective-permute-start.21 = (f32[192,512]{1,0:T(8,128)S(1)}, f32[192,512]{1,0:T(8,128)S(1)}, u32[]{:S(2)}, u32[]{:S(2)}) collective-permute-start(f32[192,512]{1,0:T(8,128)S(1)} %get-tuple-element.67), channel_id=1, source_target_pairs={{0,2},{2,4},{4,6},{6,7},{7,5},{5,3},{3,1},{1,0},{8,9},{10,8},{12,1... | collective-permute-start | bytes 1179656 | tf_op jit(solution)/shard_map/ppermute | solution.py:282
  30.7 0.9 collective-permute-done.9.refs_3_
  31.6 2.3 %shard_map.48 = f32[384,512]{1,0:T(8,128)S(1)} custom-call(s32[17]{0:T(128)S(1)} %fusion.5.table, f32[1536,1024]{1,0:T(8,128)S(1)} %copy-done, f32[1536,1024]{1,0:T(8,128)S(1)} %copy-done, f32[1024,256]{1,0:T(8,128)S(1)} %collective-permute-done.refs_2_, f32[1024,256]{1,0:T(8,128)S(1)} %collective-permute-done.9.refs_3_), custom_call_target="tpu_custom_call" | custom-call | bytes 14680064 | tf_op jit(solution)/shard_map/pallas_call | solution.py:50
  33.9 1.4 %collective-permute-start.11 = (f32[192,512]{1,0:T(8,128)S(1)}, f32[192,512]{1,0:T(8,128)S(1)}, u32[]{:S(2)}, u32[]{:S(2)}) collective-permute-start(f32[192,512]{1,0:T(8,128)S(1)} %get-tuple-element.103), channel_id=1, source_target_pairs={{0,1},{2,0},{4,2},{6,4},{7,6},{5,7},{3,5},{1,3},{8,10},{10,12},{12... | collective-permute-start | bytes 1179656 | tf_op jit(solution)/shard_map/ppermute | solution.py:282
  35.4 0.6 collective-permute-start.10
  36.6 1.4 %collective-permute-start.24 = (f32[192,512]{1,0:T(8,128)S(1)}, f32[192,512]{1,0:T(8,128)S(1)}, u32[]{:S(2)}, u32[]{:S(2)}) collective-permute-start(f32[192,512]{1,0:T(8,128)S(1)} %get-tuple-element.68), channel_id=1, source_target_pairs={{0,1},{2,0},{4,2},{6,4},{7,6},{5,7},{3,5},{1,3},{8,10},{10,12},{12... | collective-permute-start | bytes 1179656 | tf_op jit(solution)/shard_map/ppermute | solution.py:282
  38.7 5.1 %shard_map.49 = f32[1152,512]{1,0:T(8,128)S(1)} custom-call(s32[17]{0:T(128)S(1)} %fusion.5.table, f32[1536,1024]{1,0:T(8,128)S(1)} %copy-done, f32[1536,1024]{1,0:T(8,128)S(1)} %copy-done, f32[1024,256]{1,0:T(8,128)S(1)} %collective-permute-done.refs_2_, f32[1024,256]{1,0:T(8,128)S(1)} %collective-permute-done.9.refs_3_), custom_call_target="tpu_custom_call" | custom-call | bytes 14680064 | tf_op jit(solution)/shard_map/pallas_call | solution.py:50
  43.8 6.4 %collective-permute-done.15 = f32[64,512]{1,0:T(8,128)S(1)} collective-permute-done((f32[64,512]{1,0:T(8,128)S(1)}, f32[64,512]{1,0:T(8,128)S(1)}, u32[]{:S(2)}, u32[]{:S(2)}) %collective-permute-start.15) | collective-permute-done | bytes 131104 | tf_op jit(solution)/shard_map/ppermute | solution.py:300
  50.9 1.4 %collective-permute-start.17 = (f32[64,512]{1,0:T(8,128)S(1)}, f32[64,512]{1,0:T(8,128)S(1)}, u32[]{:S(2)}, u32[]{:S(2)}) collective-permute-start(f32[64,512]{1,0:T(8,128)S(1)} %collective-permute-done.8), channel_id=1, source_target_pairs={{0,1},{2,0},{4,2},{6,4},{7,6},{5,7},{3,5},{1,3},{8,10},{10,12},{12... | collective-permute-start | bytes 393224 | tf_op jit(solution)/shard_map/ppermute | solution.py:302
  53.0 1.6 %collective-permute-start.13 = (f32[192,512]{1,0:T(8,128)S(1)}, f32[192,512]{1,0:T(8,128)S(1)}, u32[]{:S(2)}, u32[]{:S(2)}) collective-permute-start(f32[192,512]{1,0:T(8,128)S(1)} %get-tuple-element.60), channel_id=1, source_target_pairs={{0,2},{2,4},{4,6},{6,7},{7,5},{5,3},{3,1},{1,0},{8,9},{10,8},{12,1... | collective-permute-start | bytes 1179656 | tf_op jit(solution)/shard_map/ppermute | solution.py:282
  54.7 2.6 %collective-permute-done.17 = f32[64,512]{1,0:T(8,128)S(1)} collective-permute-done((f32[64,512]{1,0:T(8,128)S(1)}, f32[64,512]{1,0:T(8,128)S(1)}, u32[]{:S(2)}, u32[]{:S(2)}) %collective-permute-start.17) | collective-permute-done | bytes 131104 | tf_op jit(solution)/shard_map/ppermute | solution.py:302
  57.3 1.4 %collective-permute-start.14 = (f32[192,512]{1,0:T(8,128)S(1)}, f32[192,512]{1,0:T(8,128)S(1)}, u32[]{:S(2)}, u32[]{:S(2)}) collective-permute-start(f32[192,512]{1,0:T(8,128)S(1)} %get-tuple-element.61), channel_id=1, source_target_pairs={{0,1},{2,0},{4,2},{6,4},{7,6},{5,7},{3,5},{1,3},{8,10},{10,12},{12... | collective-permute-start | bytes 1179656 | tf_op jit(solution)/shard_map/ppermute | solution.py:282
  58.7 4.2 %collective-permute-done.16 = f32[64,512]{1,0:T(8,128)S(1)} collective-permute-done((f32[64,512]{1,0:T(8,128)S(1)}, f32[64,512]{1,0:T(8,128)S(1)}, u32[]{:S(2)}, u32[]{:S(2)}) %collective-permute-start.16) | collective-permute-done | bytes 131104 | tf_op jit(solution)/shard_map/ppermute | solution.py:300
  62.9 0.6 collective-permute-start.18
  63.7 2.1 %collective-permute-start.25 = (f32[192,512]{1,0:T(8,128)S(1)}, f32[192,512]{1,0:T(8,128)S(1)}, u32[]{:S(2)}, u32[]{:S(2)}) collective-permute-start(f32[192,512]{1,0:T(8,128)S(1)} %get-tuple-element.95), channel_id=1, source_target_pairs={{0,1},{2,0},{4,2},{6,4},{7,6},{5,7},{3,5},{1,3},{8,10},{10,12},{12... | collective-permute-start | bytes 1179656 | tf_op jit(solution)/shard_map/ppermute | solution.py:282
  65.8 5.5 %collective-permute-done.13 = f32[192,512]{1,0:T(8,128)S(1)} collective-permute-done((f32[192,512]{1,0:T(8,128)S(1)}, f32[192,512]{1,0:T(8,128)S(1)}, u32[]{:S(2)}, u32[]{:S(2)}) %collective-permute-start.13) | collective-permute-done | bytes 393248 | tf_op jit(solution)/shard_map/ppermute | solution.py:282
  71.7 6.1 %collective-permute-done.25 = f32[192,512]{1,0:T(8,128)S(1)} collective-permute-done((f32[192,512]{1,0:T(8,128)S(1)}, f32[192,512]{1,0:T(8,128)S(1)}, u32[]{:S(2)}, u32[]{:S(2)}) %collective-permute-start.25) | collective-permute-done | bytes 393248 | tf_op jit(solution)/shard_map/ppermute | solution.py:282
  78.0 2.5 %collective-permute-done.19 = f32[192,512]{1,0:T(8,128)S(1)} collective-permute-done((f32[192,512]{1,0:T(8,128)S(1)}, f32[192,512]{1,0:T(8,128)S(1)}, u32[]{:S(2)}, u32[]{:S(2)}) %collective-permute-start.19) | collective-permute-done | bytes 393248 | tf_op jit(solution)/shard_map/ppermute | solution.py:282
  80.6 1.3 collective-permute-start.20
  81.8 0.8 collective-permute-start.27
  82.9 1.6 %shard_map.50 = (f32[512,384]{1,0:T(8,128)S(1)}, bf16[512,512]{1,0:T(8,128)(2,1)S(1)}, bf16[512,512]{1,0:T(8,128)(2,1)S(1)}, bf16[384,512]{1,0:T(8,128)(2,1)S(1)}, bf16[384,512]{1,0:T(8,128)(2,1)S(1)}) custom-call(s32[17]{0:T(128)S(1)} %fusion.5.table, f32[192,512]{1,0:T(8,128)S(1)} %fusion.1.refs_0_, f32[192,512]{1,0:T(8,128)S(1)} %collective-permute-done.26.refs_1_, ...), custom_call_target="tpu_custom_call" | custom-call | flops 603979776 | bytes 2883584 | tf_op jit(solution)/shard_map/pallas_call | solution.py:50
  84.5 7.0 %collective-permute-done.20 = f32[192,512]{1,0:T(8,128)S(1)} collective-permute-done((f32[192,512]{1,0:T(8,128)S(1)}, f32[192,512]{1,0:T(8,128)S(1)}, u32[]{:S(2)}, u32[]{:S(2)}) %collective-permute-start.20) | collective-permute-done | bytes 393248 | tf_op jit(solution)/shard_map/ppermute | solution.py:350
  91.8 1.7 %collective-permute-done.28.refs_6_ = f32[192,512]{1,0:T(8,128)S(1)} collective-permute-done((f32[192,512]{1,0:T(8,128)S(1)}, f32[192,512]{1,0:T(8,128)S(1)}, u32[]{:S(2)}, u32[]{:S(2)}) %collective-permute-start.28) | collective-permute-done | bytes 393248 | tf_op jit(solution)/shard_map/ppermute | solution.py:254
  93.5 3.7 %shard_map.51 = (f32[512,256]{1,0:T(8,128)S(1)}, f32[256,512]{1,0:T(8,128)S(1)}, bf16[512,384]{1,0:T(8,128)(2,1)S(1)}, bf16[512,384]{1,0:T(8,128)(2,1)S(1)}, bf1...) custom-call(s32[17]{0:T(128)S(1)} %fusion.5.table, f32[512,384]{1,0:T(8,128)S(1)} %get-tuple-element.78.refs_0_, ...), custom_call_target="tpu_custom_call" | custom-call | flops 1207959552 | bytes 5242880 | tf_op jit(solution)/shard_map/pallas_call | solution.py:50
  97.7 1.4 %collective-permute-start.31 = (f32[256,512]{1,0:T(8,128)S(1)}, f32[256,512]{1,0:T(8,128)S(1)}, u32[]{:S(2)}, u32[]{:S(2)}) collective-permute-start(f32[256,512]{1,0:T(8,128)S(1)} %get-tuple-element.92), channel_id=1, source_target_pairs={{0,1},{1,0},{2,3},{3,2},{4,5},{5,4},{6,7},{7,6},{8,9},{9,8},{10,11... | collective-permute-start | bytes 1572872 | tf_op jit(solution)/shard_map/ppermute | solution.py:257
  99.1 1.9 %shard_map.52 = (f32[512,256]{1,0:T(8,128)S(1)}, f32[256,512]{1,0:T(8,128)S(1)}) custom-call(s32[17]{0:T(128)S(1)} %fusion.5.table, bf16[512,384]{1,0:T(8,128)(2,1)S(1)} %get-tuple-element.85.refs_0_, bf16[512,384]{1,0:T(8,128)(2,1)S(1)} %get-tuple-element.86.refs_1_, bf16[384,512]{1,0:T(8,128)(2,1)S(1)} %get-tuple-element.81.refs_3_.refs_2_, ...), custom_call_target="tpu_custom_call" | custom-call | flops 603979776 | bytes 4718592 | tf_op jit(solution)/shard_map/pallas_call | solution.py:50
  101.0 10.2 %collective-permute-done.29 = f32[512,256]{1,0:T(8,128)S(1)} collective-permute-done((f32[512,256]{1,0:T(8,128)S(1)}, f32[512,256]{1,0:T(8,128)S(1)}, u32[]{:S(2)}, u32[]{:S(2)}) %collective-permute-start.29) | collective-permute-done | bytes 524320 | tf_op jit(solution)/shard_map/ppermute | solution.py:254
  111.3 1.5 %collective-permute-start.30 = (f32[256,256]{1,0:T(8,128)S(1)}, f32[256,256]{1,0:T(8,128)S(1)}, u32[]{:S(2)}, u32[]{:S(2)}) collective-permute-start(f32[256,256]{1,0:T(8,128)S(1)} %slice.109), channel_id=1, source_target_pairs={{0,1},{1,0},{2,3},{3,2},{4,5},{5,4},{6,7},{7,6},{8,9},{9,8},{10,11... | collective-permute-start | bytes 786440 | tf_op jit(solution)/shard_map/ppermute | solution.py:257
  113.5 5.4 %collective-permute-done.30 = f32[256,256]{1,0:T(8,128)S(1)} collective-permute-done((f32[256,256]{1,0:T(8,128)S(1)}, f32[256,256]{1,0:T(8,128)S(1)}, u32[]{:S(2)}, u32[]{:S(2)}) %collective-permute-start.30) | collective-permute-done | bytes 262176 | tf_op jit(solution)/shard_map/ppermute | solution.py:257
  118.9 1.2 collective-permute-done.32
  120.3 2.7 %collective-permute-start.35 = (f32[64,512]{1,0:T(8,128)S(1)}, f32[64,512]{1,0:T(8,128)S(1)}, u32[]{:S(2)}, u32[]{:S(2)}) collective-permute-start(f32[64,512]{1,0:T(8,128)S(1)} %get-tuple-element.107), channel_id=1, source_target_pairs={{0,6},{1,7},{2,4},{3,5},{4,2},{5,3},{6,0},{7,1},{8,14},{9,15},{10,... | collective-permute-start | bytes 393224 | tf_op jit(solution)/shard_map/ppermute | solution.py:257
  123.3 1.4 %collective-permute-start.34 = (f32[64,512]{1,0:T(8,128)S(1)}, f32[64,512]{1,0:T(8,128)S(1)}, u32[]{:S(2)}, u32[]{:S(2)}) collective-permute-start(f32[64,512]{1,0:T(8,128)S(1)} %get-tuple-element.110), channel_id=1, source_target_pairs={{0,4},{1,5},{2,6},{3,7},{4,0},{5,1},{6,2},{7,3},{8,12},{9,13},{10,... | collective-permute-start | bytes 393224 | tf_op jit(solution)/shard_map/ppermute | solution.py:257
  124.7 3.9 %collective-permute-done.35.refs_2_ = f32[64,512]{1,0:T(8,128)S(1)} collective-permute-done((f32[64,512]{1,0:T(8,128)S(1)}, f32[64,512]{1,0:T(8,128)S(1)}, u32[]{:S(2)}, u32[]{:S(2)}) %collective-permute-start.35) | collective-permute-done | bytes 131104 | tf_op jit(solution)/shard_map/ppermute | solution.py:257
  128.6 0.9 collective-permute-done.33.refs_0_
  129.6 3.8 %collective-permute-done.34.refs_1_ = f32[64,512]{1,0:T(8,128)S(1)} collective-permute-done((f32[64,512]{1,0:T(8,128)S(1)}, f32[64,512]{1,0:T(8,128)S(1)}, u32[]{:S(2)}, u32[]{:S(2)}) %collective-permute-start.34) | collective-permute-done | bytes 131104 | tf_op jit(solution)/shard_map/ppermute | solution.py:257
  134.0 1.2 collective-permute-done.36.other_ref
  135.2 1.3 shard_map.54
  (68 shorter events, 9.2 us)
Async XLA Ops:
  0.0 7.4 %collective-permute-start.1 = (f32[1024,256]{1,0:T(8,128)}, f32[1024,256]{1,0:T(8,128)S(1)}, u32[]{:S(2)}, u32[]{:S(2)}) collective-permute-start(f32[1024,256]{1,0:T(8,128)} %refs_2_.3), channel_id=1, source_target_pairs={{0,8},{8,0},{16,24},{24,16},{1,9},{9,1},{17,25},{25,17},{2,10},{10... | collective-permute-start | bytes 3145736 | tf_op jit(solution)/shard_map/ppermute | solution.py:254
  0.5 28.4 %collective-permute-start = (f32[1024,256]{1,0:T(8,128)}, f32[1024,256]{1,0:T(8,128)S(1)}, u32[]{:S(2)}, u32[]{:S(2)}) collective-permute-start(f32[1024,256]{1,0:T(8,128)} %refs_2_.3), channel_id=1, source_target_pairs={{0,16},{8,24},{16,0},{24,8},{1,17},{9,25},{17,1},{25,9},{2,18},{10... | collective-permute-start | bytes 3145736 | tf_op jit(solution)/shard_map/ppermute | solution.py:254
  4.0 1.3 collective-permute-start.2
  5.4 8.4 %collective-permute-start.4 = (f32[64,512]{1,0:T(8,128)S(1)}, f32[64,512]{1,0:T(8,128)S(1)}, u32[]{:S(2)}, u32[]{:S(2)}) collective-permute-start(f32[64,512]{1,0:T(8,128)S(1)} %pad_maximum_fusion.4), channel_id=1, source_target_pairs={{0,1},{2,0},{4,2},{6,4},{7,6},{5,7},{3,5},{1,3},{8,10},{10,12},{12... | collective-permute-start | bytes 393224 | tf_op jit(solution)/shard_map/ppermute | solution.py:302
  6.9 6.8 %collective-permute-start.3 = (f32[64,512]{1,0:T(8,128)S(1)}, f32[64,512]{1,0:T(8,128)S(1)}, u32[]{:S(2)}, u32[]{:S(2)}) collective-permute-start(f32[64,512]{1,0:T(8,128)S(1)} %pad_maximum_fusion.4), channel_id=1, source_target_pairs={{0,2},{2,4},{4,6},{6,7},{7,5},{5,3},{3,1},{1,0},{8,9},{10,8},{12,1... | collective-permute-start | bytes 393224 | tf_op jit(solution)/shard_map/ppermute | solution.py:300
  7.4 2.8 %copy-start = (f32[1536,1024]{1,0:T(8,128)S(1)}, f32[1536,1024]{1,0:T(8,128)}, u32[]{:S(2)}) copy-start(f32[1536,1024]{1,0:T(8,128)} %refs_1_.7) | copy-start | bytes 18874372
  10.2 1.2 copy-start.1
  13.8 15.1 %collective-permute-start.7 = (f32[64,512]{1,0:T(8,128)S(1)}, f32[64,512]{1,0:T(8,128)S(1)}, u32[]{:S(2)}, u32[]{:S(2)}) collective-permute-start(f32[64,512]{1,0:T(8,128)S(1)} %collective-permute-done.3), channel_id=1, source_target_pairs={{0,2},{2,4},{4,6},{6,7},{7,5},{5,3},{3,1},{1,0},{8,9},{10,8},{12,1... | collective-permute-start | bytes 393224 | tf_op jit(solution)/shard_map/ppermute | solution.py:300
  15.4 13.5 %collective-permute-start.8 = (f32[64,512]{1,0:T(8,128)S(1)}, f32[64,512]{1,0:T(8,128)S(1)}, u32[]{:S(2)}, u32[]{:S(2)}) collective-permute-start(f32[64,512]{1,0:T(8,128)S(1)} %collective-permute-done.4), channel_id=1, source_target_pairs={{0,1},{2,0},{4,2},{6,4},{7,6},{5,7},{3,5},{1,3},{8,10},{10,12},{12... | collective-permute-start | bytes 393224 | tf_op jit(solution)/shard_map/ppermute | solution.py:302
  15.9 12.9 %collective-permute-start.6 = (f32[192,512]{1,0:T(8,128)S(1)}, f32[192,512]{1,0:T(8,128)S(1)}, u32[]{:S(2)}, u32[]{:S(2)}) collective-permute-start(f32[192,512]{1,0:T(8,128)S(1)} %get-tuple-element.105), channel_id=1, source_target_pairs={{0,1},{2,0},{4,2},{6,4},{7,6},{5,7},{3,5},{1,3},{8,10},{10,12},{12... | collective-permute-start | bytes 1179656 | tf_op jit(solution)/shard_map/ppermute | solution.py:282
  17.4 11.4 %collective-permute-start.5 = (f32[192,512]{1,0:T(8,128)S(1)}, f32[192,512]{1,0:T(8,128)S(1)}, u32[]{:S(2)}, u32[]{:S(2)}) collective-permute-start(f32[192,512]{1,0:T(8,128)S(1)} %get-tuple-element.106), channel_id=1, source_target_pairs={{0,2},{2,4},{4,6},{6,7},{7,5},{5,3},{3,1},{1,0},{8,9},{10,8},{12,1... | collective-permute-start | bytes 1179656 | tf_op jit(solution)/shard_map/ppermute | solution.py:282
  28.9 2.7 %collective-permute-start.9 = (f32[1024,256]{1,0:T(8,128)S(1)}, f32[1024,256]{1,0:T(8,128)S(1)}, u32[]{:S(2)}, u32[]{:S(2)}) collective-permute-start(f32[1024,256]{1,0:T(8,128)S(1)} %collective-permute-done.refs_2_), channel_id=1, source_target_pairs={{0,8},{8,0},{16,24},{24,16},{1,9},{9,1},{17,25},{25,17},{2,10},{10... | collective-permute-start | bytes 3145736 | tf_op jit(solution)/shard_map/ppermute | solution.py:254
  29.1 9.0 %collective-permute-start.21 = (f32[192,512]{1,0:T(8,128)S(1)}, f32[192,512]{1,0:T(8,128)S(1)}, u32[]{:S(2)}, u32[]{:S(2)}) collective-permute-start(f32[192,512]{1,0:T(8,128)S(1)} %get-tuple-element.67), channel_id=1, source_target_pairs={{0,2},{2,4},{4,6},{6,7},{7,5},{5,3},{3,1},{1,0},{8,9},{10,8},{12,1... | collective-permute-start | bytes 1179656 | tf_op jit(solution)/shard_map/ppermute | solution.py:282
  33.9 16.9 %collective-permute-start.11 = (f32[192,512]{1,0:T(8,128)S(1)}, f32[192,512]{1,0:T(8,128)S(1)}, u32[]{:S(2)}, u32[]{:S(2)}) collective-permute-start(f32[192,512]{1,0:T(8,128)S(1)} %get-tuple-element.103), channel_id=1, source_target_pairs={{0,1},{2,0},{4,2},{6,4},{7,6},{5,7},{3,5},{1,3},{8,10},{10,12},{12... | collective-permute-start | bytes 1179656 | tf_op jit(solution)/shard_map/ppermute | solution.py:282
  35.4 16.9 %collective-permute-start.10 = (f32[192,512]{1,0:T(8,128)S(1)}, f32[192,512]{1,0:T(8,128)S(1)}, u32[]{:S(2)}, u32[]{:S(2)}) collective-permute-start(f32[192,512]{1,0:T(8,128)S(1)} %get-tuple-element.104), channel_id=1, source_target_pairs={{0,2},{2,4},{4,6},{6,7},{7,5},{5,3},{3,1},{1,0},{8,9},{10,8},{12,1... | collective-permute-start | bytes 1179656 | tf_op jit(solution)/shard_map/ppermute | solution.py:282
  36.0 17.0 %collective-permute-start.12 = (f32[5,64,512]{2,1,0:T(8,128)S(1)}, f32[5,64,512]{2,1,0:T(8,128)S(1)}, u32[]{:S(2)}, u32[]{:S(2)}) collective-permute-start(f32[5,64,512]{2,1,0:T(8,128)S(1)} %bitcast_dynamic-update-slice_fusion), channel_id=1, source_target_pairs={{0,16},{8,24},{16,0},{24,8},{1,17},{9,25},{17,1},{25,9},{2,18},{10... | collective-permute-start | bytes 1966088 | tf_op jit(solution)/shard_map/ppermute | solution.py:254
  36.6 27.0 %collective-permute-start.24 = (f32[192,512]{1,0:T(8,128)S(1)}, f32[192,512]{1,0:T(8,128)S(1)}, u32[]{:S(2)}, u32[]{:S(2)}) collective-permute-start(f32[192,512]{1,0:T(8,128)S(1)} %get-tuple-element.68), channel_id=1, source_target_pairs={{0,1},{2,0},{4,2},{6,4},{7,6},{5,7},{3,5},{1,3},{8,10},{10,12},{12... | collective-permute-start | bytes 1179656 | tf_op jit(solution)/shard_map/ppermute | solution.py:282
  38.0 12.2 %collective-permute-start.15 = (f32[64,512]{1,0:T(8,128)S(1)}, f32[64,512]{1,0:T(8,128)S(1)}, u32[]{:S(2)}, u32[]{:S(2)}) collective-permute-start(f32[64,512]{1,0:T(8,128)S(1)} %collective-permute-done.7), channel_id=1, source_target_pairs={{0,2},{2,4},{4,6},{6,7},{7,5},{5,3},{3,1},{1,0},{8,9},{10,8},{12,1... | collective-permute-start | bytes 393224 | tf_op jit(solution)/shard_map/ppermute | solution.py:300
  50.3 13.3 %collective-permute-start.22 = (f32[192,512]{1,0:T(8,128)S(1)}, f32[192,512]{1,0:T(8,128)S(1)}, u32[]{:S(2)}, u32[]{:S(2)}) collective-permute-start(f32[192,512]{1,0:T(8,128)S(1)} %slice_add_fusion.4), channel_id=1, source_target_pairs={{0,2},{2,4},{4,6},{6,7},{7,5},{5,3},{3,1},{1,0},{8,9},{10,8},{12,1... | collective-permute-start | bytes 1179656 | tf_op jit(solution)/shard_map/ppermute | solution.py:282
  50.9 6.4 %collective-permute-start.17 = (f32[64,512]{1,0:T(8,128)S(1)}, f32[64,512]{1,0:T(8,128)S(1)}, u32[]{:S(2)}, u32[]{:S(2)}) collective-permute-start(f32[64,512]{1,0:T(8,128)S(1)} %collective-permute-done.8), channel_id=1, source_target_pairs={{0,1},{2,0},{4,2},{6,4},{7,6},{5,7},{3,5},{1,3},{8,10},{10,12},{12... | collective-permute-start | bytes 393224 | tf_op jit(solution)/shard_map/ppermute | solution.py:302
  52.3 10.6 %collective-permute-start.16 = (f32[64,512]{1,0:T(8,128)S(1)}, f32[64,512]{1,0:T(8,128)S(1)}, u32[]{:S(2)}, u32[]{:S(2)}) collective-permute-start(f32[64,512]{1,0:T(8,128)S(1)} %collective-permute-done.15), channel_id=1, source_target_pairs={{0,2},{2,4},{4,6},{6,7},{7,5},{5,3},{3,1},{1,0},{8,9},{10,8},{12,1... | collective-permute-start | bytes 393224 | tf_op jit(solution)/shard_map/ppermute | solution.py:300
  53.0 18.3 %collective-permute-start.13 = (f32[192,512]{1,0:T(8,128)S(1)}, f32[192,512]{1,0:T(8,128)S(1)}, u32[]{:S(2)}, u32[]{:S(2)}) collective-permute-start(f32[192,512]{1,0:T(8,128)S(1)} %get-tuple-element.60), channel_id=1, source_target_pairs={{0,2},{2,4},{4,6},{6,7},{7,5},{5,3},{3,1},{1,0},{8,9},{10,8},{12,1... | collective-permute-start | bytes 1179656 | tf_op jit(solution)/shard_map/ppermute | solution.py:282
  57.3 14.0 %collective-permute-start.14 = (f32[192,512]{1,0:T(8,128)S(1)}, f32[192,512]{1,0:T(8,128)S(1)}, u32[]{:S(2)}, u32[]{:S(2)}) collective-permute-start(f32[192,512]{1,0:T(8,128)S(1)} %get-tuple-element.61), channel_id=1, source_target_pairs={{0,1},{2,0},{4,2},{6,4},{7,6},{5,7},{3,5},{1,3},{8,10},{10,12},{12... | collective-permute-start | bytes 1179656 | tf_op jit(solution)/shard_map/ppermute | solution.py:282
  62.9 8.5 %collective-permute-start.18 = (f32[3,64,512]{2,1,0:T(8,128)S(1)}, f32[3,64,512]{2,1,0:T(8,128)S(1)}, u32[]{:S(2)}, u32[]{:S(2)}) collective-permute-start(f32[3,64,512]{2,1,0:T(8,128)S(1)} %pad_maximum_fusion.2), channel_id=1, source_target_pairs={{0,16},{8,24},{16,0},{24,8},{1,17},{9,25},{17,1},{25,9},{2,18},{10... | collective-permute-start | bytes 1179656 | tf_op jit(solution)/shard_map/ppermute | solution.py:254
  63.7 14.1 %collective-permute-start.25 = (f32[192,512]{1,0:T(8,128)S(1)}, f32[192,512]{1,0:T(8,128)S(1)}, u32[]{:S(2)}, u32[]{:S(2)}) collective-permute-start(f32[192,512]{1,0:T(8,128)S(1)} %get-tuple-element.95), channel_id=1, source_target_pairs={{0,1},{2,0},{4,2},{6,4},{7,6},{5,7},{3,5},{1,3},{8,10},{10,12},{12... | collective-permute-start | bytes 1179656 | tf_op jit(solution)/shard_map/ppermute | solution.py:282
  65.8 12.0 %collective-permute-start.23 = (f32[192,512]{1,0:T(8,128)S(1)}, f32[192,512]{1,0:T(8,128)S(1)}, u32[]{:S(2)}, u32[]{:S(2)}) collective-permute-start(f32[192,512]{1,0:T(8,128)S(1)} %get-tuple-element.96), channel_id=1, source_target_pairs={{0,2},{2,4},{4,6},{6,7},{7,5},{5,3},{3,1},{1,0},{8,9},{10,8},{12,1... | collective-permute-start | bytes 1179656 | tf_op jit(solution)/shard_map/ppermute | solution.py:326
  71.5 9.0 %collective-permute-start.19 = (f32[192,512]{1,0:T(8,128)S(1)}, f32[192,512]{1,0:T(8,128)S(1)}, u32[]{:S(2)}, u32[]{:S(2)}) collective-permute-start(f32[192,512]{1,0:T(8,128)S(1)} %get-tuple-element.66), channel_id=1, source_target_pairs={{0,2},{2,4},{4,6},{6,7},{7,5},{5,3},{3,1},{1,0},{8,9},{10,8},{12,1... | collective-permute-start | bytes 1179656 | tf_op jit(solution)/shard_map/ppermute | solution.py:282
  77.9 5.0 %collective-permute-start.26 = (f32[192,512]{1,0:T(8,128)S(1)}, f32[192,512]{1,0:T(8,128)S(1)}, u32[]{:S(2)}, u32[]{:S(2)}) collective-permute-start(f32[192,512]{1,0:T(8,128)S(1)} %fusion.1.refs_0_), channel_id=1, source_target_pairs={{0,8},{8,0},{16,24},{24,16},{1,9},{9,1},{17,25},{25,17},{2,10},{10... | collective-permute-start | bytes 1179656 | tf_op jit(solution)/shard_map/ppermute | solution.py:254
  80.6 11.0 %collective-permute-start.20 = (f32[192,512]{1,0:T(8,128)S(1)}, f32[192,512]{1,0:T(8,128)S(1)}, u32[]{:S(2)}, u32[]{:S(2)}) collective-permute-start(f32[192,512]{1,0:T(8,128)S(1)} %slice_add_fusion.5), channel_id=1, source_target_pairs={{0,2},{2,4},{4,6},{6,7},{7,5},{5,3},{3,1},{1,0},{8,9},{10,8},{12,1... | collective-permute-start | bytes 1179656 | tf_op jit(solution)/shard_map/ppermute | solution.py:350
  81.8 9.8 %collective-permute-start.27 = (f32[192,512]{1,0:T(8,128)S(1)}, f32[192,512]{1,0:T(8,128)S(1)}, u32[]{:S(2)}, u32[]{:S(2)}) collective-permute-start(f32[192,512]{1,0:T(8,128)S(1)} %get-tuple-element.84), channel_id=1, source_target_pairs={{0,1},{2,0},{4,2},{6,4},{7,6},{5,7},{3,5},{1,3},{8,10},{10,12},{12... | collective-permute-start | bytes 1179656 | tf_op jit(solution)/shard_map/ppermute | solution.py:282
  91.7 1.8 %collective-permute-start.28 = (f32[192,512]{1,0:T(8,128)S(1)}, f32[192,512]{1,0:T(8,128)S(1)}, u32[]{:S(2)}, u32[]{:S(2)}) collective-permute-start(f32[192,512]{1,0:T(8,128)S(1)} %fusion.refs_5_), channel_id=1, source_target_pairs={{0,8},{8,0},{16,24},{24,16},{1,9},{9,1},{17,25},{25,17},{2,10},{10... | collective-permute-start | bytes 1179656 | tf_op jit(solution)/shard_map/ppermute | solution.py:254
  97.2 14.0 %collective-permute-start.29 = (f32[512,256]{1,0:T(8,128)S(1)}, f32[512,256]{1,0:T(8,128)S(1)}, u32[]{:S(2)}, u32[]{:S(2)}) collective-permute-start(f32[512,256]{1,0:T(8,128)S(1)} %get-tuple-element.90), channel_id=1, source_target_pairs={{0,16},{8,24},{16,0},{24,8},{1,17},{9,25},{17,1},{25,9},{2,18},{10... | collective-permute-start | bytes 1572872 | tf_op jit(solution)/shard_map/ppermute | solution.py:254
  97.7 15.1 %collective-permute-start.31 = (f32[256,512]{1,0:T(8,128)S(1)}, f32[256,512]{1,0:T(8,128)S(1)}, u32[]{:S(2)}, u32[]{:S(2)}) collective-permute-start(f32[256,512]{1,0:T(8,128)S(1)} %get-tuple-element.92), channel_id=1, source_target_pairs={{0,1},{1,0},{2,3},{3,2},{4,5},{5,4},{6,7},{7,6},{8,9},{9,8},{10,11... | collective-permute-start | bytes 1572872 | tf_op jit(solution)/shard_map/ppermute | solution.py:257
  111.3 7.6 %collective-permute-start.30 = (f32[256,256]{1,0:T(8,128)S(1)}, f32[256,256]{1,0:T(8,128)S(1)}, u32[]{:S(2)}, u32[]{:S(2)}) collective-permute-start(f32[256,256]{1,0:T(8,128)S(1)} %slice.109), channel_id=1, source_target_pairs={{0,1},{1,0},{2,3},{3,2},{4,5},{5,4},{6,7},{7,6},{8,9},{9,8},{10,11... | collective-permute-start | bytes 786440 | tf_op jit(solution)/shard_map/ppermute | solution.py:257
  112.9 7.3 %collective-permute-start.32 = (f32[256,256]{1,0:T(8,128)S(1)}, f32[256,256]{1,0:T(8,128)S(1)}, u32[]{:S(2)}, u32[]{:S(2)}) collective-permute-start(f32[256,256]{1,0:T(8,128)S(1)} %slice.111), channel_id=1, source_target_pairs={{0,16},{8,24},{16,0},{24,8},{1,17},{9,25},{17,1},{25,9},{2,18},{10... | collective-permute-start | bytes 786440 | tf_op jit(solution)/shard_map/ppermute | solution.py:254
  120.3 8.3 %collective-permute-start.35 = (f32[64,512]{1,0:T(8,128)S(1)}, f32[64,512]{1,0:T(8,128)S(1)}, u32[]{:S(2)}, u32[]{:S(2)}) collective-permute-start(f32[64,512]{1,0:T(8,128)S(1)} %get-tuple-element.107), channel_id=1, source_target_pairs={{0,6},{1,7},{2,4},{3,5},{4,2},{5,3},{6,0},{7,1},{8,14},{9,15},{10,... | collective-permute-start | bytes 393224 | tf_op jit(solution)/shard_map/ppermute | solution.py:257
  123.0 6.6 %collective-permute-start.33 = (f32[64,512]{1,0:T(8,128)S(1)}, f32[64,512]{1,0:T(8,128)S(1)}, u32[]{:S(2)}, u32[]{:S(2)}) collective-permute-start(f32[64,512]{1,0:T(8,128)S(1)} %get-tuple-element.109), channel_id=1, source_target_pairs={{0,2},{1,3},{2,0},{3,1},{4,6},{5,7},{6,4},{7,5},{8,10},{9,11},{10,... | collective-permute-start | bytes 393224 | tf_op jit(solution)/shard_map/ppermute | solution.py:257
  123.3 10.0 %collective-permute-start.34 = (f32[64,512]{1,0:T(8,128)S(1)}, f32[64,512]{1,0:T(8,128)S(1)}, u32[]{:S(2)}, u32[]{:S(2)}) collective-permute-start(f32[64,512]{1,0:T(8,128)S(1)} %get-tuple-element.110), channel_id=1, source_target_pairs={{0,4},{1,5},{2,6},{3,7},{4,0},{5,1},{6,2},{7,3},{8,12},{9,13},{10,... | collective-permute-start | bytes 393224 | tf_op jit(solution)/shard_map/ppermute | solution.py:257
  133.9 1.3 collective-permute-start.36

commit v4 on v3

--- a/solution.py
+++ b/solution.py
@@ -12,6 +12,7 @@
 NEAR_COST, FAR_COST = 40, 0
 EARLY, PINS = 2, 2
 TIE1, TIE2 = 2, 3
+CUTS = 2
 ROWS_OVER_ROWS = ((0,), (0,))
 LANES_OVER_LANES = ((1,), (1,))
 
@@ -119,12 +120,13 @@
         rows = slice(k * height, (k + 1) * height)
         near_high_ref[rows, :], near_low_ref[rows, :] = split(ref[...])
     n, height, _ = near_ref.shape
-    near = []
-    for k in range(n):
-        at = table[order_at + k]
-        near.append(near_ref[at])
-        rows = slice(k * height, (k + 1) * height)
-        high_ref[rows, :], low_ref[rows, :] = split(far_ref[at])
+    near, far = [], []
+    for half in range(2):
+        places = [table[order_at + k] for k in range(half * n // 2, (half + 1) * n // 2)]
+        for rows in (slice(0, height // 2), slice(height // 2, height)):
+            near += [near_ref[at, rows, :] for at in places]
+            far += [far_ref[at, rows, :] for at in places]
+    high_ref[...], low_ref[...] = split(jnp.concatenate(far, axis=0))
     near = split(jnp.concatenate(near, axis=0))
     projected_ref[...] = dot3(near, (near_high_ref[...], near_low_ref[...]), LANES_OVER_LANES)
 
@@ -145,9 +147,10 @@
         at += width
 
 
-def sent_kernel(scale_inv, n_high, table, *refs):
+def sent_kernel(scale_inv, n_high, n_pieces, table, *refs):
     projected_ref, comp_high_ref, comp_low_ref, near_high_ref, near_low_ref, *refs = refs
-    *pieces, a_ref, b_ref, sq_high_ref, sq_low_ref, far_high_ref, far_low_ref = refs
+    pieces, refs = refs[:n_pieces], refs[n_pieces:]
+    a0_ref, a1_ref, b0_ref, b1_ref, sq_high_ref, sq_low_ref, far_high_ref, far_low_ref = refs
 
     @pl.when(pl.program_id(0) == 0)
     def _():
@@ -161,7 +164,7 @@
     )
     squared = split(projected * projected)
     sq_high_ref[...], sq_low_ref[...] = squared
-    width = near_high_ref.shape[1] // 2
+    width, half = near_high_ref.shape[1] // 2, a0_ref.shape[0]
 
     def columns(core, highs):
         return zip(
@@ -169,17 +172,21 @@
             columns_of(near_low_ref, far_low_ref, width, core, highs),
         )
 
-    store_moments(a_ref, squared, scale_inv, columns(0, range(n_high // 2, n_high)))
+    for k, ref in enumerate((a0_ref, a1_ref)):
+        rows = [x[k * half : (k + 1) * half] for x in squared]
+        store_moments(ref, rows, scale_inv, columns(0, range(n_high // 2, n_high)))
 
     @pl.when(pl.program_id(0) == 1)
     def _():
-        store_moments(b_ref, squared, scale_inv, columns(1, range(n_high)))
+        for k, ref in enumerate((b0_ref, b1_ref)):
+            rows = [x[k * half : (k + 1) * half] for x in squared]
+            store_moments(ref, rows, scale_inv, columns(1, range(n_high)))
 
 
 def kept_kernel(scale_inv, n_high, table, *refs):
-    sq_high_ref, sq_low_ref, near_high_ref, near_low_ref, far_high_ref, far_low_ref, a_ref, b_ref = refs
-    squared = sq_high_ref[...], sq_low_ref[...]
-    width = near_high_ref.shape[1] // 2
+    sq_high_ref, sq_low_ref, near_high_ref, near_low_ref, far_high_ref, far_low_ref, *refs = refs
+    a0_ref, a1_ref, b0_ref, b1_ref = refs
+    width, half = near_high_ref.shape[1] // 2, a0_ref.shape[0]
 
     def columns(core, highs):
         return zip(
@@ -187,18 +194,26 @@
             columns_of(near_low_ref, far_low_ref, width, core, highs),
         )
 
-    store_moments(a_ref, squared, scale_inv, columns(0, range(n_high // 2)))
+    for k, ref in enumerate((a0_ref, a1_ref)):
+        rows = [x[k * half : (k + 1) * half, :] for x in (sq_high_ref, sq_low_ref)]
+        store_moments(ref, rows, scale_inv, columns(0, range(n_high // 2)))
 
     @pl.when(pl.program_id(0) == 0)
     def _():
-        store_moments(b_ref, squared, scale_inv, columns(1, range(n_high)))
-
-
-def divide_kernel(core_at, table, own_ref, *refs):
-    *others, kept_ref, sent_ref = refs
-    total = own_ref[...]
-    for ref in others:
-        total = total + ref[...]
+        for k, ref in enumerate((b0_ref, b1_ref)):
+            rows = [x[k * half : (k + 1) * half, :] for x in (sq_high_ref, sq_low_ref)]
+            store_moments(ref, rows, scale_inv, columns(1, range(n_high)))
+
+
+def divide_kernel(core_at, table, *refs):
+    *parts, kept_ref, sent_ref = refs
+    totals = []
+    for half in (parts[: len(parts) // 2], parts[len(parts) // 2 :]):
+        total = half[0][...]
+        for ref in half[1:]:
+            total = total + ref[...]
+        totals.append(total)
+    total = jnp.concatenate(totals, axis=0)
     width = kept_ref.shape[1]
     for core in (0, 1):
 
@@ -347,59 +362,66 @@
             flops=6 * n_tall * n_deep * n_wide,
         )
         held = rounds(far_part, min(TIE2, reach), reach, held)
-        arrived = lax.ppermute(held[0], both, streams[0])
+        cuts = [slice(k * height // CUTS, (k + 1) * height // CUTS) for k in range(CUTS)]
+        arrived = [lax.ppermute(held[0][rows], both, streams[0]) for rows in cuts]
         arrived, near_side = lax.optimization_barrier((arrived, near_side))
-        far_sum = arrived + held[1]
-        far_rows = [far_sum, swap(far_sum, 1)]
+        far_rows = [x + held[1][rows] for x, rows in zip(arrived, cuts)]
+        far_rows += [swap(x, 1) for x in far_rows]
         scale_inv = float((samples.shape[0] * n_rows) ** -0.5)
-        tile, wide = n_tall // 2, n_wide // 2
+        half, wide, n_way = n_tall // 4, n_wide // 2, n_feat // 2
         whole = lambda a: pl.BlockSpec(a.shape, lambda i, t: (0, 0))
-        tiled = lambda a: pl.BlockSpec((tile, a.shape[1]), lambda i, t: (i, 0))
-        half_a, half_b = f32(n_tall, n_high // 2 * wide), f32(tile, n_high * wide)
+        tiled = lambda a: pl.BlockSpec((a.shape[0] // 2, a.shape[1]), lambda i, t: (i, 0))
+        half_a, half_b = f32(2 * half, n_high // 2 * wide), f32(half, n_high * wide)
         squares, rows_split = [bf16(n_tall, n_deep)] * 2, [bf16(n_deep, f_wide)] * 2
-        a_sent, b_sent, *squared_and_far = call(
-            functools.partial(sent_kernel, scale_inv, n_high),
-            [half_a, half_b] + squares + rows_split,
+        *sent, sq_high, sq_low, far_high, far_low = call(
+            functools.partial(sent_kernel, scale_inv, n_high, len(far_rows)),
+            [half_a] * 2 + [half_b] * 2 + squares + rows_split,
             table,
             *near_side,
             *far_rows,
             grid=(2,),
             in_specs=[tiled(x) for x in near_side[:3]] + [whole(x) for x in near_side[3:]] + [whole(x) for x in far_rows],
-            out_specs=[tiled(half_a), whole(half_b)] + [tiled(x) for x in squares] + [whole(x) for x in rows_split],
+            out_specs=[tiled(half_a)] * 2
+            + [whole(half_b)] * 2
+            + [tiled(x) for x in squares]
+            + [whole(x) for x in rows_split],
             flops=6 * n_tall * n_deep * (f_wide + n_wide // 2 * n_high),
         )
-        a_kept, b_kept = call(
+        kept = call(
             functools.partial(kept_kernel, scale_inv, n_high),
-            [half_a, half_b],
+            [half_a] * 2 + [half_b] * 2,
             table,
-            *squared_and_far[:2],
+            sq_high,
+            sq_low,
             *near_side[3:],
-            *squared_and_far[2:],
+            far_high,
+            far_low,
             grid=(2,),
             in_specs=[tiled(x) for x in squares] + [whole(x) for x in near_side[3:]] + [whole(x) for x in rows_split],
-            out_specs=[tiled(half_a), whole(half_b)],
+            out_specs=[tiled(half_a)] * 2 + [whole(half_b)] * 2,
             flops=6 * n_tall * n_deep * (n_wide // 2 * n_high),
         )
 
         def over_rows(x, bits):
             for bit in bits:
-                half = x.shape[1] // 2
-                x = x[:, :half] + swap(x[:, half:], bit)
+                cols = x.shape[1] // 2
+                x = x[:, :cols] + swap(x[:, cols:], bit)
             return x
 
-        a = over_rows(a_kept + swap(a_sent, high_bits[-1]), high_bits[-2::-1])
-        a = a[:tile] + swap_feat(a[tile:], 1)
-        b = over_rows(b_kept + swap_feat(b_sent, 1), high_bits[::-1])
-        joint = jnp.concatenate([a, b], axis=1)
-        step = joint.shape[0] // (n_feat // 2)
-        parts = [joint[k * step : (k + 1) * step] for k in range(n_feat // 2)]
-        parts = parts[:1] + [swap_feat(part, 2 * k) for k, part in enumerate(parts) if k]
-        width = joint.shape[1] // 2
-        kept, sent = call(
-            functools.partial(divide_kernel, core_at), [f32(step, width)] * 2, table, *parts
-        )
+        def over_chips(a_sent, b_sent, a_kept, b_kept):
+            a = over_rows(a_kept + swap(a_sent, high_bits[-1]), high_bits[-2::-1])
+            a = a[:half] + swap_feat(a[half:], 1)
+            b = over_rows(b_kept + swap_feat(b_sent, 1), high_bits[::-1])
+            joint = jnp.concatenate([a, b], axis=1)
+            step = half // n_way
+            parts = [joint[k * step : (k + 1) * step] for k in range(n_way)]
+            return parts[:1] + [swap_feat(part, 2 * k) for k, part in enumerate(parts) if k]
+
+        parts = over_chips(*sent[::2], *kept[::2]) + over_chips(*sent[1::2], *kept[1::2])
+        height = 2 * half // n_way
+        kept, sent = call(functools.partial(divide_kernel, core_at), [f32(height, wide)] * 2, table, *parts)
         return call(
-            functools.partial(assemble_kernel, core_at), [f32(width, 2 * step)], table, kept, swap(sent, 1)
+            functools.partial(assemble_kernel, core_at), [f32(wide, 2 * height)], table, kept, swap(sent, 1)
         )[0]
 
     placed = (P("rows", "feat"), P("feat", "rows"), P("rows", "feat"))

time: 137 us -> 133 us (0.971)
  waiting for transfers between devices: 69.8 us -> 54 us
  starting transfers between devices: 35.1 us -> 47.5 us
    ppermute x5 -> x10, waiting for transfers between devices: 14 us -> 5.38 us  [swap_feat(): return lax.ppermute(a, 'feat', [(i, i ^ bit) for i in range(n_feat)])]
    ppermute x5 -> x10, starting transfers between devices: 7.34 us -> 14.2 us  [swap_feat(): return lax.ppermute(a, 'feat', [(i, i ^ bit) for i in range(n_feat)])]
    ppermute x11 -> x14, waiting for transfers between devices: 15.7 us -> 10.2 us  [swap(): return lax.ppermute(a, 'rows', [(i, i ^ bit) for i in range(n_rows)])]
    ppermute x1 -> x2, waiting for transfers between devices: 7.04 us -> 3.06 us  [on_device(): arrived = [lax.ppermute(held[0][rows], both, streams[0]) for rows in cuts]]
    ppermute x11 -> x14, starting transfers between devices: 5.81 us -> 8.47 us  [swap(): return lax.ppermute(a, 'rows', [(i, i ^ bit) for i in range(n_rows)])]
    ppermute x1, waiting for transfers between devices: 0.01 us -> 1.97 us  [on_device(): near = lax.ppermute(near[0], both, streams[0]) + near[1]]
    ppermute x1 -> x2, starting transfers between devices: 1.27 us -> 2.85 us  [on_device(): arrived = [lax.ppermute(held[0][rows], both, streams[0]) for rows in cuts]]
  transfers between devices with their start and end apart: 37 -> 46, of which waited for: 18 -> 22; matrix products, arithmetic and copies ran while one was open for 2% -> 3% of each run, Pallas kernels for 13% -> 14%
where the time goes in v4:
time: 133 us; the launch traced here: 132 us
  waiting for transfers between devices  54 us (41%)
  starting transfers between devices  47.5 us (36%)
  Pallas kernels  23.2 us (17%)
  local copies, waits for them, and re-layouts  5.94 us (4%)
  other arithmetic  1.46 us (1%)
    pallas_call x9, Pallas kernels, call(): pl.pallas_call(kernel, out_shape=outs, grid_spec=pltpu.PrefetchScalarGrid...  23.2 us
    ppermute x12, waiting for transfers between devices, rounds(): held[s] = lax.ppermute(held[s], both, streams[s]) + piece  20.1 us
    ppermute x12, starting transfers between devices, rounds(): held[s] = lax.ppermute(held[s], both, streams[s]) + piece  15.1 us
    ppermute x10, starting transfers between devices, swap_feat(): return lax.ppermute(a, 'feat', [(i, i ^ bit) for i in range(n_feat)])  14.2 us
    ppermute x4, waiting for transfers between devices, pass_components(): line[step] = lax.ppermute(line[step - 1], both, streams[0])  10.6 us
    ppermute x14, waiting for transfers between devices, swap(): return lax.ppermute(a, 'rows', [(i, i ^ bit) for i in range(n_rows)])  10.2 us
    ppermute x14, starting transfers between devices, swap(): return lax.ppermute(a, 'rows', [(i, i ^ bit) for i in range(n_rows)])  8.47 us
    ppermute x10, waiting for transfers between devices, swap_feat(): return lax.ppermute(a, 'feat', [(i, i ^ bit) for i in range(n_feat)])  5.38 us
  transfers between devices with their start and end apart: 46, of which 22 were waited for; matrix products, arithmetic and copies ran while one was open for 3% of the time, Pallas kernels for 14%

profile of v4, /device:TPU:0, one launch (start us, length us, event | category | flops | bytes accessed | tf_op | source)
XLA Modules:
  0.0 132.5 jit_solution(656043004090753291)
XLA Ops:
  0.5 2.5 %collective-permute-start = (f32[1024,256]{1,0:T(8,128)}, f32[1024,256]{1,0:T(8,128)S(1)}, u32[]{:S(2)}, u32[]{:S(2)}) collective-permute-start(f32[1024,256]{1,0:T(8,128)} %refs_2_.3), channel_id=1, source_target_pairs={{0,16},{8,24},{16,0},{24,8},{1,17},{9,25},{17,1},{25,9},{2,18},{10... | collective-permute-start | bytes 3145736 | tf_op jit(solution)/shard_map/ppermute | solution.py:269
  3.0 1.0 copy.7
  5.4 1.5 %collective-permute-start.4 = (f32[64,512]{1,0:T(8,128)S(1)}, f32[64,512]{1,0:T(8,128)S(1)}, u32[]{:S(2)}, u32[]{:S(2)}) collective-permute-start(f32[64,512]{1,0:T(8,128)S(1)} %pad_maximum_fusion.3), channel_id=1, source_target_pairs={{0,1},{2,0},{4,2},{6,4},{7,6},{5,7},{3,5},{1,3},{8,10},{10,12},{12... | collective-permute-start | bytes 393224 | tf_op jit(solution)/shard_map/ppermute | solution.py:317
  7.4 2.8 %copy-done = f32[1536,1024]{1,0:T(8,128)S(1)} copy-done((f32[1536,1024]{1,0:T(8,128)S(1)}, f32[1536,1024]{1,0:T(8,128)}, u32[]{:S(2)}) %copy-start) | copy-done | bytes 6291480
  10.2 1.2 copy-done.1
  11.5 2.2 %shard_map.46 = f32[384,512]{1,0:T(8,128)S(1)} custom-call(s32[17]{0:T(128)S(1)} %fusion.7.table, f32[1536,1024]{1,0:T(8,128)S(1)} %copy-done, f32[1536,1024]{1,0:T(8,128)S(1)} %copy-done, f32[1024,256]{1,0:T(8,128)S(1)} %copy-done.1, f32[1024,256]{1,0:T(8,128)S(1)} %collective-permute-done.1.refs_3_), custom_call_target="tpu_custom_call" | custom-call | flops 16106127360 | bytes 14680064 | tf_op jit(solution)/shard_map/pallas_call | solution.py:51
  13.8 1.6 %collective-permute-start.7 = (f32[64,512]{1,0:T(8,128)S(1)}, f32[64,512]{1,0:T(8,128)S(1)}, u32[]{:S(2)}, u32[]{:S(2)}) collective-permute-start(f32[64,512]{1,0:T(8,128)S(1)} %collective-permute-done.3), channel_id=1, source_target_pairs={{0,2},{2,4},{4,6},{6,7},{7,5},{5,3},{3,1},{1,0},{8,9},{10,8},{12,1... | collective-permute-start | bytes 393224 | tf_op jit(solution)/shard_map/ppermute | solution.py:315
  15.9 1.5 %collective-permute-start.6 = (f32[192,512]{1,0:T(8,128)S(1)}, f32[192,512]{1,0:T(8,128)S(1)}, u32[]{:S(2)}, u32[]{:S(2)}) collective-permute-start(f32[192,512]{1,0:T(8,128)S(1)} %get-tuple-element.117), channel_id=1, source_target_pairs={{0,1},{2,0},{4,2},{6,4},{7,6},{5,7},{3,5},{1,3},{8,10},{10,12},{12... | collective-permute-start | bytes 1179656 | tf_op jit(solution)/shard_map/ppermute | solution.py:297
  17.9 5.1 %shard_map.47 = f32[1152,512]{1,0:T(8,128)S(1)} custom-call(s32[17]{0:T(128)S(1)} %fusion.7.table, f32[1536,1024]{1,0:T(8,128)S(1)} %copy-done, f32[1536,1024]{1,0:T(8,128)S(1)} %copy-done, f32[1024,256]{1,0:T(8,128)S(1)} %copy-done.1, f32[1024,256]{1,0:T(8,128)S(1)} %collective-permute-done.1.refs_3_), custom_call_target="tpu_custom_call" | custom-call | flops 48318382080 | bytes 14680064 | tf_op jit(solution)/shard_map/pallas_call | solution.py:51
  23.0 5.7 %collective-permute-done.6 = f32[192,512]{1,0:T(8,128)S(1)} collective-permute-done((f32[192,512]{1,0:T(8,128)S(1)}, f32[192,512]{1,0:T(8,128)S(1)}, u32[]{:S(2)}, u32[]{:S(2)}) %collective-permute-start.6) | collective-permute-done | bytes 393248 | tf_op jit(solution)/shard_map/ppermute | solution.py:297
  29.1 1.6 %collective-permute-start.22 = (f32[192,512]{1,0:T(8,128)S(1)}, f32[192,512]{1,0:T(8,128)S(1)}, u32[]{:S(2)}, u32[]{:S(2)}) collective-permute-start(f32[192,512]{1,0:T(8,128)S(1)} %get-tuple-element.72), channel_id=1, source_target_pairs={{0,2},{2,4},{4,6},{6,7},{7,5},{5,3},{3,1},{1,0},{8,9},{10,8},{12,1... | collective-permute-start | bytes 1179656 | tf_op jit(solution)/shard_map/ppermute | solution.py:297
  31.6 2.3 %shard_map.48 = f32[384,512]{1,0:T(8,128)S(1)} custom-call(s32[17]{0:T(128)S(1)} %fusion.7.table, f32[1536,1024]{1,0:T(8,128)S(1)} %copy-done, f32[1536,1024]{1,0:T(8,128)S(1)} %copy-done, f32[1024,256]{1,0:T(8,128)S(1)} %collective-permute-done.refs_2_, f32[1024,256]{1,0:T(8,128)S(1)} %collective-permute-done.9.refs_3_), custom_call_target="tpu_custom_call" | custom-call | bytes 14680064 | tf_op jit(solution)/shard_map/pallas_call | solution.py:51
  33.9 1.4 %collective-permute-start.11 = (f32[192,512]{1,0:T(8,128)S(1)}, f32[192,512]{1,0:T(8,128)S(1)}, u32[]{:S(2)}, u32[]{:S(2)}) collective-permute-start(f32[192,512]{1,0:T(8,128)S(1)} %get-tuple-element.115), channel_id=1, source_target_pairs={{0,1},{2,0},{4,2},{6,4},{7,6},{5,7},{3,5},{1,3},{8,10},{10,12},{12... | collective-permute-start | bytes 1179656 | tf_op jit(solution)/shard_map/ppermute | solution.py:297
  36.6 1.4 %collective-permute-start.25 = (f32[192,512]{1,0:T(8,128)S(1)}, f32[192,512]{1,0:T(8,128)S(1)}, u32[]{:S(2)}, u32[]{:S(2)}) collective-permute-start(f32[192,512]{1,0:T(8,128)S(1)} %get-tuple-element.73), channel_id=1, source_target_pairs={{0,1},{2,0},{4,2},{6,4},{7,6},{5,7},{3,5},{1,3},{8,10},{10,12},{12... | collective-permute-start | bytes 1179656 | tf_op jit(solution)/shard_map/ppermute | solution.py:297
  38.7 5.1 %shard_map.49 = f32[1152,512]{1,0:T(8,128)S(1)} custom-call(s32[17]{0:T(128)S(1)} %fusion.7.table, f32[1536,1024]{1,0:T(8,128)S(1)} %copy-done, f32[1536,1024]{1,0:T(8,128)S(1)} %copy-done, f32[1024,256]{1,0:T(8,128)S(1)} %collective-permute-done.refs_2_, f32[1024,256]{1,0:T(8,128)S(1)} %collective-permute-done.9.refs_3_), custom_call_target="tpu_custom_call" | custom-call | bytes 14680064 | tf_op jit(solution)/shard_map/pallas_call | solution.py:51
  43.8 6.4 %collective-permute-done.15 = f32[64,512]{1,0:T(8,128)S(1)} collective-permute-done((f32[64,512]{1,0:T(8,128)S(1)}, f32[64,512]{1,0:T(8,128)S(1)}, u32[]{:S(2)}, u32[]{:S(2)}) %collective-permute-start.15) | collective-permute-done | bytes 131104 | tf_op jit(solution)/shard_map/ppermute | solution.py:315
  50.9 1.4 %collective-permute-start.17 = (f32[64,512]{1,0:T(8,128)S(1)}, f32[64,512]{1,0:T(8,128)S(1)}, u32[]{:S(2)}, u32[]{:S(2)}) collective-permute-start(f32[64,512]{1,0:T(8,128)S(1)} %collective-permute-done.8), channel_id=1, source_target_pairs={{0,1},{2,0},{4,2},{6,4},{7,6},{5,7},{3,5},{1,3},{8,10},{10,12},{12... | collective-permute-start | bytes 393224 | tf_op jit(solution)/shard_map/ppermute | solution.py:317
  53.0 1.6 %collective-permute-start.13 = (f32[192,512]{1,0:T(8,128)S(1)}, f32[192,512]{1,0:T(8,128)S(1)}, u32[]{:S(2)}, u32[]{:S(2)}) collective-permute-start(f32[192,512]{1,0:T(8,128)S(1)} %get-tuple-element.65), channel_id=1, source_target_pairs={{0,2},{2,4},{4,6},{6,7},{7,5},{5,3},{3,1},{1,0},{8,9},{10,8},{12,1... | collective-permute-start | bytes 1179656 | tf_op jit(solution)/shard_map/ppermute | solution.py:297
  54.7 2.6 %collective-permute-done.17 = f32[64,512]{1,0:T(8,128)S(1)} collective-permute-done((f32[64,512]{1,0:T(8,128)S(1)}, f32[64,512]{1,0:T(8,128)S(1)}, u32[]{:S(2)}, u32[]{:S(2)}) %collective-permute-start.17) | collective-permute-done | bytes 131104 | tf_op jit(solution)/shard_map/ppermute | solution.py:317
  57.3 1.4 %collective-permute-start.14 = (f32[192,512]{1,0:T(8,128)S(1)}, f32[192,512]{1,0:T(8,128)S(1)}, u32[]{:S(2)}, u32[]{:S(2)}) collective-permute-start(f32[192,512]{1,0:T(8,128)S(1)} %get-tuple-element.66), channel_id=1, source_target_pairs={{0,1},{2,0},{4,2},{6,4},{7,6},{5,7},{3,5},{1,3},{8,10},{10,12},{12... | collective-permute-start | bytes 1179656 | tf_op jit(solution)/shard_map/ppermute | solution.py:297
  58.7 4.2 %collective-permute-done.16 = f32[64,512]{1,0:T(8,128)S(1)} collective-permute-done((f32[64,512]{1,0:T(8,128)S(1)}, f32[64,512]{1,0:T(8,128)S(1)}, u32[]{:S(2)}, u32[]{:S(2)}) %collective-permute-start.16) | collective-permute-done | bytes 131104 | tf_op jit(solution)/shard_map/ppermute | solution.py:315
  63.7 2.1 %collective-permute-start.26 = (f32[192,512]{1,0:T(8,128)S(1)}, f32[192,512]{1,0:T(8,128)S(1)}, u32[]{:S(2)}, u32[]{:S(2)}) collective-permute-start(f32[192,512]{1,0:T(8,128)S(1)} %get-tuple-element.107), channel_id=1, source_target_pairs={{0,1},{2,0},{4,2},{6,4},{7,6},{5,7},{3,5},{1,3},{8,10},{10,12},{12... | collective-permute-start | bytes 1179656 | tf_op jit(solution)/shard_map/ppermute | solution.py:297
  65.8 5.5 %collective-permute-done.13 = f32[192,512]{1,0:T(8,128)S(1)} collective-permute-done((f32[192,512]{1,0:T(8,128)S(1)}, f32[192,512]{1,0:T(8,128)S(1)}, u32[]{:S(2)}, u32[]{:S(2)}) %collective-permute-start.13) | collective-permute-done | bytes 393248 | tf_op jit(solution)/shard_map/ppermute | solution.py:297
  71.7 2.0 %collective-permute-start.28 = (f32[192,512]{1,0:T(8,128)S(1)}, f32[192,512]{1,0:T(8,128)S(1)}, u32[]{:S(2)}, u32[]{:S(2)}) collective-permute-start(f32[192,512]{1,0:T(8,128)S(1)} %get-tuple-element.89), channel_id=1, source_target_pairs={{0,1},{2,0},{4,2},{6,4},{7,6},{5,7},{3,5},{1,3},{8,10},{10,12},{12... | collective-permute-start | bytes 1179656 | tf_op jit(solution)/shard_map/ppermute | solution.py:297
  73.7 4.1 %collective-permute-done.26 = f32[192,512]{1,0:T(8,128)S(1)} collective-permute-done((f32[192,512]{1,0:T(8,128)S(1)}, f32[192,512]{1,0:T(8,128)S(1)}, u32[]{:S(2)}, u32[]{:S(2)}) %collective-permute-start.26) | collective-permute-done | bytes 393248 | tf_op jit(solution)/shard_map/ppermute | solution.py:297
  77.8 2.0 %collective-permute-done.24 = f32[192,512]{1,0:T(8,128)S(1)} collective-permute-done((f32[192,512]{1,0:T(8,128)S(1)}, f32[192,512]{1,0:T(8,128)S(1)}, u32[]{:S(2)}, u32[]{:S(2)}) %collective-permute-start.24) | collective-permute-done | bytes 393248 | tf_op jit(solution)/shard_map/ppermute | solution.py:341
  79.9 4.8 %collective-permute-done.19 = f32[192,512]{1,0:T(8,128)S(1)} collective-permute-done((f32[192,512]{1,0:T(8,128)S(1)}, f32[192,512]{1,0:T(8,128)S(1)}, u32[]{:S(2)}, u32[]{:S(2)}) %collective-permute-start.19) | collective-permute-done | bytes 393248 | tf_op jit(solution)/shard_map/ppermute | solution.py:297
  84.9 1.3 collective-permute-start.21
  86.2 1.6 %collective-permute-start.20 = (f32[96,512]{1,0:T(8,128)S(1)}, f32[96,512]{1,0:T(8,128)S(1)}, u32[]{:S(2)}, u32[]{:S(2)}) collective-permute-start(f32[96,512]{1,0:T(8,128)S(1)} %get-tuple-element.122), channel_id=1, source_target_pairs={{0,2},{2,4},{4,6},{6,7},{7,5},{5,3},{3,1},{1,0},{8,9},{10,8},{12,1... | collective-permute-start | bytes 589832 | tf_op jit(solution)/shard_map/ppermute | solution.py:366
  88.0 1.6 %shard_map.50 = (f32[512,384]{1,0:T(8,128)S(1)}, bf16[512,512]{1,0:T(8,128)(2,1)S(1)}, bf16[512,512]{1,0:T(8,128)(2,1)S(1)}, bf16[384,512]{1,0:T(8,128)(2,1)S(1)}, bf16[384,512]{1,0:T(8,128)(2,1)S(1)}) custom-call(s32[17]{0:T(128)S(1)} %fusion.7.table, f32[192,512]{1,0:T(8,128)S(1)} %fusion.refs_0_, f32[192,512]{1,0:T(8,128)S(1)} %collective-permute-done.27.refs_1_, ...), custom_call_target="tpu_custom_call" | custom-call | flops 603979776 | bytes 2883584 | tf_op jit(solution)/shard_map/pallas_call | solution.py:51
  89.7 1.0 collective-permute-done.21
  90.6 2.1 %collective-permute-done.20 = f32[96,512]{1,0:T(8,128)S(1)} collective-permute-done((f32[96,512]{1,0:T(8,128)S(1)}, f32[96,512]{1,0:T(8,128)S(1)}, u32[]{:S(2)}, u32[]{:S(2)}) %collective-permute-start.20) | collective-permute-done | bytes 196640 | tf_op jit(solution)/shard_map/ppermute | solution.py:366
  94.6 3.1 %shard_map.51 = (f32[256,256]{1,0:T(8,128)S(1)}, f32[256,256]{1,0:T(8,128)S(1)}, f32[128,512]{1,0:T(8,128)S(1)}, f32[128,512]{1,0:T(8,128)S(1)}, bf16[512,384]{1...) custom-call(s32[17]{0:T(128)S(1)} %fusion.7.table, ...), custom_call_target="tpu_custom_call" | custom-call | flops 1207959552 | bytes 5242880 | tf_op jit(solution)/shard_map/pallas_call | solution.py:51
  98.2 1.6 %collective-permute-start.33 = (f32[128,512]{1,0:T(8,128)S(1)}, f32[128,512]{1,0:T(8,128)S(1)}, u32[]{:S(2)}, u32[]{:S(2)}) collective-permute-start(f32[128,512]{1,0:T(8,128)S(1)} %get-tuple-element.98), channel_id=1, source_target_pairs={{0,1},{1,0},{2,3},{3,2},{4,5},{5,4},{6,7},{7,6},{8,9},{9,8},{10,11... | collective-permute-start | bytes 786440 | tf_op jit(solution)/shard_map/ppermute | solution.py:272
  99.8 1.5 %collective-permute-start.38 = (f32[256,256]{1,0:T(8,128)S(1)}, f32[256,256]{1,0:T(8,128)S(1)}, u32[]{:S(2)}, u32[]{:S(2)}) collective-permute-start(f32[256,256]{1,0:T(8,128)S(1)} %get-tuple-element.100), channel_id=1, source_target_pairs={{0,16},{8,24},{16,0},{24,8},{1,17},{9,25},{17,1},{25,9},{2,18},{10... | collective-permute-start | bytes 786440 | tf_op jit(solution)/shard_map/ppermute | solution.py:269
  101.8 1.9 %shard_map.52 = (f32[256,256]{1,0:T(8,128)S(1)}, f32[256,256]{1,0:T(8,128)S(1)}, f32[128,512]{1,0:T(8,128)S(1)}, f32[128,512]{1,0:T(8,128)S(1)}) custom-call(s32[17]{0:T(128)S(1)} %fusion.7.table, bf16[512,384]{1,0:T(8,128)(2,1)S(1)} %get-tuple-element.91.refs_0_, bf16[512,384]{1,0:T(8,128)(2,1)S(1)} %get-tuple-element.92.refs_1_, ...), custom_call_target="tpu_custom_call" | custom-call | flops 603979776 | bytes 4718592 | tf_op jit(solution)/shard_map/pallas_call | solution.py:51
  103.7 3.2 %collective-permute-done.31 = f32[256,256]{1,0:T(8,128)S(1)} collective-permute-done((f32[256,256]{1,0:T(8,128)S(1)}, f32[256,256]{1,0:T(8,128)S(1)}, u32[]{:S(2)}, u32[]{:S(2)}) %collective-permute-start.31) | collective-permute-done | bytes 262176 | tf_op jit(solution)/shard_map/ppermute | solution.py:269
  106.9 1.6 %collective-permute-start.32 = (f32[128,256]{1,0:T(8,128)S(1)}, f32[128,256]{1,0:T(8,128)S(1)}, u32[]{:S(2)}, u32[]{:S(2)}) collective-permute-start(f32[128,256]{1,0:T(8,128)S(1)} %slice.161), channel_id=1, source_target_pairs={{0,1},{1,0},{2,3},{3,2},{4,5},{5,4},{6,7},{7,6},{8,9},{9,8},{10,11... | collective-permute-start | bytes 393224 | tf_op jit(solution)/shard_map/ppermute | solution.py:272
  109.2 3.3 %collective-permute-done.38 = f32[256,256]{1,0:T(8,128)S(1)} collective-permute-done((f32[256,256]{1,0:T(8,128)S(1)}, f32[256,256]{1,0:T(8,128)S(1)}, u32[]{:S(2)}, u32[]{:S(2)}) %collective-permute-start.38) | collective-permute-done | bytes 262176 | tf_op jit(solution)/shard_map/ppermute | solution.py:269
  112.5 1.6 %collective-permute-start.39 = (f32[128,256]{1,0:T(8,128)S(1)}, f32[128,256]{1,0:T(8,128)S(1)}, u32[]{:S(2)}, u32[]{:S(2)}) collective-permute-start(f32[128,256]{1,0:T(8,128)S(1)} %slice.171), channel_id=1, source_target_pairs={{0,1},{1,0},{2,3},{3,2},{4,5},{5,4},{6,7},{7,6},{8,9},{9,8},{10,11... | collective-permute-start | bytes 393224 | tf_op jit(solution)/shard_map/ppermute | solution.py:272
  115.8 3.2 %collective-permute-start.37 = (f32[32,512]{1,0:T(8,128)S(1)}, f32[32,512]{1,0:T(8,128)S(1)}, u32[]{:S(2)}, u32[]{:S(2)}) collective-permute-start(f32[32,512]{1,0:T(8,128)S(1)} %get-tuple-element.127), channel_id=1, source_target_pairs={{0,6},{1,7},{2,4},{3,5},{4,2},{5,3},{6,0},{7,1},{8,14},{9,15},{10,... | collective-permute-start | bytes 196616 | tf_op jit(solution)/shard_map/ppermute | solution.py:272
  118.9 1.3 collective-permute-start.36
  120.3 3.2 %collective-permute-start.44 = (f32[32,512]{1,0:T(8,128)S(1)}, f32[32,512]{1,0:T(8,128)S(1)}, u32[]{:S(2)}, u32[]{:S(2)}) collective-permute-start(f32[32,512]{1,0:T(8,128)S(1)} %get-tuple-element.123), channel_id=1, source_target_pairs={{0,6},{1,7},{2,4},{3,5},{4,2},{5,3},{6,0},{7,1},{8,14},{9,15},{10,... | collective-permute-start | bytes 196616 | tf_op jit(solution)/shard_map/ppermute | solution.py:272
  123.5 1.3 collective-permute-start.43
  125.0 2.5 %collective-permute-done.36.refs_2_ = f32[32,512]{1,0:T(8,128)S(1)} collective-permute-done((f32[32,512]{1,0:T(8,128)S(1)}, f32[32,512]{1,0:T(8,128)S(1)}, u32[]{:S(2)}, u32[]{:S(2)}) %collective-permute-start.36) | collective-permute-done | bytes 65568 | tf_op jit(solution)/shard_map/ppermute | solution.py:272
  127.5 1.1 collective-permute-done.42.refs_5_
  129.9 1.2 collective-permute-done.45.other_ref
  131.2 1.3 shard_map.54
  (94 shorter events, 16.4 us)
Async XLA Ops:
  0.0 7.4 %collective-permute-start.1 = (f32[1024,256]{1,0:T(8,128)}, f32[1024,256]{1,0:T(8,128)S(1)}, u32[]{:S(2)}, u32[]{:S(2)}) collective-permute-start(f32[1024,256]{1,0:T(8,128)} %refs_2_.3), channel_id=1, source_target_pairs={{0,8},{8,0},{16,24},{24,16},{1,9},{9,1},{17,25},{25,17},{2,10},{10... | collective-permute-start | bytes 3145736 | tf_op jit(solution)/shard_map/ppermute | solution.py:269
  0.5 28.4 %collective-permute-start = (f32[1024,256]{1,0:T(8,128)}, f32[1024,256]{1,0:T(8,128)S(1)}, u32[]{:S(2)}, u32[]{:S(2)}) collective-permute-start(f32[1024,256]{1,0:T(8,128)} %refs_2_.3), channel_id=1, source_target_pairs={{0,16},{8,24},{16,0},{24,8},{1,17},{9,25},{17,1},{25,9},{2,18},{10... | collective-permute-start | bytes 3145736 | tf_op jit(solution)/shard_map/ppermute | solution.py:269
  4.0 1.3 collective-permute-start.2
  5.4 8.4 %collective-permute-start.4 = (f32[64,512]{1,0:T(8,128)S(1)}, f32[64,512]{1,0:T(8,128)S(1)}, u32[]{:S(2)}, u32[]{:S(2)}) collective-permute-start(f32[64,512]{1,0:T(8,128)S(1)} %pad_maximum_fusion.3), channel_id=1, source_target_pairs={{0,1},{2,0},{4,2},{6,4},{7,6},{5,7},{3,5},{1,3},{8,10},{10,12},{12... | collective-permute-start | bytes 393224 | tf_op jit(solution)/shard_map/ppermute | solution.py:317
  6.9 6.8 %collective-permute-start.3 = (f32[64,512]{1,0:T(8,128)S(1)}, f32[64,512]{1,0:T(8,128)S(1)}, u32[]{:S(2)}, u32[]{:S(2)}) collective-permute-start(f32[64,512]{1,0:T(8,128)S(1)} %pad_maximum_fusion.3), channel_id=1, source_target_pairs={{0,2},{2,4},{4,6},{6,7},{7,5},{5,3},{3,1},{1,0},{8,9},{10,8},{12,1... | collective-permute-start | bytes 393224 | tf_op jit(solution)/shard_map/ppermute | solution.py:315
  7.4 2.8 %copy-start = (f32[1536,1024]{1,0:T(8,128)S(1)}, f32[1536,1024]{1,0:T(8,128)}, u32[]{:S(2)}) copy-start(f32[1536,1024]{1,0:T(8,128)} %refs_1_.7) | copy-start | bytes 18874372
  10.2 1.2 copy-start.1
  13.8 15.1 %collective-permute-start.7 = (f32[64,512]{1,0:T(8,128)S(1)}, f32[64,512]{1,0:T(8,128)S(1)}, u32[]{:S(2)}, u32[]{:S(2)}) collective-permute-start(f32[64,512]{1,0:T(8,128)S(1)} %collective-permute-done.3), channel_id=1, source_target_pairs={{0,2},{2,4},{4,6},{6,7},{7,5},{5,3},{3,1},{1,0},{8,9},{10,8},{12,1... | collective-permute-start | bytes 393224 | tf_op jit(solution)/shard_map/ppermute | solution.py:315
  15.4 13.5 %collective-permute-start.8 = (f32[64,512]{1,0:T(8,128)S(1)}, f32[64,512]{1,0:T(8,128)S(1)}, u32[]{:S(2)}, u32[]{:S(2)}) collective-permute-start(f32[64,512]{1,0:T(8,128)S(1)} %collective-permute-done.4), channel_id=1, source_target_pairs={{0,1},{2,0},{4,2},{6,4},{7,6},{5,7},{3,5},{1,3},{8,10},{10,12},{12... | collective-permute-start | bytes 393224 | tf_op jit(solution)/shard_map/ppermute | solution.py:317
  15.9 12.9 %collective-permute-start.6 = (f32[192,512]{1,0:T(8,128)S(1)}, f32[192,512]{1,0:T(8,128)S(1)}, u32[]{:S(2)}, u32[]{:S(2)}) collective-permute-start(f32[192,512]{1,0:T(8,128)S(1)} %get-tuple-element.117), channel_id=1, source_target_pairs={{0,1},{2,0},{4,2},{6,4},{7,6},{5,7},{3,5},{1,3},{8,10},{10,12},{12... | collective-permute-start | bytes 1179656 | tf_op jit(solution)/shard_map/ppermute | solution.py:297
  17.4 11.4 %collective-permute-start.5 = (f32[192,512]{1,0:T(8,128)S(1)}, f32[192,512]{1,0:T(8,128)S(1)}, u32[]{:S(2)}, u32[]{:S(2)}) collective-permute-start(f32[192,512]{1,0:T(8,128)S(1)} %get-tuple-element.118), channel_id=1, source_target_pairs={{0,2},{2,4},{4,6},{6,7},{7,5},{5,3},{3,1},{1,0},{8,9},{10,8},{12,1... | collective-permute-start | bytes 1179656 | tf_op jit(solution)/shard_map/ppermute | solution.py:297
  28.9 2.7 %collective-permute-start.9 = (f32[1024,256]{1,0:T(8,128)S(1)}, f32[1024,256]{1,0:T(8,128)S(1)}, u32[]{:S(2)}, u32[]{:S(2)}) collective-permute-start(f32[1024,256]{1,0:T(8,128)S(1)} %collective-permute-done.refs_2_), channel_id=1, source_target_pairs={{0,8},{8,0},{16,24},{24,16},{1,9},{9,1},{17,25},{25,17},{2,10},{10... | collective-permute-start | bytes 3145736 | tf_op jit(solution)/shard_map/ppermute | solution.py:269
  29.1 9.0 %collective-permute-start.22 = (f32[192,512]{1,0:T(8,128)S(1)}, f32[192,512]{1,0:T(8,128)S(1)}, u32[]{:S(2)}, u32[]{:S(2)}) collective-permute-start(f32[192,512]{1,0:T(8,128)S(1)} %get-tuple-element.72), channel_id=1, source_target_pairs={{0,2},{2,4},{4,6},{6,7},{7,5},{5,3},{3,1},{1,0},{8,9},{10,8},{12,1... | collective-permute-start | bytes 1179656 | tf_op jit(solution)/shard_map/ppermute | solution.py:297
  33.9 16.9 %collective-permute-start.11 = (f32[192,512]{1,0:T(8,128)S(1)}, f32[192,512]{1,0:T(8,128)S(1)}, u32[]{:S(2)}, u32[]{:S(2)}) collective-permute-start(f32[192,512]{1,0:T(8,128)S(1)} %get-tuple-element.115), channel_id=1, source_target_pairs={{0,1},{2,0},{4,2},{6,4},{7,6},{5,7},{3,5},{1,3},{8,10},{10,12},{12... | collective-permute-start | bytes 1179656 | tf_op jit(solution)/shard_map/ppermute | solution.py:297
  35.4 16.9 %collective-permute-start.10 = (f32[192,512]{1,0:T(8,128)S(1)}, f32[192,512]{1,0:T(8,128)S(1)}, u32[]{:S(2)}, u32[]{:S(2)}) collective-permute-start(f32[192,512]{1,0:T(8,128)S(1)} %get-tuple-element.116), channel_id=1, source_target_pairs={{0,2},{2,4},{4,6},{6,7},{7,5},{5,3},{3,1},{1,0},{8,9},{10,8},{12,1... | collective-permute-start | bytes 1179656 | tf_op jit(solution)/shard_map/ppermute | solution.py:297
  36.0 17.0 %collective-permute-start.12 = (f32[5,64,512]{2,1,0:T(8,128)S(1)}, f32[5,64,512]{2,1,0:T(8,128)S(1)}, u32[]{:S(2)}, u32[]{:S(2)}) collective-permute-start(f32[5,64,512]{2,1,0:T(8,128)S(1)} %bitcast_dynamic-update-slice_fusion), channel_id=1, source_target_pairs={{0,16},{8,24},{16,0},{24,8},{1,17},{9,25},{17,1},{25,9},{2,18},{10... | collective-permute-start | bytes 1966088 | tf_op jit(solution)/shard_map/ppermute | solution.py:269
  36.6 27.0 %collective-permute-start.25 = (f32[192,512]{1,0:T(8,128)S(1)}, f32[192,512]{1,0:T(8,128)S(1)}, u32[]{:S(2)}, u32[]{:S(2)}) collective-permute-start(f32[192,512]{1,0:T(8,128)S(1)} %get-tuple-element.73), channel_id=1, source_target_pairs={{0,1},{2,0},{4,2},{6,4},{7,6},{5,7},{3,5},{1,3},{8,10},{10,12},{12... | collective-permute-start | bytes 1179656 | tf_op jit(solution)/shard_map/ppermute | solution.py:297
  38.0 12.2 %collective-permute-start.15 = (f32[64,512]{1,0:T(8,128)S(1)}, f32[64,512]{1,0:T(8,128)S(1)}, u32[]{:S(2)}, u32[]{:S(2)}) collective-permute-start(f32[64,512]{1,0:T(8,128)S(1)} %collective-permute-done.7), channel_id=1, source_target_pairs={{0,2},{2,4},{4,6},{6,7},{7,5},{5,3},{3,1},{1,0},{8,9},{10,8},{12,1... | collective-permute-start | bytes 393224 | tf_op jit(solution)/shard_map/ppermute | solution.py:315
  50.3 13.3 %collective-permute-start.23 = (f32[192,512]{1,0:T(8,128)S(1)}, f32[192,512]{1,0:T(8,128)S(1)}, u32[]{:S(2)}, u32[]{:S(2)}) collective-permute-start(f32[192,512]{1,0:T(8,128)S(1)} %slice_add_fusion.4), channel_id=1, source_target_pairs={{0,2},{2,4},{4,6},{6,7},{7,5},{5,3},{3,1},{1,0},{8,9},{10,8},{12,1... | collective-permute-start | bytes 1179656 | tf_op jit(solution)/shard_map/ppermute | solution.py:297
  50.9 6.4 %collective-permute-start.17 = (f32[64,512]{1,0:T(8,128)S(1)}, f32[64,512]{1,0:T(8,128)S(1)}, u32[]{:S(2)}, u32[]{:S(2)}) collective-permute-start(f32[64,512]{1,0:T(8,128)S(1)} %collective-permute-done.8), channel_id=1, source_target_pairs={{0,1},{2,0},{4,2},{6,4},{7,6},{5,7},{3,5},{1,3},{8,10},{10,12},{12... | collective-permute-start | bytes 393224 | tf_op jit(solution)/shard_map/ppermute | solution.py:317
  52.3 10.6 %collective-permute-start.16 = (f32[64,512]{1,0:T(8,128)S(1)}, f32[64,512]{1,0:T(8,128)S(1)}, u32[]{:S(2)}, u32[]{:S(2)}) collective-permute-start(f32[64,512]{1,0:T(8,128)S(1)} %collective-permute-done.15), channel_id=1, source_target_pairs={{0,2},{2,4},{4,6},{6,7},{7,5},{5,3},{3,1},{1,0},{8,9},{10,8},{12,1... | collective-permute-start | bytes 393224 | tf_op jit(solution)/shard_map/ppermute | solution.py:315
  53.0 18.3 %collective-permute-start.13 = (f32[192,512]{1,0:T(8,128)S(1)}, f32[192,512]{1,0:T(8,128)S(1)}, u32[]{:S(2)}, u32[]{:S(2)}) collective-permute-start(f32[192,512]{1,0:T(8,128)S(1)} %get-tuple-element.65), channel_id=1, source_target_pairs={{0,2},{2,4},{4,6},{6,7},{7,5},{5,3},{3,1},{1,0},{8,9},{10,8},{12,1... | collective-permute-start | bytes 1179656 | tf_op jit(solution)/shard_map/ppermute | solution.py:297
  57.3 14.0 %collective-permute-start.14 = (f32[192,512]{1,0:T(8,128)S(1)}, f32[192,512]{1,0:T(8,128)S(1)}, u32[]{:S(2)}, u32[]{:S(2)}) collective-permute-start(f32[192,512]{1,0:T(8,128)S(1)} %get-tuple-element.66), channel_id=1, source_target_pairs={{0,1},{2,0},{4,2},{6,4},{7,6},{5,7},{3,5},{1,3},{8,10},{10,12},{12... | collective-permute-start | bytes 1179656 | tf_op jit(solution)/shard_map/ppermute | solution.py:297
  62.9 8.5 %collective-permute-start.18 = (f32[3,64,512]{2,1,0:T(8,128)S(1)}, f32[3,64,512]{2,1,0:T(8,128)S(1)}, u32[]{:S(2)}, u32[]{:S(2)}) collective-permute-start(f32[3,64,512]{2,1,0:T(8,128)S(1)} %pad_maximum_fusion.2), channel_id=1, source_target_pairs={{0,16},{8,24},{16,0},{24,8},{1,17},{9,25},{17,1},{25,9},{2,18},{10... | collective-permute-start | bytes 1179656 | tf_op jit(solution)/shard_map/ppermute | solution.py:269
  63.7 14.1 %collective-permute-start.26 = (f32[192,512]{1,0:T(8,128)S(1)}, f32[192,512]{1,0:T(8,128)S(1)}, u32[]{:S(2)}, u32[]{:S(2)}) collective-permute-start(f32[192,512]{1,0:T(8,128)S(1)} %get-tuple-element.107), channel_id=1, source_target_pairs={{0,1},{2,0},{4,2},{6,4},{7,6},{5,7},{3,5},{1,3},{8,10},{10,12},{12... | collective-permute-start | bytes 1179656 | tf_op jit(solution)/shard_map/ppermute | solution.py:297
  65.8 14.0 %collective-permute-start.24 = (f32[192,512]{1,0:T(8,128)S(1)}, f32[192,512]{1,0:T(8,128)S(1)}, u32[]{:S(2)}, u32[]{:S(2)}) collective-permute-start(f32[192,512]{1,0:T(8,128)S(1)} %get-tuple-element.108), channel_id=1, source_target_pairs={{0,2},{2,4},{4,6},{6,7},{7,5},{5,3},{3,1},{1,0},{8,9},{10,8},{12,1... | collective-permute-start | bytes 1179656 | tf_op jit(solution)/shard_map/ppermute | solution.py:341
  71.5 13.2 %collective-permute-start.19 = (f32[192,512]{1,0:T(8,128)S(1)}, f32[192,512]{1,0:T(8,128)S(1)}, u32[]{:S(2)}, u32[]{:S(2)}) collective-permute-start(f32[192,512]{1,0:T(8,128)S(1)} %get-tuple-element.71), channel_id=1, source_target_pairs={{0,2},{2,4},{4,6},{6,7},{7,5},{5,3},{3,1},{1,0},{8,9},{10,8},{12,1... | collective-permute-start | bytes 1179656 | tf_op jit(solution)/shard_map/ppermute | solution.py:297
  71.7 13.0 %collective-permute-start.28 = (f32[192,512]{1,0:T(8,128)S(1)}, f32[192,512]{1,0:T(8,128)S(1)}, u32[]{:S(2)}, u32[]{:S(2)}) collective-permute-start(f32[192,512]{1,0:T(8,128)S(1)} %get-tuple-element.89), channel_id=1, source_target_pairs={{0,1},{2,0},{4,2},{6,4},{7,6},{5,7},{3,5},{1,3},{8,10},{10,12},{12... | collective-permute-start | bytes 1179656 | tf_op jit(solution)/shard_map/ppermute | solution.py:297
  79.9 8.2 %collective-permute-start.27 = (f32[192,512]{1,0:T(8,128)S(1)}, f32[192,512]{1,0:T(8,128)S(1)}, u32[]{:S(2)}, u32[]{:S(2)}) collective-permute-start(f32[192,512]{1,0:T(8,128)S(1)} %fusion.refs_0_), channel_id=1, source_target_pairs={{0,8},{8,0},{16,24},{24,16},{1,9},{9,1},{17,25},{25,17},{2,10},{10... | collective-permute-start | bytes 1179656 | tf_op jit(solution)/shard_map/ppermute | solution.py:269
  84.9 5.7 %collective-permute-start.21 = (f32[96,512]{1,0:T(8,128)S(1)}, f32[96,512]{1,0:T(8,128)S(1)}, u32[]{:S(2)}, u32[]{:S(2)}) collective-permute-start(f32[96,512]{1,0:T(8,128)S(1)} %get-tuple-element.121), channel_id=1, source_target_pairs={{0,2},{2,4},{4,6},{6,7},{7,5},{5,3},{3,1},{1,0},{8,9},{10,8},{12,1... | collective-permute-start | bytes 589832 | tf_op jit(solution)/shard_map/ppermute | solution.py:366
  86.2 6.6 %collective-permute-start.20 = (f32[96,512]{1,0:T(8,128)S(1)}, f32[96,512]{1,0:T(8,128)S(1)}, u32[]{:S(2)}, u32[]{:S(2)}) collective-permute-start(f32[96,512]{1,0:T(8,128)S(1)} %get-tuple-element.122), channel_id=1, source_target_pairs={{0,2},{2,4},{4,6},{6,7},{7,5},{5,3},{3,1},{1,0},{8,9},{10,8},{12,1... | collective-permute-start | bytes 589832 | tf_op jit(solution)/shard_map/ppermute | solution.py:366
  92.8 1.5 %collective-permute-start.30 = (f32[96,512]{1,0:T(8,128)S(1)}, f32[96,512]{1,0:T(8,128)S(1)}, u32[]{:S(2)}, u32[]{:S(2)}) collective-permute-start(f32[96,512]{1,0:T(8,128)S(1)} %get-tuple-element.119.refs_6_), channel_id=1, source_target_pairs={{0,8},{8,0},{16,24},{24,16},{1,9},{9,1},{17,25},{25,17},{2,10},{10... | collective-permute-start | bytes 589832 | tf_op jit(solution)/shard_map/ppermute | solution.py:269
  92.9 1.7 %collective-permute-start.29 = (f32[96,512]{1,0:T(8,128)S(1)}, f32[96,512]{1,0:T(8,128)S(1)}, u32[]{:S(2)}, u32[]{:S(2)}) collective-permute-start(f32[96,512]{1,0:T(8,128)S(1)} %get-tuple-element.120.refs_5_), channel_id=1, source_target_pairs={{0,8},{8,0},{16,24},{24,16},{1,9},{9,1},{17,25},{25,17},{2,10},{10... | collective-permute-start | bytes 589832 | tf_op jit(solution)/shard_map/ppermute | solution.py:269
  97.7 9.2 %collective-permute-start.31 = (f32[256,256]{1,0:T(8,128)S(1)}, f32[256,256]{1,0:T(8,128)S(1)}, u32[]{:S(2)}, u32[]{:S(2)}) collective-permute-start(f32[256,256]{1,0:T(8,128)S(1)} %get-tuple-element.96), channel_id=1, source_target_pairs={{0,16},{8,24},{16,0},{24,8},{1,17},{9,25},{17,1},{25,9},{2,18},{10... | collective-permute-start | bytes 786440 | tf_op jit(solution)/shard_map/ppermute | solution.py:269
  98.2 10.3 %collective-permute-start.33 = (f32[128,512]{1,0:T(8,128)S(1)}, f32[128,512]{1,0:T(8,128)S(1)}, u32[]{:S(2)}, u32[]{:S(2)}) collective-permute-start(f32[128,512]{1,0:T(8,128)S(1)} %get-tuple-element.98), channel_id=1, source_target_pairs={{0,1},{1,0},{2,3},{3,2},{4,5},{5,4},{6,7},{7,6},{8,9},{9,8},{10,11... | collective-permute-start | bytes 786440 | tf_op jit(solution)/shard_map/ppermute | solution.py:272
  99.8 12.7 %collective-permute-start.38 = (f32[256,256]{1,0:T(8,128)S(1)}, f32[256,256]{1,0:T(8,128)S(1)}, u32[]{:S(2)}, u32[]{:S(2)}) collective-permute-start(f32[256,256]{1,0:T(8,128)S(1)} %get-tuple-element.100), channel_id=1, source_target_pairs={{0,16},{8,24},{16,0},{24,8},{1,17},{9,25},{17,1},{25,9},{2,18},{10... | collective-permute-start | bytes 786440 | tf_op jit(solution)/shard_map/ppermute | solution.py:269
  101.3 12.9 %collective-permute-start.40 = (f32[128,512]{1,0:T(8,128)S(1)}, f32[128,512]{1,0:T(8,128)S(1)}, u32[]{:S(2)}, u32[]{:S(2)}) collective-permute-start(f32[128,512]{1,0:T(8,128)S(1)} %get-tuple-element.102), channel_id=1, source_target_pairs={{0,1},{1,0},{2,3},{3,2},{4,5},{5,4},{6,7},{7,6},{8,9},{9,8},{10,11... | collective-permute-start | bytes 786440 | tf_op jit(solution)/shard_map/ppermute | solution.py:272
  106.9 8.8 %collective-permute-start.32 = (f32[128,256]{1,0:T(8,128)S(1)}, f32[128,256]{1,0:T(8,128)S(1)}, u32[]{:S(2)}, u32[]{:S(2)}) collective-permute-start(f32[128,256]{1,0:T(8,128)S(1)} %slice.161), channel_id=1, source_target_pairs={{0,1},{1,0},{2,3},{3,2},{4,5},{5,4},{6,7},{7,6},{8,9},{9,8},{10,11... | collective-permute-start | bytes 393224 | tf_op jit(solution)/shard_map/ppermute | solution.py:272
  108.6 7.1 %collective-permute-start.34 = (f32[128,256]{1,0:T(8,128)S(1)}, f32[128,256]{1,0:T(8,128)S(1)}, u32[]{:S(2)}, u32[]{:S(2)}) collective-permute-start(f32[128,256]{1,0:T(8,128)S(1)} %slice.163), channel_id=1, source_target_pairs={{0,16},{8,24},{16,0},{24,8},{1,17},{9,25},{17,1},{25,9},{2,18},{10... | collective-permute-start | bytes 393224 | tf_op jit(solution)/shard_map/ppermute | solution.py:269
  112.5 7.7 %collective-permute-start.39 = (f32[128,256]{1,0:T(8,128)S(1)}, f32[128,256]{1,0:T(8,128)S(1)}, u32[]{:S(2)}, u32[]{:S(2)}) collective-permute-start(f32[128,256]{1,0:T(8,128)S(1)} %slice.171), channel_id=1, source_target_pairs={{0,1},{1,0},{2,3},{3,2},{4,5},{5,4},{6,7},{7,6},{8,9},{9,8},{10,11... | collective-permute-start | bytes 393224 | tf_op jit(solution)/shard_map/ppermute | solution.py:272
  114.2 6.0 %collective-permute-start.41 = (f32[128,256]{1,0:T(8,128)S(1)}, f32[128,256]{1,0:T(8,128)S(1)}, u32[]{:S(2)}, u32[]{:S(2)}) collective-permute-start(f32[128,256]{1,0:T(8,128)S(1)} %slice.173), channel_id=1, source_target_pairs={{0,16},{8,24},{16,0},{24,8},{1,17},{9,25},{17,1},{25,9},{2,18},{10... | collective-permute-start | bytes 393224 | tf_op jit(solution)/shard_map/ppermute | solution.py:269
  115.8 7.7 %collective-permute-start.37 = (f32[32,512]{1,0:T(8,128)S(1)}, f32[32,512]{1,0:T(8,128)S(1)}, u32[]{:S(2)}, u32[]{:S(2)}) collective-permute-start(f32[32,512]{1,0:T(8,128)S(1)} %get-tuple-element.127), channel_id=1, source_target_pairs={{0,6},{1,7},{2,4},{3,5},{4,2},{5,3},{6,0},{7,1},{8,14},{9,15},{10,... | collective-permute-start | bytes 196616 | tf_op jit(solution)/shard_map/ppermute | solution.py:272
  118.9 6.1 %collective-permute-start.35 = (f32[32,512]{1,0:T(8,128)S(1)}, f32[32,512]{1,0:T(8,128)S(1)}, u32[]{:S(2)}, u32[]{:S(2)}) collective-permute-start(f32[32,512]{1,0:T(8,128)S(1)} %get-tuple-element.129), channel_id=1, source_target_pairs={{0,2},{1,3},{2,0},{3,1},{4,6},{5,7},{6,4},{7,5},{8,10},{9,11},{10,... | collective-permute-start | bytes 196616 | tf_op jit(solution)/shard_map/ppermute | solution.py:272
  118.9 8.6 %collective-permute-start.36 = (f32[32,512]{1,0:T(8,128)S(1)}, f32[32,512]{1,0:T(8,128)S(1)}, u32[]{:S(2)}, u32[]{:S(2)}) collective-permute-start(f32[32,512]{1,0:T(8,128)S(1)} %get-tuple-element.130), channel_id=1, source_target_pairs={{0,4},{1,5},{2,6},{3,7},{4,0},{5,1},{6,2},{7,3},{8,12},{9,13},{10,... | collective-permute-start | bytes 196616 | tf_op jit(solution)/shard_map/ppermute | solution.py:272
  120.3 7.2 %collective-permute-start.44 = (f32[32,512]{1,0:T(8,128)S(1)}, f32[32,512]{1,0:T(8,128)S(1)}, u32[]{:S(2)}, u32[]{:S(2)}) collective-permute-start(f32[32,512]{1,0:T(8,128)S(1)} %get-tuple-element.123), channel_id=1, source_target_pairs={{0,6},{1,7},{2,4},{3,5},{4,2},{5,3},{6,0},{7,1},{8,14},{9,15},{10,... | collective-permute-start | bytes 196616 | tf_op jit(solution)/shard_map/ppermute | solution.py:272
  123.5 5.1 %collective-permute-start.42 = (f32[32,512]{1,0:T(8,128)S(1)}, f32[32,512]{1,0:T(8,128)S(1)}, u32[]{:S(2)}, u32[]{:S(2)}) collective-permute-start(f32[32,512]{1,0:T(8,128)S(1)} %get-tuple-element.125), channel_id=1, source_target_pairs={{0,2},{1,3},{2,0},{3,1},{4,6},{5,7},{6,4},{7,5},{8,10},{9,11},{10,... | collective-permute-start | bytes 196616 | tf_op jit(solution)/shard_map/ppermute | solution.py:272
  123.5 5.8 %collective-permute-start.43 = (f32[32,512]{1,0:T(8,128)S(1)}, f32[32,512]{1,0:T(8,128)S(1)}, u32[]{:S(2)}, u32[]{:S(2)}) collective-permute-start(f32[32,512]{1,0:T(8,128)S(1)} %get-tuple-element.126), channel_id=1, source_target_pairs={{0,4},{1,5},{2,6},{3,7},{4,0},{5,1},{6,2},{7,3},{8,12},{9,13},{10,... | collective-permute-start | bytes 196616 | tf_op jit(solution)/shard_map/ppermute | solution.py:272
  129.9 1.3 collective-permute-start.45

commit v5 on v4

--- a/solution.py
+++ b/solution.py
@@ -12,7 +12,6 @@
 NEAR_COST, FAR_COST = 40, 0
 EARLY, PINS = 2, 2
 TIE1, TIE2 = 2, 3
-CUTS = 2
 ROWS_OVER_ROWS = ((0,), (0,))
 LANES_OVER_LANES = ((1,), (1,))
 
@@ -323,6 +322,8 @@
         first_near, line = lax.optimization_barrier((near_part[0], line))
         near_part = (first_near, near_part[1])
         near = rounds(near_part, 0, 1, [None, None])
+        later_near, line = lax.optimization_barrier((near_part[1], line))
+        near_part = (near_part[0], later_near)
         for t in range(1, reach):
             if t == EARLY:
                 far, near = lax.optimization_barrier((far, near))
@@ -362,10 +363,9 @@
             flops=6 * n_tall * n_deep * n_wide,
         )
         held = rounds(far_part, min(TIE2, reach), reach, held)
-        cuts = [slice(k * height // CUTS, (k + 1) * height // CUTS) for k in range(CUTS)]
-        arrived = [lax.ppermute(held[0][rows], both, streams[0]) for rows in cuts]
+        arrived = lax.ppermute(held[0], both, streams[0])
         arrived, near_side = lax.optimization_barrier((arrived, near_side))
-        far_rows = [x + held[1][rows] for x, rows in zip(arrived, cuts)]
+        far_rows = [arrived + held[1]]
         far_rows += [swap(x, 1) for x in far_rows]
         scale_inv = float((samples.shape[0] * n_rows) ** -0.5)
         half, wide, n_way = n_tall // 4, n_wide // 2, n_feat // 2

time: 133 us -> 131 us (0.985)
    ppermute x12, waiting for transfers between devices: 20.1 us -> 15 us  [rounds(): held[s] = lax.ppermute(held[s], both, streams[s]) + piece]
    ppermute x2 -> x1, waiting for transfers between devices: 3.06 us -> 7.28 us  [on_device(): arrived = lax.ppermute(held[0], both, streams[0])]
    ppermute x1, waiting for transfers between devices: 1.97 us -> 0.01 us  [on_device(): near = lax.ppermute(near[0], both, streams[0]) + near[1]]
    ppermute x14 -> x13, starting transfers between devices: 8.47 us -> 9.75 us  [swap(): return lax.ppermute(a, 'rows', [(i, i ^ bit) for i in range(n_rows)])]
    ppermute x2 -> x1, starting transfers between devices: 2.85 us -> 1.64 us  [on_device(): arrived = lax.ppermute(held[0], both, streams[0])]
    ppermute x14 -> x13, waiting for transfers between devices: 10.2 us -> 11.2 us  [swap(): return lax.ppermute(a, 'rows', [(i, i ^ bit) for i in range(n_rows)])]
  transfers between devices with their start and end apart: 46 -> 44, of which waited for: 22 -> 22; matrix products, arithmetic and copies ran while one was open for 3% -> 2% of each run, Pallas kernels for 14% -> 14%
where the time goes in v5:
time: 131 us
  waiting for transfers between devices  53.5 us (41%)
  starting transfers between devices  46.8 us (36%)
  Pallas kernels  23.2 us (18%)
  local copies, waits for them, and re-layouts  5.91 us (5%)
  other arithmetic  1.41 us (1%)
    pallas_call x9, Pallas kernels, call(): pl.pallas_call(kernel, out_shape=outs, grid_spec=pltpu.PrefetchScalarGrid...  23.2 us
    ppermute x12, starting transfers between devices, rounds(): held[s] = lax.ppermute(held[s], both, streams[s]) + piece  15.5 us
    ppermute x12, waiting for transfers between devices, rounds(): held[s] = lax.ppermute(held[s], both, streams[s]) + piece  15 us
    ppermute x10, starting transfers between devices, swap_feat(): return lax.ppermute(a, 'feat', [(i, i ^ bit) for i in range(n_feat)])  12.9 us
    ppermute x13, waiting for transfers between devices, swap(): return lax.ppermute(a, 'rows', [(i, i ^ bit) for i in range(n_rows)])  11.2 us
    ppermute x4, waiting for transfers between devices, pass_components(): line[step] = lax.ppermute(line[step - 1], both, streams[0])  10.4 us
    ppermute x13, starting transfers between devices, swap(): return lax.ppermute(a, 'rows', [(i, i ^ bit) for i in range(n_rows)])  9.75 us
    ppermute x1, waiting for transfers between devices, on_device(): arrived = lax.ppermute(held[0], both, streams[0])  7.28 us
  transfers between devices with their start and end apart: 44, of which 22 were waited for; matrix products, arithmetic and copies ran while one was open for 2% of the time, Pallas kernels for 14%

profile of v5, /device:TPU:0, one launch (start us, length us, event | category | flops | bytes accessed | tf_op | source)
XLA Modules:
  0.0 131.2 jit_solution(17049777505863853516)
XLA Ops:
  0.5 2.5 %collective-permute-start = (f32[1024,256]{1,0:T(8,128)}, f32[1024,256]{1,0:T(8,128)S(1)}, u32[]{:S(2)}, u32[]{:S(2)}) collective-permute-start(f32[1024,256]{1,0:T(8,128)} %refs_2_.3), channel_id=1, source_target_pairs={{0,16},{8,24},{16,0},{24,8},{1,17},{9,25},{17,1},{25,9},{2,18},{10... | collective-permute-start | bytes 3145736 | tf_op jit(solution)/shard_map/ppermute | solution.py:268
  3.0 1.0 copy.7
  5.4 1.5 %collective-permute-start.4 = (f32[64,512]{1,0:T(8,128)S(1)}, f32[64,512]{1,0:T(8,128)S(1)}, u32[]{:S(2)}, u32[]{:S(2)}) collective-permute-start(f32[64,512]{1,0:T(8,128)S(1)} %pad_maximum_fusion.3), channel_id=1, source_target_pairs={{0,1},{2,0},{4,2},{6,4},{7,6},{5,7},{3,5},{1,3},{8,10},{10,12},{12... | collective-permute-start | bytes 393224 | tf_op jit(solution)/shard_map/ppermute | solution.py:316
  7.4 2.8 %copy-done = f32[1536,1024]{1,0:T(8,128)S(1)} copy-done((f32[1536,1024]{1,0:T(8,128)S(1)}, f32[1536,1024]{1,0:T(8,128)}, u32[]{:S(2)}) %copy-start) | copy-done | bytes 6291480
  10.2 1.2 copy-done.1
  11.5 2.2 %shard_map.46 = f32[384,512]{1,0:T(8,128)S(1)} custom-call(s32[17]{0:T(128)S(1)} %fusion.7.table, f32[1536,1024]{1,0:T(8,128)S(1)} %copy-done, f32[1536,1024]{1,0:T(8,128)S(1)} %copy-done, f32[1024,256]{1,0:T(8,128)S(1)} %copy-done.1, f32[1024,256]{1,0:T(8,128)S(1)} %collective-permute-done.1.refs_3_), custom_call_target="tpu_custom_call" | custom-call | flops 16106127360 | bytes 14680064 | tf_op jit(solution)/shard_map/pallas_call | solution.py:50
  13.8 1.5 %collective-permute-start.6 = (f32[192,512]{1,0:T(8,128)S(1)}, f32[192,512]{1,0:T(8,128)S(1)}, u32[]{:S(2)}, u32[]{:S(2)}) collective-permute-start(f32[192,512]{1,0:T(8,128)S(1)} %get-tuple-element.121), channel_id=1, source_target_pairs={{0,1},{2,0},{4,2},{6,4},{7,6},{5,7},{3,5},{1,3},{8,10},{10,12},{12... | collective-permute-start | bytes 1179656 | tf_op jit(solution)/shard_map/ppermute | solution.py:296
  15.9 5.1 %shard_map.47 = f32[1152,512]{1,0:T(8,128)S(1)} custom-call(s32[17]{0:T(128)S(1)} %fusion.7.table, f32[1536,1024]{1,0:T(8,128)S(1)} %copy-done, f32[1536,1024]{1,0:T(8,128)S(1)} %copy-done, f32[1024,256]{1,0:T(8,128)S(1)} %copy-done.1, f32[1024,256]{1,0:T(8,128)S(1)} %collective-permute-done.1.refs_3_), custom_call_target="tpu_custom_call" | custom-call | flops 48318382080 | bytes 14680064 | tf_op jit(solution)/shard_map/pallas_call | solution.py:50
  21.0 1.6 %collective-permute-start.7 = (f32[64,512]{1,0:T(8,128)S(1)}, f32[64,512]{1,0:T(8,128)S(1)}, u32[]{:S(2)}, u32[]{:S(2)}) collective-permute-start(f32[64,512]{1,0:T(8,128)S(1)} %collective-permute-done.3), channel_id=1, source_target_pairs={{0,2},{2,4},{4,6},{6,7},{7,5},{5,3},{3,1},{1,0},{8,9},{10,8},{12,1... | collective-permute-start | bytes 393224 | tf_op jit(solution)/shard_map/ppermute | solution.py:314
  23.1 2.8 %collective-permute-done.6 = f32[192,512]{1,0:T(8,128)S(1)} collective-permute-done((f32[192,512]{1,0:T(8,128)S(1)}, f32[192,512]{1,0:T(8,128)S(1)}, u32[]{:S(2)}, u32[]{:S(2)}) %collective-permute-start.6) | collective-permute-done | bytes 393248 | tf_op jit(solution)/shard_map/ppermute | solution.py:296
  26.0 1.4 %collective-permute-done.7 = f32[64,512]{1,0:T(8,128)S(1)} collective-permute-done((f32[64,512]{1,0:T(8,128)S(1)}, f32[64,512]{1,0:T(8,128)S(1)}, u32[]{:S(2)}, u32[]{:S(2)}) %collective-permute-start.7) | collective-permute-done | bytes 131104 | tf_op jit(solution)/shard_map/ppermute | solution.py:314
  27.3 1.3 collective-permute-done.8
  28.7 1.6 %collective-permute-start.21 = (f32[192,512]{1,0:T(8,128)S(1)}, f32[192,512]{1,0:T(8,128)S(1)}, u32[]{:S(2)}, u32[]{:S(2)}) collective-permute-start(f32[192,512]{1,0:T(8,128)S(1)} %get-tuple-element.79), channel_id=1, source_target_pairs={{0,2},{2,4},{4,6},{6,7},{7,5},{5,3},{3,1},{1,0},{8,9},{10,8},{12,1... | collective-permute-start | bytes 1179656 | tf_op jit(solution)/shard_map/ppermute | solution.py:296
  31.3 2.2 %shard_map.48 = f32[384,512]{1,0:T(8,128)S(1)} custom-call(s32[17]{0:T(128)S(1)} %fusion.7.table, f32[1536,1024]{1,0:T(8,128)S(1)} %copy-done, f32[1536,1024]{1,0:T(8,128)S(1)} %copy-done, f32[1024,256]{1,0:T(8,128)S(1)} %collective-permute-done.refs_2_, f32[1024,256]{1,0:T(8,128)S(1)} %collective-permute-done.9.refs_3_), custom_call_target="tpu_custom_call" | custom-call | bytes 14680064 | tf_op jit(solution)/shard_map/pallas_call | solution.py:50
  34.1 1.6 %collective-permute-start.10 = (f32[192,512]{1,0:T(8,128)S(1)}, f32[192,512]{1,0:T(8,128)S(1)}, u32[]{:S(2)}, u32[]{:S(2)}) collective-permute-start(f32[192,512]{1,0:T(8,128)S(1)} %get-tuple-element.120), channel_id=1, source_target_pairs={{0,2},{2,4},{4,6},{6,7},{7,5},{5,3},{3,1},{1,0},{8,9},{10,8},{12,1... | collective-permute-start | bytes 1179656 | tf_op jit(solution)/shard_map/ppermute | solution.py:296
  36.2 1.2 collective-permute-start.24
  38.3 5.1 %shard_map.49 = f32[1152,512]{1,0:T(8,128)S(1)} custom-call(s32[17]{0:T(128)S(1)} %fusion.7.table, f32[1536,1024]{1,0:T(8,128)S(1)} %copy-done, f32[1536,1024]{1,0:T(8,128)S(1)} %copy-done, f32[1024,256]{1,0:T(8,128)S(1)} %collective-permute-done.refs_2_, f32[1024,256]{1,0:T(8,128)S(1)} %collective-permute-done.9.refs_3_), custom_call_target="tpu_custom_call" | custom-call | bytes 14680064 | tf_op jit(solution)/shard_map/pallas_call | solution.py:50
  43.4 5.6 %collective-permute-done.15 = f32[64,512]{1,0:T(8,128)S(1)} collective-permute-done((f32[64,512]{1,0:T(8,128)S(1)}, f32[64,512]{1,0:T(8,128)S(1)}, u32[]{:S(2)}, u32[]{:S(2)}) %collective-permute-start.15) | collective-permute-done | bytes 131104 | tf_op jit(solution)/shard_map/ppermute | solution.py:314
  49.0 1.6 %collective-permute-start.22 = (f32[192,512]{1,0:T(8,128)S(1)}, f32[192,512]{1,0:T(8,128)S(1)}, u32[]{:S(2)}, u32[]{:S(2)}) collective-permute-start(f32[192,512]{1,0:T(8,128)S(1)} %slice_add_fusion.8), channel_id=1, source_target_pairs={{0,2},{2,4},{4,6},{6,7},{7,5},{5,3},{3,1},{1,0},{8,9},{10,8},{12,1... | collective-permute-start | bytes 1179656 | tf_op jit(solution)/shard_map/ppermute | solution.py:296
  51.0 1.6 %collective-permute-start.16 = (f32[64,512]{1,0:T(8,128)S(1)}, f32[64,512]{1,0:T(8,128)S(1)}, u32[]{:S(2)}, u32[]{:S(2)}) collective-permute-start(f32[64,512]{1,0:T(8,128)S(1)} %collective-permute-done.15), channel_id=1, source_target_pairs={{0,2},{2,4},{4,6},{6,7},{7,5},{5,3},{3,1},{1,0},{8,9},{10,8},{12,1... | collective-permute-start | bytes 393224 | tf_op jit(solution)/shard_map/ppermute | solution.py:314
  52.7 1.6 %collective-permute-start.13 = (f32[192,512]{1,0:T(8,128)S(1)}, f32[192,512]{1,0:T(8,128)S(1)}, u32[]{:S(2)}, u32[]{:S(2)}) collective-permute-start(f32[192,512]{1,0:T(8,128)S(1)} %get-tuple-element.72), channel_id=1, source_target_pairs={{0,2},{2,4},{4,6},{6,7},{7,5},{5,3},{3,1},{1,0},{8,9},{10,8},{12,1... | collective-permute-start | bytes 1179656 | tf_op jit(solution)/shard_map/ppermute | solution.py:296
  54.3 2.6 %collective-permute-done.17 = f32[64,512]{1,0:T(8,128)S(1)} collective-permute-done((f32[64,512]{1,0:T(8,128)S(1)}, f32[64,512]{1,0:T(8,128)S(1)}, u32[]{:S(2)}, u32[]{:S(2)}) %collective-permute-start.17) | collective-permute-done | bytes 131104 | tf_op jit(solution)/shard_map/ppermute | solution.py:316
  57.4 3.5 %collective-permute-done.16 = f32[64,512]{1,0:T(8,128)S(1)} collective-permute-done((f32[64,512]{1,0:T(8,128)S(1)}, f32[64,512]{1,0:T(8,128)S(1)}, u32[]{:S(2)}, u32[]{:S(2)}) %collective-permute-start.16) | collective-permute-done | bytes 131104 | tf_op jit(solution)/shard_map/ppermute | solution.py:314
  61.0 1.4 %collective-permute-start.18 = (f32[3,64,512]{2,1,0:T(8,128)S(1)}, f32[3,64,512]{2,1,0:T(8,128)S(1)}, u32[]{:S(2)}, u32[]{:S(2)}) collective-permute-start(f32[3,64,512]{2,1,0:T(8,128)S(1)} %pad_maximum_fusion.2), channel_id=1, source_target_pairs={{0,16},{8,24},{16,0},{24,8},{1,17},{9,25},{17,1},{25,9},{2,18},{10... | collective-permute-start | bytes 1179656 | tf_op jit(solution)/shard_map/ppermute | solution.py:268
  62.6 2.8 %collective-permute-start.25 = (f32[192,512]{1,0:T(8,128)S(1)}, f32[192,512]{1,0:T(8,128)S(1)}, u32[]{:S(2)}, u32[]{:S(2)}) collective-permute-start(f32[192,512]{1,0:T(8,128)S(1)} %get-tuple-element.111), channel_id=1, source_target_pairs={{0,1},{2,0},{4,2},{6,4},{7,6},{5,7},{3,5},{1,3},{8,10},{10,12},{12... | collective-permute-start | bytes 1179656 | tf_op jit(solution)/shard_map/ppermute | solution.py:296
  65.4 4.0 %collective-permute-done.13 = f32[192,512]{1,0:T(8,128)S(1)} collective-permute-done((f32[192,512]{1,0:T(8,128)S(1)}, f32[192,512]{1,0:T(8,128)S(1)}, u32[]{:S(2)}, u32[]{:S(2)}) %collective-permute-start.13) | collective-permute-done | bytes 393248 | tf_op jit(solution)/shard_map/ppermute | solution.py:296
  69.8 1.6 %collective-permute-start.19 = (f32[192,512]{1,0:T(8,128)S(1)}, f32[192,512]{1,0:T(8,128)S(1)}, u32[]{:S(2)}, u32[]{:S(2)}) collective-permute-start(f32[192,512]{1,0:T(8,128)S(1)} %get-tuple-element.78), channel_id=1, source_target_pairs={{0,2},{2,4},{4,6},{6,7},{7,5},{5,3},{3,1},{1,0},{8,9},{10,8},{12,1... | collective-permute-start | bytes 1179656 | tf_op jit(solution)/shard_map/ppermute | solution.py:296
  71.4 6.1 %collective-permute-done.25 = f32[192,512]{1,0:T(8,128)S(1)} collective-permute-done((f32[192,512]{1,0:T(8,128)S(1)}, f32[192,512]{1,0:T(8,128)S(1)}, u32[]{:S(2)}, u32[]{:S(2)}) %collective-permute-start.25) | collective-permute-done | bytes 393248 | tf_op jit(solution)/shard_map/ppermute | solution.py:296
  77.6 2.2 %collective-permute-done.19 = f32[192,512]{1,0:T(8,128)S(1)} collective-permute-done((f32[192,512]{1,0:T(8,128)S(1)}, f32[192,512]{1,0:T(8,128)S(1)}, u32[]{:S(2)}, u32[]{:S(2)}) %collective-permute-start.19) | collective-permute-done | bytes 393248 | tf_op jit(solution)/shard_map/ppermute | solution.py:296
  79.9 1.6 %collective-permute-start.20 = (f32[192,512]{1,0:T(8,128)S(1)}, f32[192,512]{1,0:T(8,128)S(1)}, u32[]{:S(2)}, u32[]{:S(2)}) collective-permute-start(f32[192,512]{1,0:T(8,128)S(1)} %slice_add_fusion.1), channel_id=1, source_target_pairs={{0,2},{2,4},{4,6},{6,7},{7,5},{5,3},{3,1},{1,0},{8,9},{10,8},{12,1... | collective-permute-start | bytes 1179656 | tf_op jit(solution)/shard_map/ppermute | solution.py:366
  82.2 1.6 %shard_map.50 = (f32[512,384]{1,0:T(8,128)S(1)}, bf16[512,512]{1,0:T(8,128)(2,1)S(1)}, bf16[512,512]{1,0:T(8,128)(2,1)S(1)}, bf16[384,512]{1,0:T(8,128)(2,1)S(1)}, bf16[384,512]{1,0:T(8,128)(2,1)S(1)}) custom-call(s32[17]{0:T(128)S(1)} %fusion.7.table, f32[192,512]{1,0:T(8,128)S(1)} %add_add_fusion.refs_0_, f32[192,512]{1,0:T(8,128)S(1)} %collective-permute-done.26.refs_1_, ...), custom_call_target="tpu_custom_call" | custom-call | flops 603979776 | bytes 2883584 | tf_op jit(solution)/shard_map/pallas_call | solution.py:50
  83.9 7.3 %collective-permute-done.20 = f32[192,512]{1,0:T(8,128)S(1)} collective-permute-done((f32[192,512]{1,0:T(8,128)S(1)}, f32[192,512]{1,0:T(8,128)S(1)}, u32[]{:S(2)}, u32[]{:S(2)}) %collective-permute-start.20) | collective-permute-done | bytes 393248 | tf_op jit(solution)/shard_map/ppermute | solution.py:366
  91.3 1.7 %collective-permute-done.28.refs_6_ = f32[192,512]{1,0:T(8,128)S(1)} collective-permute-done((f32[192,512]{1,0:T(8,128)S(1)}, f32[192,512]{1,0:T(8,128)S(1)}, u32[]{:S(2)}, u32[]{:S(2)}) %collective-permute-start.28) | collective-permute-done | bytes 393248 | tf_op jit(solution)/shard_map/ppermute | solution.py:268
  93.0 3.1 %shard_map.51 = (f32[256,256]{1,0:T(8,128)S(1)}, f32[256,256]{1,0:T(8,128)S(1)}, f32[128,512]{1,0:T(8,128)S(1)}, f32[128,512]{1,0:T(8,128)S(1)}, bf16[512,384]{1...) custom-call(s32[17]{0:T(128)S(1)} %fusion.7.table, ...), custom_call_target="tpu_custom_call" | custom-call | flops 1207959552 | bytes 5242880 | tf_op jit(solution)/shard_map/pallas_call | solution.py:50
  96.7 1.2 collective-permute-start.31
  98.8 1.5 %collective-permute-start.38 = (f32[128,512]{1,0:T(8,128)S(1)}, f32[128,512]{1,0:T(8,128)S(1)}, u32[]{:S(2)}, u32[]{:S(2)}) collective-permute-start(f32[128,512]{1,0:T(8,128)S(1)} %get-tuple-element.108), channel_id=1, source_target_pairs={{0,1},{1,0},{2,3},{3,2},{4,5},{5,4},{6,7},{7,6},{8,9},{9,8},{10,11... | collective-permute-start | bytes 786440 | tf_op jit(solution)/shard_map/ppermute | solution.py:271
  100.3 1.9 %shard_map.52 = (f32[256,256]{1,0:T(8,128)S(1)}, f32[256,256]{1,0:T(8,128)S(1)}, f32[128,512]{1,0:T(8,128)S(1)}, f32[128,512]{1,0:T(8,128)S(1)}) custom-call(s32[17]{0:T(128)S(1)} %fusion.7.table, bf16[512,384]{1,0:T(8,128)(2,1)S(1)} %get-tuple-element.97.refs_0_, bf16[512,384]{1,0:T(8,128)(2,1)S(1)} %get-tuple-element.98.refs_1_, ...), custom_call_target="tpu_custom_call" | custom-call | flops 603979776 | bytes 4718592 | tf_op jit(solution)/shard_map/pallas_call | solution.py:50
  102.1 3.2 %collective-permute-done.29 = f32[256,256]{1,0:T(8,128)S(1)} collective-permute-done((f32[256,256]{1,0:T(8,128)S(1)}, f32[256,256]{1,0:T(8,128)S(1)}, u32[]{:S(2)}, u32[]{:S(2)}) %collective-permute-start.29) | collective-permute-done | bytes 262176 | tf_op jit(solution)/shard_map/ppermute | solution.py:268
  106.1 1.5 %collective-permute-start.32 = (f32[128,256]{1,0:T(8,128)S(1)}, f32[128,256]{1,0:T(8,128)S(1)}, u32[]{:S(2)}, u32[]{:S(2)}) collective-permute-start(f32[128,256]{1,0:T(8,128)S(1)} %slice.137), channel_id=1, source_target_pairs={{0,16},{8,24},{16,0},{24,8},{1,17},{9,25},{17,1},{25,9},{2,18},{10... | collective-permute-start | bytes 393224 | tf_op jit(solution)/shard_map/ppermute | solution.py:268
  107.5 3.4 %collective-permute-done.36 = f32[256,256]{1,0:T(8,128)S(1)} collective-permute-done((f32[256,256]{1,0:T(8,128)S(1)}, f32[256,256]{1,0:T(8,128)S(1)}, u32[]{:S(2)}, u32[]{:S(2)}) %collective-permute-start.36) | collective-permute-done | bytes 262176 | tf_op jit(solution)/shard_map/ppermute | solution.py:268
  111.7 1.5 %collective-permute-start.39 = (f32[128,256]{1,0:T(8,128)S(1)}, f32[128,256]{1,0:T(8,128)S(1)}, u32[]{:S(2)}, u32[]{:S(2)}) collective-permute-start(f32[128,256]{1,0:T(8,128)S(1)} %slice.147), channel_id=1, source_target_pairs={{0,16},{8,24},{16,0},{24,8},{1,17},{9,25},{17,1},{25,9},{2,18},{10... | collective-permute-start | bytes 393224 | tf_op jit(solution)/shard_map/ppermute | solution.py:268
  114.2 3.5 %collective-permute-start.35 = (f32[32,512]{1,0:T(8,128)S(1)}, f32[32,512]{1,0:T(8,128)S(1)}, u32[]{:S(2)}, u32[]{:S(2)}) collective-permute-start(f32[32,512]{1,0:T(8,128)S(1)} %get-tuple-element.127), channel_id=1, source_target_pairs={{0,6},{1,7},{2,4},{3,5},{4,2},{5,3},{6,0},{7,1},{8,14},{9,15},{10,... | collective-permute-start | bytes 196616 | tf_op jit(solution)/shard_map/ppermute | solution.py:271
  118.8 3.5 %collective-permute-start.42 = (f32[32,512]{1,0:T(8,128)S(1)}, f32[32,512]{1,0:T(8,128)S(1)}, u32[]{:S(2)}, u32[]{:S(2)}) collective-permute-start(f32[32,512]{1,0:T(8,128)S(1)} %get-tuple-element.123), channel_id=1, source_target_pairs={{0,6},{1,7},{2,4},{3,5},{4,2},{5,3},{6,0},{7,1},{8,14},{9,15},{10,... | collective-permute-start | bytes 196616 | tf_op jit(solution)/shard_map/ppermute | solution.py:271
  122.3 1.0 collective-permute-start.41
  124.0 2.0 %collective-permute-done.34.refs_2_ = f32[32,512]{1,0:T(8,128)S(1)} collective-permute-done((f32[32,512]{1,0:T(8,128)S(1)}, f32[32,512]{1,0:T(8,128)S(1)}, u32[]{:S(2)}, u32[]{:S(2)}) %collective-permute-start.34) | collective-permute-done | bytes 65568 | tf_op jit(solution)/shard_map/ppermute | solution.py:271
  126.1 1.2 collective-permute-done.40.refs_5_
  128.7 1.2 collective-permute-done.43.other_ref
  129.9 1.3 shard_map.54
  (89 shorter events, 16.1 us)
Async XLA Ops:
  0.0 7.4 %collective-permute-start.1 = (f32[1024,256]{1,0:T(8,128)}, f32[1024,256]{1,0:T(8,128)S(1)}, u32[]{:S(2)}, u32[]{:S(2)}) collective-permute-start(f32[1024,256]{1,0:T(8,128)} %refs_2_.3), channel_id=1, source_target_pairs={{0,8},{8,0},{16,24},{24,16},{1,9},{9,1},{17,25},{25,17},{2,10},{10... | collective-permute-start | bytes 3145736 | tf_op jit(solution)/shard_map/ppermute | solution.py:268
  0.5 28.2 %collective-permute-start = (f32[1024,256]{1,0:T(8,128)}, f32[1024,256]{1,0:T(8,128)S(1)}, u32[]{:S(2)}, u32[]{:S(2)}) collective-permute-start(f32[1024,256]{1,0:T(8,128)} %refs_2_.3), channel_id=1, source_target_pairs={{0,16},{8,24},{16,0},{24,8},{1,17},{9,25},{17,1},{25,9},{2,18},{10... | collective-permute-start | bytes 3145736 | tf_op jit(solution)/shard_map/ppermute | solution.py:268
  4.0 1.3 %collective-permute-start.2 = (f32[64,256]{1,0:T(8,128)S(1)}, f32[64,256]{1,0:T(8,128)S(1)}, u32[]{:S(2)}, u32[]{:S(2)}) collective-permute-start(f32[64,256]{1,0:T(8,128)S(1)} %dynamic-slice_bitcast_fusion), channel_id=1, source_target_pairs={{0,8},{8,0},{16,24},{24,16},{1,9},{9,1},{17,25},{25,17},{2,10},{10... | collective-permute-start | bytes 196616 | tf_op jit(solution)/shard_map/ppermute | solution.py:268
  5.4 8.4 %collective-permute-start.4 = (f32[64,512]{1,0:T(8,128)S(1)}, f32[64,512]{1,0:T(8,128)S(1)}, u32[]{:S(2)}, u32[]{:S(2)}) collective-permute-start(f32[64,512]{1,0:T(8,128)S(1)} %pad_maximum_fusion.3), channel_id=1, source_target_pairs={{0,1},{2,0},{4,2},{6,4},{7,6},{5,7},{3,5},{1,3},{8,10},{10,12},{12... | collective-permute-start | bytes 393224 | tf_op jit(solution)/shard_map/ppermute | solution.py:316
  6.9 6.8 %collective-permute-start.3 = (f32[64,512]{1,0:T(8,128)S(1)}, f32[64,512]{1,0:T(8,128)S(1)}, u32[]{:S(2)}, u32[]{:S(2)}) collective-permute-start(f32[64,512]{1,0:T(8,128)S(1)} %pad_maximum_fusion.3), channel_id=1, source_target_pairs={{0,2},{2,4},{4,6},{6,7},{7,5},{5,3},{3,1},{1,0},{8,9},{10,8},{12,1... | collective-permute-start | bytes 393224 | tf_op jit(solution)/shard_map/ppermute | solution.py:314
  7.4 2.8 %copy-start = (f32[1536,1024]{1,0:T(8,128)S(1)}, f32[1536,1024]{1,0:T(8,128)}, u32[]{:S(2)}) copy-start(f32[1536,1024]{1,0:T(8,128)} %refs_1_.7) | copy-start | bytes 18874372
  10.2 1.2 copy-start.1
  13.8 12.0 %collective-permute-start.6 = (f32[192,512]{1,0:T(8,128)S(1)}, f32[192,512]{1,0:T(8,128)S(1)}, u32[]{:S(2)}, u32[]{:S(2)}) collective-permute-start(f32[192,512]{1,0:T(8,128)S(1)} %get-tuple-element.121), channel_id=1, source_target_pairs={{0,1},{2,0},{4,2},{6,4},{7,6},{5,7},{3,5},{1,3},{8,10},{10,12},{12... | collective-permute-start | bytes 1179656 | tf_op jit(solution)/shard_map/ppermute | solution.py:296
  15.3 10.5 %collective-permute-start.5 = (f32[192,512]{1,0:T(8,128)S(1)}, f32[192,512]{1,0:T(8,128)S(1)}, u32[]{:S(2)}, u32[]{:S(2)}) collective-permute-start(f32[192,512]{1,0:T(8,128)S(1)} %get-tuple-element.122), channel_id=1, source_target_pairs={{0,2},{2,4},{4,6},{6,7},{7,5},{5,3},{3,1},{1,0},{8,9},{10,8},{12,1... | collective-permute-start | bytes 1179656 | tf_op jit(solution)/shard_map/ppermute | solution.py:296
  21.0 6.3 %collective-permute-start.7 = (f32[64,512]{1,0:T(8,128)S(1)}, f32[64,512]{1,0:T(8,128)S(1)}, u32[]{:S(2)}, u32[]{:S(2)}) collective-permute-start(f32[64,512]{1,0:T(8,128)S(1)} %collective-permute-done.3), channel_id=1, source_target_pairs={{0,2},{2,4},{4,6},{6,7},{7,5},{5,3},{3,1},{1,0},{8,9},{10,8},{12,1... | collective-permute-start | bytes 393224 | tf_op jit(solution)/shard_map/ppermute | solution.py:314
  22.6 6.0 %collective-permute-start.8 = (f32[64,512]{1,0:T(8,128)S(1)}, f32[64,512]{1,0:T(8,128)S(1)}, u32[]{:S(2)}, u32[]{:S(2)}) collective-permute-start(f32[64,512]{1,0:T(8,128)S(1)} %collective-permute-done.4), channel_id=1, source_target_pairs={{0,1},{2,0},{4,2},{6,4},{7,6},{5,7},{3,5},{1,3},{8,10},{10,12},{12... | collective-permute-start | bytes 393224 | tf_op jit(solution)/shard_map/ppermute | solution.py:316
  28.6 2.7 %collective-permute-start.9 = (f32[1024,256]{1,0:T(8,128)S(1)}, f32[1024,256]{1,0:T(8,128)S(1)}, u32[]{:S(2)}, u32[]{:S(2)}) collective-permute-start(f32[1024,256]{1,0:T(8,128)S(1)} %collective-permute-done.refs_2_), channel_id=1, source_target_pairs={{0,8},{8,0},{16,24},{24,16},{1,9},{9,1},{17,25},{25,17},{2,10},{10... | collective-permute-start | bytes 3145736 | tf_op jit(solution)/shard_map/ppermute | solution.py:268
  28.7 8.7 %collective-permute-start.21 = (f32[192,512]{1,0:T(8,128)S(1)}, f32[192,512]{1,0:T(8,128)S(1)}, u32[]{:S(2)}, u32[]{:S(2)}) collective-permute-start(f32[192,512]{1,0:T(8,128)S(1)} %get-tuple-element.79), channel_id=1, source_target_pairs={{0,2},{2,4},{4,6},{6,7},{7,5},{5,3},{3,1},{1,0},{8,9},{10,8},{12,1... | collective-permute-start | bytes 1179656 | tf_op jit(solution)/shard_map/ppermute | solution.py:296
  33.6 16.9 %collective-permute-start.11 = (f32[192,512]{1,0:T(8,128)S(1)}, f32[192,512]{1,0:T(8,128)S(1)}, u32[]{:S(2)}, u32[]{:S(2)}) collective-permute-start(f32[192,512]{1,0:T(8,128)S(1)} %get-tuple-element.119), channel_id=1, source_target_pairs={{0,1},{2,0},{4,2},{6,4},{7,6},{5,7},{3,5},{1,3},{8,10},{10,12},{12... | collective-permute-start | bytes 1179656 | tf_op jit(solution)/shard_map/ppermute | solution.py:296
  34.1 16.9 %collective-permute-start.10 = (f32[192,512]{1,0:T(8,128)S(1)}, f32[192,512]{1,0:T(8,128)S(1)}, u32[]{:S(2)}, u32[]{:S(2)}) collective-permute-start(f32[192,512]{1,0:T(8,128)S(1)} %get-tuple-element.120), channel_id=1, source_target_pairs={{0,2},{2,4},{4,6},{6,7},{7,5},{5,3},{3,1},{1,0},{8,9},{10,8},{12,1... | collective-permute-start | bytes 1179656 | tf_op jit(solution)/shard_map/ppermute | solution.py:296
  35.7 17.0 %collective-permute-start.12 = (f32[5,64,512]{2,1,0:T(8,128)S(1)}, f32[5,64,512]{2,1,0:T(8,128)S(1)}, u32[]{:S(2)}, u32[]{:S(2)}) collective-permute-start(f32[5,64,512]{2,1,0:T(8,128)S(1)} %bitcast_dynamic-update-slice_fusion), channel_id=1, source_target_pairs={{0,16},{8,24},{16,0},{24,8},{1,17},{9,25},{17,1},{25,9},{2,18},{10... | collective-permute-start | bytes 1966088 | tf_op jit(solution)/shard_map/ppermute | solution.py:268
  36.2 26.2 %collective-permute-start.24 = (f32[192,512]{1,0:T(8,128)S(1)}, f32[192,512]{1,0:T(8,128)S(1)}, u32[]{:S(2)}, u32[]{:S(2)}) collective-permute-start(f32[192,512]{1,0:T(8,128)S(1)} %get-tuple-element.80), channel_id=1, source_target_pairs={{0,1},{2,0},{4,2},{6,4},{7,6},{5,7},{3,5},{1,3},{8,10},{10,12},{12... | collective-permute-start | bytes 1179656 | tf_op jit(solution)/shard_map/ppermute | solution.py:296
  37.4 11.6 %collective-permute-start.15 = (f32[64,512]{1,0:T(8,128)S(1)}, f32[64,512]{1,0:T(8,128)S(1)}, u32[]{:S(2)}, u32[]{:S(2)}) collective-permute-start(f32[64,512]{1,0:T(8,128)S(1)} %collective-permute-done.7), channel_id=1, source_target_pairs={{0,2},{2,4},{4,6},{6,7},{7,5},{5,3},{3,1},{1,0},{8,9},{10,8},{12,1... | collective-permute-start | bytes 393224 | tf_op jit(solution)/shard_map/ppermute | solution.py:314
  49.0 13.5 %collective-permute-start.22 = (f32[192,512]{1,0:T(8,128)S(1)}, f32[192,512]{1,0:T(8,128)S(1)}, u32[]{:S(2)}, u32[]{:S(2)}) collective-permute-start(f32[192,512]{1,0:T(8,128)S(1)} %slice_add_fusion.8), channel_id=1, source_target_pairs={{0,2},{2,4},{4,6},{6,7},{7,5},{5,3},{3,1},{1,0},{8,9},{10,8},{12,1... | collective-permute-start | bytes 1179656 | tf_op jit(solution)/shard_map/ppermute | solution.py:296
  50.5 6.4 %collective-permute-start.17 = (f32[64,512]{1,0:T(8,128)S(1)}, f32[64,512]{1,0:T(8,128)S(1)}, u32[]{:S(2)}, u32[]{:S(2)}) collective-permute-start(f32[64,512]{1,0:T(8,128)S(1)} %collective-permute-done.8), channel_id=1, source_target_pairs={{0,1},{2,0},{4,2},{6,4},{7,6},{5,7},{3,5},{1,3},{8,10},{10,12},{12... | collective-permute-start | bytes 393224 | tf_op jit(solution)/shard_map/ppermute | solution.py:316
  51.0 10.0 %collective-permute-start.16 = (f32[64,512]{1,0:T(8,128)S(1)}, f32[64,512]{1,0:T(8,128)S(1)}, u32[]{:S(2)}, u32[]{:S(2)}) collective-permute-start(f32[64,512]{1,0:T(8,128)S(1)} %collective-permute-done.15), channel_id=1, source_target_pairs={{0,2},{2,4},{4,6},{6,7},{7,5},{5,3},{3,1},{1,0},{8,9},{10,8},{12,1... | collective-permute-start | bytes 393224 | tf_op jit(solution)/shard_map/ppermute | solution.py:314
  52.7 16.7 %collective-permute-start.13 = (f32[192,512]{1,0:T(8,128)S(1)}, f32[192,512]{1,0:T(8,128)S(1)}, u32[]{:S(2)}, u32[]{:S(2)}) collective-permute-start(f32[192,512]{1,0:T(8,128)S(1)} %get-tuple-element.72), channel_id=1, source_target_pairs={{0,2},{2,4},{4,6},{6,7},{7,5},{5,3},{3,1},{1,0},{8,9},{10,8},{12,1... | collective-permute-start | bytes 1179656 | tf_op jit(solution)/shard_map/ppermute | solution.py:296
  57.0 12.4 %collective-permute-start.14 = (f32[192,512]{1,0:T(8,128)S(1)}, f32[192,512]{1,0:T(8,128)S(1)}, u32[]{:S(2)}, u32[]{:S(2)}) collective-permute-start(f32[192,512]{1,0:T(8,128)S(1)} %get-tuple-element.73), channel_id=1, source_target_pairs={{0,1},{2,0},{4,2},{6,4},{7,6},{5,7},{3,5},{1,3},{8,10},{10,12},{12... | collective-permute-start | bytes 1179656 | tf_op jit(solution)/shard_map/ppermute | solution.py:296
  61.0 8.8 %collective-permute-start.18 = (f32[3,64,512]{2,1,0:T(8,128)S(1)}, f32[3,64,512]{2,1,0:T(8,128)S(1)}, u32[]{:S(2)}, u32[]{:S(2)}) collective-permute-start(f32[3,64,512]{2,1,0:T(8,128)S(1)} %pad_maximum_fusion.2), channel_id=1, source_target_pairs={{0,16},{8,24},{16,0},{24,8},{1,17},{9,25},{17,1},{25,9},{2,18},{10... | collective-permute-start | bytes 1179656 | tf_op jit(solution)/shard_map/ppermute | solution.py:268
  62.6 14.9 %collective-permute-start.25 = (f32[192,512]{1,0:T(8,128)S(1)}, f32[192,512]{1,0:T(8,128)S(1)}, u32[]{:S(2)}, u32[]{:S(2)}) collective-permute-start(f32[192,512]{1,0:T(8,128)S(1)} %get-tuple-element.111), channel_id=1, source_target_pairs={{0,1},{2,0},{4,2},{6,4},{7,6},{5,7},{3,5},{1,3},{8,10},{10,12},{12... | collective-permute-start | bytes 1179656 | tf_op jit(solution)/shard_map/ppermute | solution.py:296
  65.4 12.0 %collective-permute-start.23 = (f32[192,512]{1,0:T(8,128)S(1)}, f32[192,512]{1,0:T(8,128)S(1)}, u32[]{:S(2)}, u32[]{:S(2)}) collective-permute-start(f32[192,512]{1,0:T(8,128)S(1)} %get-tuple-element.112), channel_id=1, source_target_pairs={{0,2},{2,4},{4,6},{6,7},{7,5},{5,3},{3,1},{1,0},{8,9},{10,8},{12,1... | collective-permute-start | bytes 1179656 | tf_op jit(solution)/shard_map/ppermute | solution.py:342
  69.8 10.0 %collective-permute-start.19 = (f32[192,512]{1,0:T(8,128)S(1)}, f32[192,512]{1,0:T(8,128)S(1)}, u32[]{:S(2)}, u32[]{:S(2)}) collective-permute-start(f32[192,512]{1,0:T(8,128)S(1)} %get-tuple-element.78), channel_id=1, source_target_pairs={{0,2},{2,4},{4,6},{6,7},{7,5},{5,3},{3,1},{1,0},{8,9},{10,8},{12,1... | collective-permute-start | bytes 1179656 | tf_op jit(solution)/shard_map/ppermute | solution.py:296
  77.5 4.7 %collective-permute-start.26 = (f32[192,512]{1,0:T(8,128)S(1)}, f32[192,512]{1,0:T(8,128)S(1)}, u32[]{:S(2)}, u32[]{:S(2)}) collective-permute-start(f32[192,512]{1,0:T(8,128)S(1)} %add_add_fusion.refs_0_), channel_id=1, source_target_pairs={{0,8},{8,0},{16,24},{24,16},{1,9},{9,1},{17,25},{25,17},{2,10},{10... | collective-permute-start | bytes 1179656 | tf_op jit(solution)/shard_map/ppermute | solution.py:268
  79.9 11.3 %collective-permute-start.20 = (f32[192,512]{1,0:T(8,128)S(1)}, f32[192,512]{1,0:T(8,128)S(1)}, u32[]{:S(2)}, u32[]{:S(2)}) collective-permute-start(f32[192,512]{1,0:T(8,128)S(1)} %slice_add_fusion.1), channel_id=1, source_target_pairs={{0,2},{2,4},{4,6},{6,7},{7,5},{5,3},{3,1},{1,0},{8,9},{10,8},{12,1... | collective-permute-start | bytes 1179656 | tf_op jit(solution)/shard_map/ppermute | solution.py:366
  81.5 9.6 %collective-permute-start.27 = (f32[192,512]{1,0:T(8,128)S(1)}, f32[192,512]{1,0:T(8,128)S(1)}, u32[]{:S(2)}, u32[]{:S(2)}) collective-permute-start(f32[192,512]{1,0:T(8,128)S(1)} %get-tuple-element.96), channel_id=1, source_target_pairs={{0,1},{2,0},{4,2},{6,4},{7,6},{5,7},{3,5},{1,3},{8,10},{10,12},{12... | collective-permute-start | bytes 1179656 | tf_op jit(solution)/shard_map/ppermute | solution.py:296
  91.3 1.8 %collective-permute-start.28 = (f32[192,512]{1,0:T(8,128)S(1)}, f32[192,512]{1,0:T(8,128)S(1)}, u32[]{:S(2)}, u32[]{:S(2)}) collective-permute-start(f32[192,512]{1,0:T(8,128)S(1)} %fusion.refs_5_), channel_id=1, source_target_pairs={{0,8},{8,0},{16,24},{24,16},{1,9},{9,1},{17,25},{25,17},{2,10},{10... | collective-permute-start | bytes 1179656 | tf_op jit(solution)/shard_map/ppermute | solution.py:268
  96.1 9.2 %collective-permute-start.29 = (f32[256,256]{1,0:T(8,128)S(1)}, f32[256,256]{1,0:T(8,128)S(1)}, u32[]{:S(2)}, u32[]{:S(2)}) collective-permute-start(f32[256,256]{1,0:T(8,128)S(1)} %get-tuple-element.102), channel_id=1, source_target_pairs={{0,16},{8,24},{16,0},{24,8},{1,17},{9,25},{17,1},{25,9},{2,18},{10... | collective-permute-start | bytes 786440 | tf_op jit(solution)/shard_map/ppermute | solution.py:268
  96.7 9.3 %collective-permute-start.31 = (f32[128,512]{1,0:T(8,128)S(1)}, f32[128,512]{1,0:T(8,128)S(1)}, u32[]{:S(2)}, u32[]{:S(2)}) collective-permute-start(f32[128,512]{1,0:T(8,128)S(1)} %get-tuple-element.104), channel_id=1, source_target_pairs={{0,1},{1,0},{2,3},{3,2},{4,5},{5,4},{6,7},{7,6},{8,9},{9,8},{10,11... | collective-permute-start | bytes 786440 | tf_op jit(solution)/shard_map/ppermute | solution.py:271
  97.9 13.1 %collective-permute-start.36 = (f32[256,256]{1,0:T(8,128)S(1)}, f32[256,256]{1,0:T(8,128)S(1)}, u32[]{:S(2)}, u32[]{:S(2)}) collective-permute-start(f32[256,256]{1,0:T(8,128)S(1)} %get-tuple-element.106), channel_id=1, source_target_pairs={{0,16},{8,24},{16,0},{24,8},{1,17},{9,25},{17,1},{25,9},{2,18},{10... | collective-permute-start | bytes 786440 | tf_op jit(solution)/shard_map/ppermute | solution.py:268
  98.8 12.9 %collective-permute-start.38 = (f32[128,512]{1,0:T(8,128)S(1)}, f32[128,512]{1,0:T(8,128)S(1)}, u32[]{:S(2)}, u32[]{:S(2)}) collective-permute-start(f32[128,512]{1,0:T(8,128)S(1)} %get-tuple-element.108), channel_id=1, source_target_pairs={{0,1},{1,0},{2,3},{3,2},{4,5},{5,4},{6,7},{7,6},{8,9},{9,8},{10,11... | collective-permute-start | bytes 786440 | tf_op jit(solution)/shard_map/ppermute | solution.py:271
  105.4 8.7 %collective-permute-start.30 = (f32[128,256]{1,0:T(8,128)S(1)}, f32[128,256]{1,0:T(8,128)S(1)}, u32[]{:S(2)}, u32[]{:S(2)}) collective-permute-start(f32[128,256]{1,0:T(8,128)S(1)} %slice.135), channel_id=1, source_target_pairs={{0,1},{1,0},{2,3},{3,2},{4,5},{5,4},{6,7},{7,6},{8,9},{9,8},{10,11... | collective-permute-start | bytes 393224 | tf_op jit(solution)/shard_map/ppermute | solution.py:271
  106.1 8.1 %collective-permute-start.32 = (f32[128,256]{1,0:T(8,128)S(1)}, f32[128,256]{1,0:T(8,128)S(1)}, u32[]{:S(2)}, u32[]{:S(2)}) collective-permute-start(f32[128,256]{1,0:T(8,128)S(1)} %slice.137), channel_id=1, source_target_pairs={{0,16},{8,24},{16,0},{24,8},{1,17},{9,25},{17,1},{25,9},{2,18},{10... | collective-permute-start | bytes 393224 | tf_op jit(solution)/shard_map/ppermute | solution.py:268
  111.0 7.6 %collective-permute-start.37 = (f32[128,256]{1,0:T(8,128)S(1)}, f32[128,256]{1,0:T(8,128)S(1)}, u32[]{:S(2)}, u32[]{:S(2)}) collective-permute-start(f32[128,256]{1,0:T(8,128)S(1)} %slice.145), channel_id=1, source_target_pairs={{0,1},{1,0},{2,3},{3,2},{4,5},{5,4},{6,7},{7,6},{8,9},{9,8},{10,11... | collective-permute-start | bytes 393224 | tf_op jit(solution)/shard_map/ppermute | solution.py:271
  111.7 7.0 %collective-permute-start.39 = (f32[128,256]{1,0:T(8,128)S(1)}, f32[128,256]{1,0:T(8,128)S(1)}, u32[]{:S(2)}, u32[]{:S(2)}) collective-permute-start(f32[128,256]{1,0:T(8,128)S(1)} %slice.147), channel_id=1, source_target_pairs={{0,16},{8,24},{16,0},{24,8},{1,17},{9,25},{17,1},{25,9},{2,18},{10... | collective-permute-start | bytes 393224 | tf_op jit(solution)/shard_map/ppermute | solution.py:268
  114.2 8.1 %collective-permute-start.35 = (f32[32,512]{1,0:T(8,128)S(1)}, f32[32,512]{1,0:T(8,128)S(1)}, u32[]{:S(2)}, u32[]{:S(2)}) collective-permute-start(f32[32,512]{1,0:T(8,128)S(1)} %get-tuple-element.127), channel_id=1, source_target_pairs={{0,6},{1,7},{2,4},{3,5},{4,2},{5,3},{6,0},{7,1},{8,14},{9,15},{10,... | collective-permute-start | bytes 196616 | tf_op jit(solution)/shard_map/ppermute | solution.py:271
  117.7 6.3 %collective-permute-start.33 = (f32[32,512]{1,0:T(8,128)S(1)}, f32[32,512]{1,0:T(8,128)S(1)}, u32[]{:S(2)}, u32[]{:S(2)}) collective-permute-start(f32[32,512]{1,0:T(8,128)S(1)} %get-tuple-element.129), channel_id=1, source_target_pairs={{0,2},{1,3},{2,0},{3,1},{4,6},{5,7},{6,4},{7,5},{8,10},{9,11},{10,... | collective-permute-start | bytes 196616 | tf_op jit(solution)/shard_map/ppermute | solution.py:271
  117.8 8.3 %collective-permute-start.34 = (f32[32,512]{1,0:T(8,128)S(1)}, f32[32,512]{1,0:T(8,128)S(1)}, u32[]{:S(2)}, u32[]{:S(2)}) collective-permute-start(f32[32,512]{1,0:T(8,128)S(1)} %get-tuple-element.130), channel_id=1, source_target_pairs={{0,4},{1,5},{2,6},{3,7},{4,0},{5,1},{6,2},{7,3},{8,12},{9,13},{10,... | collective-permute-start | bytes 196616 | tf_op jit(solution)/shard_map/ppermute | solution.py:271
  118.8 7.3 %collective-permute-start.42 = (f32[32,512]{1,0:T(8,128)S(1)}, f32[32,512]{1,0:T(8,128)S(1)}, u32[]{:S(2)}, u32[]{:S(2)}) collective-permute-start(f32[32,512]{1,0:T(8,128)S(1)} %get-tuple-element.123), channel_id=1, source_target_pairs={{0,6},{1,7},{2,4},{3,5},{4,2},{5,3},{6,0},{7,1},{8,14},{9,15},{10,... | collective-permute-start | bytes 196616 | tf_op jit(solution)/shard_map/ppermute | solution.py:271
  122.3 5.0 %collective-permute-start.40 = (f32[32,512]{1,0:T(8,128)S(1)}, f32[32,512]{1,0:T(8,128)S(1)}, u32[]{:S(2)}, u32[]{:S(2)}) collective-permute-start(f32[32,512]{1,0:T(8,128)S(1)} %get-tuple-element.125), channel_id=1, source_target_pairs={{0,2},{1,3},{2,0},{3,1},{4,6},{5,7},{6,4},{7,5},{8,10},{9,11},{10,... | collective-permute-start | bytes 196616 | tf_op jit(solution)/shard_map/ppermute | solution.py:271
  122.3 5.7 %collective-permute-start.41 = (f32[32,512]{1,0:T(8,128)S(1)}, f32[32,512]{1,0:T(8,128)S(1)}, u32[]{:S(2)}, u32[]{:S(2)}) collective-permute-start(f32[32,512]{1,0:T(8,128)S(1)} %get-tuple-element.126), channel_id=1, source_target_pairs={{0,4},{1,5},{2,6},{3,7},{4,0},{5,1},{6,2},{7,3},{8,12},{9,13},{10,... | collective-permute-start | bytes 196616 | tf_op jit(solution)/shard_map/ppermute | solution.py:271
  128.6 1.3 %collective-permute-start.43 = (f32[64,256]{1,0:T(8,128)S(1)}, f32[64,256]{1,0:T(8,128)S(1)}, u32[]{:S(2)}, u32[]{:S(2)}) collective-permute-start(f32[64,256]{1,0:T(8,128)S(1)} %get-tuple-element.110), channel_id=1, source_target_pairs={{0,8},{8,0},{16,24},{24,16},{1,9},{9,1},{17,25},{25,17},{2,10},{10... | collective-permute-start | bytes 196616 | tf_op jit(solution)/shard_map/ppermute | solution.py:268

commit v6 on v5

--- a/solution.py
+++ b/solution.py
@@ -109,7 +109,20 @@
             flops=cost * 2 * height * together * steps * depth * width,
         )[0]
 
-    return part(0, 1), part(1, pieces // together - 1)
+    if cost:
+        rows_of = [lax.dynamic_slice_in_dim(samples, table[k] * height, height, 0) for k in range(together)]
+        first = call(
+            functools.partial(partial_kernel, core_at, together),
+            [f32(height * together, width)],
+            table,
+            *rows_of,
+            *blocks,
+            scratch_shapes=[pltpu.VMEM((depth, width), jnp.bfloat16)] * 2,
+            flops=cost * 2 * height * together * depth * width,
+        )[0]
+    else:
+        first = part(0, 1)
+    return first, part(1, pieces // together - 1)
 
 
 def near_kernel(order_at, table, *refs):
@@ -319,8 +332,6 @@
                     groups.append(jnp.stack([line[away] for away in held_order[done : len(line)]]))
 
         pass_components(1, 2)
-        first_near, line = lax.optimization_barrier((near_part[0], line))
-        near_part = (first_near, near_part[1])
         near = rounds(near_part, 0, 1, [None, None])
         later_near, line = lax.optimization_barrier((near_part[1], line))
         near_part = (near_part[0], later_near)

time: 131 us -> 131 us (level)
    unnamed x9 -> x11, local copies, waits for them, and re-layouts: 5.05 us -> 1.06 us
    dynamic_slice x0 -> x2, local copies, waits for them, and re-layouts: none -> 2.38 us  [the longest x1 1.69 us: partial_sums(): lax.dynamic_slice_in_dim(samples, table[k] * height, height, 0)]
  transfers between devices with their start and end apart: 44 -> 44, of which waited for: 22 -> 21; matrix products, arithmetic and copies ran while one was open for 2% -> 5% of each run, Pallas kernels for 14% -> 14%
where the time goes in v6:
time: 131 us
  waiting for transfers between devices  53.1 us (41%)
  starting transfers between devices  46.8 us (36%)
  Pallas kernels  23.2 us (18%)
  local copies, waits for them, and re-layouts  4.91 us (4%)
  between operations  1.62 us (1%)
  other arithmetic  1.39 us (1%)
    pallas_call x9, Pallas kernels, call(): pl.pallas_call(kernel, out_shape=outs, grid_spec=pltpu.PrefetchScalarGrid...  23.2 us
    ppermute x12, starting transfers between devices, rounds(): held[s] = lax.ppermute(held[s], both, streams[s]) + piece  15.9 us
    ppermute x12, waiting for transfers between devices, rounds(): held[s] = lax.ppermute(held[s], both, streams[s]) + piece  14.8 us
    ppermute x10, starting transfers between devices, swap_feat(): return lax.ppermute(a, 'feat', [(i, i ^ bit) for i in range(n_feat)])  13.2 us
    ppermute x4, waiting for transfers between devices, pass_components(): line[step] = lax.ppermute(line[step - 1], both, streams[0])  10.9 us
    ppermute x13, waiting for transfers between devices, swap(): return lax.ppermute(a, 'rows', [(i, i ^ bit) for i in range(n_rows)])  10.7 us
    ppermute x13, starting transfers between devices, swap(): return lax.ppermute(a, 'rows', [(i, i ^ bit) for i in range(n_rows)])  9.29 us
    ppermute x1, waiting for transfers between devices, on_device(): arrived = lax.ppermute(held[0], both, streams[0])  7.34 us
  transfers between devices with their start and end apart: 44, of which 21 were waited for; matrix products, arithmetic and copies ran while one was open for 5% of the time, Pallas kernels for 14%

profile of v6, /device:TPU:0, one launch (start us, length us, event | category | flops | bytes accessed | tf_op | source)
XLA Modules:
  0.0 131.1 jit_solution(2766065069697079620)
XLA Ops:
  0.5 2.6 %collective-permute-start = (f32[1024,256]{1,0:T(8,128)}, f32[1024,256]{1,0:T(8,128)S(1)}, u32[]{:S(2)}, u32[]{:S(2)}) collective-permute-start(f32[1024,256]{1,0:T(8,128)} %refs_2_.3), channel_id=1, source_target_pairs={{0,16},{8,24},{16,0},{24,8},{1,17},{9,25},{17,1},{25,9},{2,18},{10... | collective-permute-start | bytes 3145736 | tf_op jit(solution)/shard_map/ppermute | solution.py:281
  3.0 1.0 copy.7
  6.8 1.7 %constant_dynamic-slice_fusion = (f32[192,1024]{1,0:T(8,128)S(1)}, f32[192,1024]{1,0:T(8,128)S(1)}) fusion(f32[1536,1024]{1,0:T(8,128)} %refs_1_.5, s32[]{:T(128)S(6)} %select_n.40, s32[]{:T(128)S(6)} %select_n.39), kind=kLoop, calls=%fused_computation.49 | loop fusion | bytes 3145736 | tf_op jit(solution)/shard_map/dynamic_slice | solution.py:113
  9.3 1.5 %collective-permute-start.5 = (f32[64,512]{1,0:T(8,128)S(1)}, f32[64,512]{1,0:T(8,128)S(1)}, u32[]{:S(2)}, u32[]{:S(2)}) collective-permute-start(f32[64,512]{1,0:T(8,128)S(1)} %pad_maximum_fusion.3), channel_id=1, source_target_pairs={{0,1},{2,0},{4,2},{6,4},{7,6},{5,7},{3,5},{1,3},{8,10},{10,12},{12... | collective-permute-start | bytes 393224 | tf_op jit(solution)/shard_map/ppermute | solution.py:329
  11.4 2.2 %shard_map.46 = f32[384,512]{1,0:T(8,128)S(1)} custom-call(s32[17]{0:T(128)S(1)} %fusion.10.table, f32[192,1024]{1,0:T(8,128)S(1)} %get-tuple-element.104.refs_0_, f32[192,1024]{1,0:T(8,128)S(1)} %get-tuple-element.103.refs_1_, f32[1024,256]{1,0:T(8,128)S(1)} %copy-done, f32[1024,256]{1,0:T(8,128)S(1)} %collective-permute-done.1.refs_3_), custom_call_target="tpu_custom_call" | custom-call | flops 16106127360 | bytes 3670016 | tf_op jit(solution)/shard_map/pallas_call | solution.py:50
  13.6 1.5 %collective-permute-start.6 = (f32[192,512]{1,0:T(8,128)S(1)}, f32[192,512]{1,0:T(8,128)S(1)}, u32[]{:S(2)}, u32[]{:S(2)}) collective-permute-start(f32[192,512]{1,0:T(8,128)S(1)} %get-tuple-element.115), channel_id=1, source_target_pairs={{0,1},{2,0},{4,2},{6,4},{7,6},{5,7},{3,5},{1,3},{8,10},{10,12},{12... | collective-permute-start | bytes 1179656 | tf_op jit(solution)/shard_map/ppermute | solution.py:309
  15.7 5.1 %shard_map.47 = f32[1152,512]{1,0:T(8,128)S(1)} custom-call(s32[17]{0:T(128)S(1)} %fusion.10.table, f32[1536,1024]{1,0:T(8,128)S(1)} %bitcast.26, f32[1536,1024]{1,0:T(8,128)S(1)} %bitcast.26, f32[1024,256]{1,0:T(8,128)S(1)} %copy-done, f32[1024,256]{1,0:T(8,128)S(1)} %collective-permute-done.1.refs_3_), custom_call_target="tpu_custom_call" | custom-call | flops 48318382080 | bytes 14680064 | tf_op jit(solution)/shard_map/pallas_call | solution.py:50
  20.9 1.6 %collective-permute-start.7 = (f32[64,512]{1,0:T(8,128)S(1)}, f32[64,512]{1,0:T(8,128)S(1)}, u32[]{:S(2)}, u32[]{:S(2)}) collective-permute-start(f32[64,512]{1,0:T(8,128)S(1)} %collective-permute-done.4), channel_id=1, source_target_pairs={{0,2},{2,4},{4,6},{6,7},{7,5},{5,3},{3,1},{1,0},{8,9},{10,8},{12,1... | collective-permute-start | bytes 393224 | tf_op jit(solution)/shard_map/ppermute | solution.py:327
  22.9 2.6 %collective-permute-done.6 = f32[192,512]{1,0:T(8,128)S(1)} collective-permute-done((f32[192,512]{1,0:T(8,128)S(1)}, f32[192,512]{1,0:T(8,128)S(1)}, u32[]{:S(2)}, u32[]{:S(2)}) %collective-permute-start.6) | collective-permute-done | bytes 393248 | tf_op jit(solution)/shard_map/ppermute | solution.py:309
  25.7 1.6 %collective-permute-done.7 = f32[64,512]{1,0:T(8,128)S(1)} collective-permute-done((f32[64,512]{1,0:T(8,128)S(1)}, f32[64,512]{1,0:T(8,128)S(1)}, u32[]{:S(2)}, u32[]{:S(2)}) %collective-permute-start.7) | collective-permute-done | bytes 131104 | tf_op jit(solution)/shard_map/ppermute | solution.py:327
  27.3 1.2 collective-permute-done.8
  28.6 1.6 %collective-permute-start.21 = (f32[192,512]{1,0:T(8,128)S(1)}, f32[192,512]{1,0:T(8,128)S(1)}, u32[]{:S(2)}, u32[]{:S(2)}) collective-permute-start(f32[192,512]{1,0:T(8,128)S(1)} %get-tuple-element.71), channel_id=1, source_target_pairs={{0,2},{2,4},{4,6},{6,7},{7,5},{5,3},{3,1},{1,0},{8,9},{10,8},{12,1... | collective-permute-start | bytes 1179656 | tf_op jit(solution)/shard_map/ppermute | solution.py:309
  31.2 2.3 %shard_map.48 = f32[384,512]{1,0:T(8,128)S(1)} custom-call(s32[17]{0:T(128)S(1)} %fusion.10.table, f32[1536,1024]{1,0:T(8,128)S(1)} %bitcast.26, f32[1536,1024]{1,0:T(8,128)S(1)} %bitcast.26, f32[1024,256]{1,0:T(8,128)S(1)} %collective-permute-done.refs_2_, f32[1024,256]{1,0:T(8,128)S(1)} %collective-permute-done.9.refs_3_), custom_call_target="tpu_custom_call" | custom-call | bytes 14680064 | tf_op jit(solution)/shard_map/pallas_call | solution.py:50
  34.1 1.5 %collective-permute-start.10 = (f32[192,512]{1,0:T(8,128)S(1)}, f32[192,512]{1,0:T(8,128)S(1)}, u32[]{:S(2)}, u32[]{:S(2)}) collective-permute-start(f32[192,512]{1,0:T(8,128)S(1)} %get-tuple-element.114), channel_id=1, source_target_pairs={{0,2},{2,4},{4,6},{6,7},{7,5},{5,3},{3,1},{1,0},{8,9},{10,8},{12,1... | collective-permute-start | bytes 1179656 | tf_op jit(solution)/shard_map/ppermute | solution.py:309
  35.9 1.5 %collective-permute-start.24 = (f32[192,512]{1,0:T(8,128)S(1)}, f32[192,512]{1,0:T(8,128)S(1)}, u32[]{:S(2)}, u32[]{:S(2)}) collective-permute-start(f32[192,512]{1,0:T(8,128)S(1)} %get-tuple-element.72), channel_id=1, source_target_pairs={{0,1},{2,0},{4,2},{6,4},{7,6},{5,7},{3,5},{1,3},{8,10},{10,12},{12... | collective-permute-start | bytes 1179656 | tf_op jit(solution)/shard_map/ppermute | solution.py:309
  38.1 5.1 %shard_map.49 = f32[1152,512]{1,0:T(8,128)S(1)} custom-call(s32[17]{0:T(128)S(1)} %fusion.10.table, f32[1536,1024]{1,0:T(8,128)S(1)} %bitcast.26, f32[1536,1024]{1,0:T(8,128)S(1)} %bitcast.26, f32[1024,256]{1,0:T(8,128)S(1)} %collective-permute-done.refs_2_, f32[1024,256]{1,0:T(8,128)S(1)} %collective-permute-done.9.refs_3_), custom_call_target="tpu_custom_call" | custom-call | bytes 14680064 | tf_op jit(solution)/shard_map/pallas_call | solution.py:50
  43.2 5.7 %collective-permute-done.15 = f32[64,512]{1,0:T(8,128)S(1)} collective-permute-done((f32[64,512]{1,0:T(8,128)S(1)}, f32[64,512]{1,0:T(8,128)S(1)}, u32[]{:S(2)}, u32[]{:S(2)}) %collective-permute-start.15) | collective-permute-done | bytes 131104 | tf_op jit(solution)/shard_map/ppermute | solution.py:327
  48.9 1.4 %collective-permute-start.22 = (f32[192,512]{1,0:T(8,128)S(1)}, f32[192,512]{1,0:T(8,128)S(1)}, u32[]{:S(2)}, u32[]{:S(2)}) collective-permute-start(f32[192,512]{1,0:T(8,128)S(1)} %slice_add_fusion.8), channel_id=1, source_target_pairs={{0,2},{2,4},{4,6},{6,7},{7,5},{5,3},{3,1},{1,0},{8,9},{10,8},{12,1... | collective-permute-start | bytes 1179656 | tf_op jit(solution)/shard_map/ppermute | solution.py:309
  51.0 1.4 %collective-permute-start.16 = (f32[64,512]{1,0:T(8,128)S(1)}, f32[64,512]{1,0:T(8,128)S(1)}, u32[]{:S(2)}, u32[]{:S(2)}) collective-permute-start(f32[64,512]{1,0:T(8,128)S(1)} %collective-permute-done.15), channel_id=1, source_target_pairs={{0,2},{2,4},{4,6},{6,7},{7,5},{5,3},{3,1},{1,0},{8,9},{10,8},{12,1... | collective-permute-start | bytes 393224 | tf_op jit(solution)/shard_map/ppermute | solution.py:327
  52.6 1.6 %collective-permute-start.13 = (f32[192,512]{1,0:T(8,128)S(1)}, f32[192,512]{1,0:T(8,128)S(1)}, u32[]{:S(2)}, u32[]{:S(2)}) collective-permute-start(f32[192,512]{1,0:T(8,128)S(1)} %get-tuple-element.64), channel_id=1, source_target_pairs={{0,2},{2,4},{4,6},{6,7},{7,5},{5,3},{3,1},{1,0},{8,9},{10,8},{12,1... | collective-permute-start | bytes 1179656 | tf_op jit(solution)/shard_map/ppermute | solution.py:309
  54.2 2.6 %collective-permute-done.17 = f32[64,512]{1,0:T(8,128)S(1)} collective-permute-done((f32[64,512]{1,0:T(8,128)S(1)}, f32[64,512]{1,0:T(8,128)S(1)}, u32[]{:S(2)}, u32[]{:S(2)}) %collective-permute-start.17) | collective-permute-done | bytes 131104 | tf_op jit(solution)/shard_map/ppermute | solution.py:329
  57.4 3.5 %collective-permute-done.16 = f32[64,512]{1,0:T(8,128)S(1)} collective-permute-done((f32[64,512]{1,0:T(8,128)S(1)}, f32[64,512]{1,0:T(8,128)S(1)}, u32[]{:S(2)}, u32[]{:S(2)}) %collective-permute-start.16) | collective-permute-done | bytes 131104 | tf_op jit(solution)/shard_map/ppermute | solution.py:327
  61.0 1.4 %collective-permute-start.18 = (f32[3,64,512]{2,1,0:T(8,128)S(1)}, f32[3,64,512]{2,1,0:T(8,128)S(1)}, u32[]{:S(2)}, u32[]{:S(2)}) collective-permute-start(f32[3,64,512]{2,1,0:T(8,128)S(1)} %pad_maximum_fusion.2), channel_id=1, source_target_pairs={{0,16},{8,24},{16,0},{24,8},{1,17},{9,25},{17,1},{25,9},{2,18},{10... | collective-permute-start | bytes 1179656 | tf_op jit(solution)/shard_map/ppermute | solution.py:281
  62.5 2.9 %collective-permute-start.25 = (f32[192,512]{1,0:T(8,128)S(1)}, f32[192,512]{1,0:T(8,128)S(1)}, u32[]{:S(2)}, u32[]{:S(2)}) collective-permute-start(f32[192,512]{1,0:T(8,128)S(1)} %get-tuple-element.105), channel_id=1, source_target_pairs={{0,1},{2,0},{4,2},{6,4},{7,6},{5,7},{3,5},{1,3},{8,10},{10,12},{12... | collective-permute-start | bytes 1179656 | tf_op jit(solution)/shard_map/ppermute | solution.py:309
  65.4 3.9 %collective-permute-done.13 = f32[192,512]{1,0:T(8,128)S(1)} collective-permute-done((f32[192,512]{1,0:T(8,128)S(1)}, f32[192,512]{1,0:T(8,128)S(1)}, u32[]{:S(2)}, u32[]{:S(2)}) %collective-permute-start.13) | collective-permute-done | bytes 393248 | tf_op jit(solution)/shard_map/ppermute | solution.py:309
  69.7 1.6 %collective-permute-start.19 = (f32[192,512]{1,0:T(8,128)S(1)}, f32[192,512]{1,0:T(8,128)S(1)}, u32[]{:S(2)}, u32[]{:S(2)}) collective-permute-start(f32[192,512]{1,0:T(8,128)S(1)} %get-tuple-element.70), channel_id=1, source_target_pairs={{0,2},{2,4},{4,6},{6,7},{7,5},{5,3},{3,1},{1,0},{8,9},{10,8},{12,1... | collective-permute-start | bytes 1179656 | tf_op jit(solution)/shard_map/ppermute | solution.py:309
  71.3 6.0 %collective-permute-done.25 = f32[192,512]{1,0:T(8,128)S(1)} collective-permute-done((f32[192,512]{1,0:T(8,128)S(1)}, f32[192,512]{1,0:T(8,128)S(1)}, u32[]{:S(2)}, u32[]{:S(2)}) %collective-permute-start.25) | collective-permute-done | bytes 393248 | tf_op jit(solution)/shard_map/ppermute | solution.py:309
  77.5 2.2 %collective-permute-done.19 = f32[192,512]{1,0:T(8,128)S(1)} collective-permute-done((f32[192,512]{1,0:T(8,128)S(1)}, f32[192,512]{1,0:T(8,128)S(1)}, u32[]{:S(2)}, u32[]{:S(2)}) %collective-permute-start.19) | collective-permute-done | bytes 393248 | tf_op jit(solution)/shard_map/ppermute | solution.py:309
  79.7 1.7 %collective-permute-start.20 = (f32[192,512]{1,0:T(8,128)S(1)}, f32[192,512]{1,0:T(8,128)S(1)}, u32[]{:S(2)}, u32[]{:S(2)}) collective-permute-start(f32[192,512]{1,0:T(8,128)S(1)} %slice_add_fusion.1), channel_id=1, source_target_pairs={{0,2},{2,4},{4,6},{6,7},{7,5},{5,3},{3,1},{1,0},{8,9},{10,8},{12,1... | collective-permute-start | bytes 1179656 | tf_op jit(solution)/shard_map/ppermute | solution.py:377
  82.0 1.6 %shard_map.50 = (f32[512,384]{1,0:T(8,128)S(1)}, bf16[512,512]{1,0:T(8,128)(2,1)S(1)}, bf16[512,512]{1,0:T(8,128)(2,1)S(1)}, bf16[384,512]{1,0:T(8,128)(2,1)S(1)}, bf16[384,512]{1,0:T(8,128)(2,1)S(1)}) custom-call(s32[17]{0:T(128)S(1)} %fusion.10.table, f32[192,512]{1,0:T(8,128)S(1)} %add_add_fusion.refs_0_, f32[192,512]{1,0:T(8,128)S(1)} %collective-permute-done.26.refs_1_, ...), custom_call_target="tpu_custom_call" | custom-call | flops 603979776 | bytes 2883584 | tf_op jit(solution)/shard_map/pallas_call | solution.py:50
  83.7 7.3 %collective-permute-done.20 = f32[192,512]{1,0:T(8,128)S(1)} collective-permute-done((f32[192,512]{1,0:T(8,128)S(1)}, f32[192,512]{1,0:T(8,128)S(1)}, u32[]{:S(2)}, u32[]{:S(2)}) %collective-permute-start.20) | collective-permute-done | bytes 393248 | tf_op jit(solution)/shard_map/ppermute | solution.py:377
  91.2 1.7 %collective-permute-done.28.refs_6_ = f32[192,512]{1,0:T(8,128)S(1)} collective-permute-done((f32[192,512]{1,0:T(8,128)S(1)}, f32[192,512]{1,0:T(8,128)S(1)}, u32[]{:S(2)}, u32[]{:S(2)}) %collective-permute-start.28) | collective-permute-done | bytes 393248 | tf_op jit(solution)/shard_map/ppermute | solution.py:281
  92.9 3.1 %shard_map.51 = (f32[256,256]{1,0:T(8,128)S(1)}, f32[256,256]{1,0:T(8,128)S(1)}, f32[128,512]{1,0:T(8,128)S(1)}, f32[128,512]{1,0:T(8,128)S(1)}, bf16[512,384]{1...) custom-call(s32[17]{0:T(128)S(1)} %fusion.10.table, ...), custom_call_target="tpu_custom_call" | custom-call | flops 1207959552 | bytes 5242880 | tf_op jit(solution)/shard_map/pallas_call | solution.py:50
  96.6 1.3 %collective-permute-start.31 = (f32[128,512]{1,0:T(8,128)S(1)}, f32[128,512]{1,0:T(8,128)S(1)}, u32[]{:S(2)}, u32[]{:S(2)}) collective-permute-start(f32[128,512]{1,0:T(8,128)S(1)} %get-tuple-element.96), channel_id=1, source_target_pairs={{0,1},{1,0},{2,3},{3,2},{4,5},{5,4},{6,7},{7,6},{8,9},{9,8},{10,11... | collective-permute-start | bytes 786440 | tf_op jit(solution)/shard_map/ppermute | solution.py:284
  98.8 1.3 %collective-permute-start.38 = (f32[128,512]{1,0:T(8,128)S(1)}, f32[128,512]{1,0:T(8,128)S(1)}, u32[]{:S(2)}, u32[]{:S(2)}) collective-permute-start(f32[128,512]{1,0:T(8,128)S(1)} %get-tuple-element.100), channel_id=1, source_target_pairs={{0,1},{1,0},{2,3},{3,2},{4,5},{5,4},{6,7},{7,6},{8,9},{9,8},{10,11... | collective-permute-start | bytes 786440 | tf_op jit(solution)/shard_map/ppermute | solution.py:284
  100.1 1.9 %shard_map.52 = (f32[256,256]{1,0:T(8,128)S(1)}, f32[256,256]{1,0:T(8,128)S(1)}, f32[128,512]{1,0:T(8,128)S(1)}, f32[128,512]{1,0:T(8,128)S(1)}) custom-call(s32[17]{0:T(128)S(1)} %fusion.10.table, bf16[512,384]{1,0:T(8,128)(2,1)S(1)} %get-tuple-element.89.refs_0_, bf16[512,384]{1,0:T(8,128)(2,1)S(1)} %get-tuple-element.90.refs_1_, ...), custom_call_target="tpu_custom_call" | custom-call | flops 603979776 | bytes 4718592 | tf_op jit(solution)/shard_map/pallas_call | solution.py:50
  102.0 3.2 %collective-permute-done.29 = f32[256,256]{1,0:T(8,128)S(1)} collective-permute-done((f32[256,256]{1,0:T(8,128)S(1)}, f32[256,256]{1,0:T(8,128)S(1)}, u32[]{:S(2)}, u32[]{:S(2)}) %collective-permute-start.29) | collective-permute-done | bytes 262176 | tf_op jit(solution)/shard_map/ppermute | solution.py:281
  106.1 1.3 %collective-permute-start.32 = (f32[128,256]{1,0:T(8,128)S(1)}, f32[128,256]{1,0:T(8,128)S(1)}, u32[]{:S(2)}, u32[]{:S(2)}) collective-permute-start(f32[128,256]{1,0:T(8,128)S(1)} %slice.149), channel_id=1, source_target_pairs={{0,16},{8,24},{16,0},{24,8},{1,17},{9,25},{17,1},{25,9},{2,18},{10... | collective-permute-start | bytes 393224 | tf_op jit(solution)/shard_map/ppermute | solution.py:281
  107.4 3.4 %collective-permute-done.36 = f32[256,256]{1,0:T(8,128)S(1)} collective-permute-done((f32[256,256]{1,0:T(8,128)S(1)}, f32[256,256]{1,0:T(8,128)S(1)}, u32[]{:S(2)}, u32[]{:S(2)}) %collective-permute-start.36) | collective-permute-done | bytes 262176 | tf_op jit(solution)/shard_map/ppermute | solution.py:281
  111.7 1.3 %collective-permute-start.39 = (f32[128,256]{1,0:T(8,128)S(1)}, f32[128,256]{1,0:T(8,128)S(1)}, u32[]{:S(2)}, u32[]{:S(2)}) collective-permute-start(f32[128,256]{1,0:T(8,128)S(1)} %slice.159), channel_id=1, source_target_pairs={{0,16},{8,24},{16,0},{24,8},{1,17},{9,25},{17,1},{25,9},{2,18},{10... | collective-permute-start | bytes 393224 | tf_op jit(solution)/shard_map/ppermute | solution.py:281
  113.0 1.0 collective-permute-done.30
  114.2 3.5 %collective-permute-start.35 = (f32[32,512]{1,0:T(8,128)S(1)}, f32[32,512]{1,0:T(8,128)S(1)}, u32[]{:S(2)}, u32[]{:S(2)}) collective-permute-start(f32[32,512]{1,0:T(8,128)S(1)} %get-tuple-element.121), channel_id=1, source_target_pairs={{0,6},{1,7},{2,4},{3,5},{4,2},{5,3},{6,0},{7,1},{8,14},{9,15},{10,... | collective-permute-start | bytes 196616 | tf_op jit(solution)/shard_map/ppermute | solution.py:284
  118.7 3.5 %collective-permute-start.42 = (f32[32,512]{1,0:T(8,128)S(1)}, f32[32,512]{1,0:T(8,128)S(1)}, u32[]{:S(2)}, u32[]{:S(2)}) collective-permute-start(f32[32,512]{1,0:T(8,128)S(1)} %get-tuple-element.117), channel_id=1, source_target_pairs={{0,6},{1,7},{2,4},{3,5},{4,2},{5,3},{6,0},{7,1},{8,14},{9,15},{10,... | collective-permute-start | bytes 196616 | tf_op jit(solution)/shard_map/ppermute | solution.py:284
  122.2 1.1 collective-permute-start.41
  124.0 2.1 %collective-permute-done.34.refs_2_ = f32[32,512]{1,0:T(8,128)S(1)} collective-permute-done((f32[32,512]{1,0:T(8,128)S(1)}, f32[32,512]{1,0:T(8,128)S(1)}, u32[]{:S(2)}, u32[]{:S(2)}) %collective-permute-start.34) | collective-permute-done | bytes 65568 | tf_op jit(solution)/shard_map/ppermute | solution.py:284
  126.0 1.1 collective-permute-done.40.refs_5_
  128.5 1.2 collective-permute-done.43.other_ref
  129.8 1.3 shard_map.54
  (95 shorter events, 16.3 us)
Async XLA Ops:
  0.0 11.3 %copy-start = (f32[1024,256]{1,0:T(8,128)S(1)}, f32[1024,256]{1,0:T(8,128)}, u32[]{:S(2)}) copy-start(f32[1024,256]{1,0:T(8,128)} %refs_2_.3) | copy-start | bytes 3145732
  0.0 11.3 %collective-permute-start.1 = (f32[1024,256]{1,0:T(8,128)}, f32[1024,256]{1,0:T(8,128)S(1)}, u32[]{:S(2)}, u32[]{:S(2)}) collective-permute-start(f32[1024,256]{1,0:T(8,128)} %refs_2_.3), channel_id=1, source_target_pairs={{0,8},{8,0},{16,24},{24,16},{1,9},{9,1},{17,25},{25,17},{2,10},{10... | collective-permute-start | bytes 3145736 | tf_op jit(solution)/shard_map/ppermute | solution.py:281
  0.5 28.0 %collective-permute-start = (f32[1024,256]{1,0:T(8,128)}, f32[1024,256]{1,0:T(8,128)S(1)}, u32[]{:S(2)}, u32[]{:S(2)}) collective-permute-start(f32[1024,256]{1,0:T(8,128)} %refs_2_.3), channel_id=1, source_target_pairs={{0,16},{8,24},{16,0},{24,8},{1,17},{9,25},{17,1},{25,9},{2,18},{10... | collective-permute-start | bytes 3145736 | tf_op jit(solution)/shard_map/ppermute | solution.py:281
  4.1 5.2 %collective-permute-start.3 = (f32[64,256]{1,0:T(8,128)S(1)}, f32[64,256]{1,0:T(8,128)S(1)}, u32[]{:S(2)}, u32[]{:S(2)}) collective-permute-start(f32[64,256]{1,0:T(8,128)S(1)} %dynamic-slice_bitcast_fusion), channel_id=1, source_target_pairs={{0,8},{8,0},{16,24},{24,16},{1,9},{9,1},{17,25},{25,17},{2,10},{10... | collective-permute-start | bytes 196616 | tf_op jit(solution)/shard_map/ppermute | solution.py:281
  6.8 8.9 %slice-start = ((s8[6291456]{0:T(1024)(128)(4,1)}), s8[4194304]{0:T(1024)(128)(4,1)S(1)}, s32[]{:S(2)}) async-start(s8[6291456]{0:T(1024)(128)(4,1)} %bitcast.25), calls=%async_computation | async-start | bytes 8388608
  9.3 11.6 %collective-permute-start.5 = (f32[64,512]{1,0:T(8,128)S(1)}, f32[64,512]{1,0:T(8,128)S(1)}, u32[]{:S(2)}, u32[]{:S(2)}) collective-permute-start(f32[64,512]{1,0:T(8,128)S(1)} %pad_maximum_fusion.3), channel_id=1, source_target_pairs={{0,1},{2,0},{4,2},{6,4},{7,6},{5,7},{3,5},{1,3},{8,10},{10,12},{12... | collective-permute-start | bytes 393224 | tf_op jit(solution)/shard_map/ppermute | solution.py:329
  10.8 10.0 %collective-permute-start.4 = (f32[64,512]{1,0:T(8,128)S(1)}, f32[64,512]{1,0:T(8,128)S(1)}, u32[]{:S(2)}, u32[]{:S(2)}) collective-permute-start(f32[64,512]{1,0:T(8,128)S(1)} %pad_maximum_fusion.3), channel_id=1, source_target_pairs={{0,2},{2,4},{4,6},{6,7},{7,5},{5,3},{3,1},{1,0},{8,9},{10,8},{12,1... | collective-permute-start | bytes 393224 | tf_op jit(solution)/shard_map/ppermute | solution.py:327
  11.4 4.4 %slice-start.1 = ((s8[6291456]{0:T(1024)(128)(4,1)}), s8[2097152]{0:T(1024)(128)(4,1)S(1)}, s32[]{:S(2)}) async-start(s8[6291456]{0:T(1024)(128)(4,1)} %bitcast.25), calls=%async_computation.1 | async-start | bytes 4194304
  13.6 11.9 %collective-permute-start.6 = (f32[192,512]{1,0:T(8,128)S(1)}, f32[192,512]{1,0:T(8,128)S(1)}, u32[]{:S(2)}, u32[]{:S(2)}) collective-permute-start(f32[192,512]{1,0:T(8,128)S(1)} %get-tuple-element.115), channel_id=1, source_target_pairs={{0,1},{2,0},{4,2},{6,4},{7,6},{5,7},{3,5},{1,3},{8,10},{10,12},{12... | collective-permute-start | bytes 1179656 | tf_op jit(solution)/shard_map/ppermute | solution.py:309
  15.2 10.4 %collective-permute-start.2 = (f32[192,512]{1,0:T(8,128)S(1)}, f32[192,512]{1,0:T(8,128)S(1)}, u32[]{:S(2)}, u32[]{:S(2)}) collective-permute-start(f32[192,512]{1,0:T(8,128)S(1)} %get-tuple-element.116), channel_id=1, source_target_pairs={{0,2},{2,4},{4,6},{6,7},{7,5},{5,3},{3,1},{1,0},{8,9},{10,8},{12,1... | collective-permute-start | bytes 1179656 | tf_op jit(solution)/shard_map/ppermute | solution.py:309
  20.9 6.4 %collective-permute-start.7 = (f32[64,512]{1,0:T(8,128)S(1)}, f32[64,512]{1,0:T(8,128)S(1)}, u32[]{:S(2)}, u32[]{:S(2)}) collective-permute-start(f32[64,512]{1,0:T(8,128)S(1)} %collective-permute-done.4), channel_id=1, source_target_pairs={{0,2},{2,4},{4,6},{6,7},{7,5},{5,3},{3,1},{1,0},{8,9},{10,8},{12,1... | collective-permute-start | bytes 393224 | tf_op jit(solution)/shard_map/ppermute | solution.py:327
  22.5 6.0 %collective-permute-start.8 = (f32[64,512]{1,0:T(8,128)S(1)}, f32[64,512]{1,0:T(8,128)S(1)}, u32[]{:S(2)}, u32[]{:S(2)}) collective-permute-start(f32[64,512]{1,0:T(8,128)S(1)} %collective-permute-done.5), channel_id=1, source_target_pairs={{0,1},{2,0},{4,2},{6,4},{7,6},{5,7},{3,5},{1,3},{8,10},{10,12},{12... | collective-permute-start | bytes 393224 | tf_op jit(solution)/shard_map/ppermute | solution.py:329
  28.5 2.7 %collective-permute-start.9 = (f32[1024,256]{1,0:T(8,128)S(1)}, f32[1024,256]{1,0:T(8,128)S(1)}, u32[]{:S(2)}, u32[]{:S(2)}) collective-permute-start(f32[1024,256]{1,0:T(8,128)S(1)} %collective-permute-done.refs_2_), channel_id=1, source_target_pairs={{0,8},{8,0},{16,24},{24,16},{1,9},{9,1},{17,25},{25,17},{2,10},{10... | collective-permute-start | bytes 3145736 | tf_op jit(solution)/shard_map/ppermute | solution.py:281
  28.6 8.8 %collective-permute-start.21 = (f32[192,512]{1,0:T(8,128)S(1)}, f32[192,512]{1,0:T(8,128)S(1)}, u32[]{:S(2)}, u32[]{:S(2)}) collective-permute-start(f32[192,512]{1,0:T(8,128)S(1)} %get-tuple-element.71), channel_id=1, source_target_pairs={{0,2},{2,4},{4,6},{6,7},{7,5},{5,3},{3,1},{1,0},{8,9},{10,8},{12,1... | collective-permute-start | bytes 1179656 | tf_op jit(solution)/shard_map/ppermute | solution.py:309
  33.5 16.9 %collective-permute-start.11 = (f32[192,512]{1,0:T(8,128)S(1)}, f32[192,512]{1,0:T(8,128)S(1)}, u32[]{:S(2)}, u32[]{:S(2)}) collective-permute-start(f32[192,512]{1,0:T(8,128)S(1)} %get-tuple-element.113), channel_id=1, source_target_pairs={{0,1},{2,0},{4,2},{6,4},{7,6},{5,7},{3,5},{1,3},{8,10},{10,12},{12... | collective-permute-start | bytes 1179656 | tf_op jit(solution)/shard_map/ppermute | solution.py:309
  34.1 16.9 %collective-permute-start.10 = (f32[192,512]{1,0:T(8,128)S(1)}, f32[192,512]{1,0:T(8,128)S(1)}, u32[]{:S(2)}, u32[]{:S(2)}) collective-permute-start(f32[192,512]{1,0:T(8,128)S(1)} %get-tuple-element.114), channel_id=1, source_target_pairs={{0,2},{2,4},{4,6},{6,7},{7,5},{5,3},{3,1},{1,0},{8,9},{10,8},{12,1... | collective-permute-start | bytes 1179656 | tf_op jit(solution)/shard_map/ppermute | solution.py:309
  35.6 17.0 %collective-permute-start.12 = (f32[5,64,512]{2,1,0:T(8,128)S(1)}, f32[5,64,512]{2,1,0:T(8,128)S(1)}, u32[]{:S(2)}, u32[]{:S(2)}) collective-permute-start(f32[5,64,512]{2,1,0:T(8,128)S(1)} %bitcast_dynamic-update-slice_fusion), channel_id=1, source_target_pairs={{0,16},{8,24},{16,0},{24,8},{1,17},{9,25},{17,1},{25,9},{2,18},{10... | collective-permute-start | bytes 1966088 | tf_op jit(solution)/shard_map/ppermute | solution.py:281
  35.9 26.4 %collective-permute-start.24 = (f32[192,512]{1,0:T(8,128)S(1)}, f32[192,512]{1,0:T(8,128)S(1)}, u32[]{:S(2)}, u32[]{:S(2)}) collective-permute-start(f32[192,512]{1,0:T(8,128)S(1)} %get-tuple-element.72), channel_id=1, source_target_pairs={{0,1},{2,0},{4,2},{6,4},{7,6},{5,7},{3,5},{1,3},{8,10},{10,12},{12... | collective-permute-start | bytes 1179656 | tf_op jit(solution)/shard_map/ppermute | solution.py:309
  37.4 11.6 %collective-permute-start.15 = (f32[64,512]{1,0:T(8,128)S(1)}, f32[64,512]{1,0:T(8,128)S(1)}, u32[]{:S(2)}, u32[]{:S(2)}) collective-permute-start(f32[64,512]{1,0:T(8,128)S(1)} %collective-permute-done.7), channel_id=1, source_target_pairs={{0,2},{2,4},{4,6},{6,7},{7,5},{5,3},{3,1},{1,0},{8,9},{10,8},{12,1... | collective-permute-start | bytes 393224 | tf_op jit(solution)/shard_map/ppermute | solution.py:327
  48.9 13.4 %collective-permute-start.22 = (f32[192,512]{1,0:T(8,128)S(1)}, f32[192,512]{1,0:T(8,128)S(1)}, u32[]{:S(2)}, u32[]{:S(2)}) collective-permute-start(f32[192,512]{1,0:T(8,128)S(1)} %slice_add_fusion.8), channel_id=1, source_target_pairs={{0,2},{2,4},{4,6},{6,7},{7,5},{5,3},{3,1},{1,0},{8,9},{10,8},{12,1... | collective-permute-start | bytes 1179656 | tf_op jit(solution)/shard_map/ppermute | solution.py:309
  50.4 6.4 %collective-permute-start.17 = (f32[64,512]{1,0:T(8,128)S(1)}, f32[64,512]{1,0:T(8,128)S(1)}, u32[]{:S(2)}, u32[]{:S(2)}) collective-permute-start(f32[64,512]{1,0:T(8,128)S(1)} %collective-permute-done.8), channel_id=1, source_target_pairs={{0,1},{2,0},{4,2},{6,4},{7,6},{5,7},{3,5},{1,3},{8,10},{10,12},{12... | collective-permute-start | bytes 393224 | tf_op jit(solution)/shard_map/ppermute | solution.py:329
  51.0 10.0 %collective-permute-start.16 = (f32[64,512]{1,0:T(8,128)S(1)}, f32[64,512]{1,0:T(8,128)S(1)}, u32[]{:S(2)}, u32[]{:S(2)}) collective-permute-start(f32[64,512]{1,0:T(8,128)S(1)} %collective-permute-done.15), channel_id=1, source_target_pairs={{0,2},{2,4},{4,6},{6,7},{7,5},{5,3},{3,1},{1,0},{8,9},{10,8},{12,1... | collective-permute-start | bytes 393224 | tf_op jit(solution)/shard_map/ppermute | solution.py:327
  52.6 16.8 %collective-permute-start.13 = (f32[192,512]{1,0:T(8,128)S(1)}, f32[192,512]{1,0:T(8,128)S(1)}, u32[]{:S(2)}, u32[]{:S(2)}) collective-permute-start(f32[192,512]{1,0:T(8,128)S(1)} %get-tuple-element.64), channel_id=1, source_target_pairs={{0,2},{2,4},{4,6},{6,7},{7,5},{5,3},{3,1},{1,0},{8,9},{10,8},{12,1... | collective-permute-start | bytes 1179656 | tf_op jit(solution)/shard_map/ppermute | solution.py:309
  56.8 12.6 %collective-permute-start.14 = (f32[192,512]{1,0:T(8,128)S(1)}, f32[192,512]{1,0:T(8,128)S(1)}, u32[]{:S(2)}, u32[]{:S(2)}) collective-permute-start(f32[192,512]{1,0:T(8,128)S(1)} %get-tuple-element.65), channel_id=1, source_target_pairs={{0,1},{2,0},{4,2},{6,4},{7,6},{5,7},{3,5},{1,3},{8,10},{10,12},{12... | collective-permute-start | bytes 1179656 | tf_op jit(solution)/shard_map/ppermute | solution.py:309
  61.0 8.7 %collective-permute-start.18 = (f32[3,64,512]{2,1,0:T(8,128)S(1)}, f32[3,64,512]{2,1,0:T(8,128)S(1)}, u32[]{:S(2)}, u32[]{:S(2)}) collective-permute-start(f32[3,64,512]{2,1,0:T(8,128)S(1)} %pad_maximum_fusion.2), channel_id=1, source_target_pairs={{0,16},{8,24},{16,0},{24,8},{1,17},{9,25},{17,1},{25,9},{2,18},{10... | collective-permute-start | bytes 1179656 | tf_op jit(solution)/shard_map/ppermute | solution.py:281
  62.5 14.8 %collective-permute-start.25 = (f32[192,512]{1,0:T(8,128)S(1)}, f32[192,512]{1,0:T(8,128)S(1)}, u32[]{:S(2)}, u32[]{:S(2)}) collective-permute-start(f32[192,512]{1,0:T(8,128)S(1)} %get-tuple-element.105), channel_id=1, source_target_pairs={{0,1},{2,0},{4,2},{6,4},{7,6},{5,7},{3,5},{1,3},{8,10},{10,12},{12... | collective-permute-start | bytes 1179656 | tf_op jit(solution)/shard_map/ppermute | solution.py:309
  65.4 11.9 %collective-permute-start.23 = (f32[192,512]{1,0:T(8,128)S(1)}, f32[192,512]{1,0:T(8,128)S(1)}, u32[]{:S(2)}, u32[]{:S(2)}) collective-permute-start(f32[192,512]{1,0:T(8,128)S(1)} %get-tuple-element.106), channel_id=1, source_target_pairs={{0,2},{2,4},{4,6},{6,7},{7,5},{5,3},{3,1},{1,0},{8,9},{10,8},{12,1... | collective-permute-start | bytes 1179656 | tf_op jit(solution)/shard_map/ppermute | solution.py:353
  69.7 10.0 %collective-permute-start.19 = (f32[192,512]{1,0:T(8,128)S(1)}, f32[192,512]{1,0:T(8,128)S(1)}, u32[]{:S(2)}, u32[]{:S(2)}) collective-permute-start(f32[192,512]{1,0:T(8,128)S(1)} %get-tuple-element.70), channel_id=1, source_target_pairs={{0,2},{2,4},{4,6},{6,7},{7,5},{5,3},{3,1},{1,0},{8,9},{10,8},{12,1... | collective-permute-start | bytes 1179656 | tf_op jit(solution)/shard_map/ppermute | solution.py:309
  77.4 4.6 %collective-permute-start.26 = (f32[192,512]{1,0:T(8,128)S(1)}, f32[192,512]{1,0:T(8,128)S(1)}, u32[]{:S(2)}, u32[]{:S(2)}) collective-permute-start(f32[192,512]{1,0:T(8,128)S(1)} %add_add_fusion.refs_0_), channel_id=1, source_target_pairs={{0,8},{8,0},{16,24},{24,16},{1,9},{9,1},{17,25},{25,17},{2,10},{10... | collective-permute-start | bytes 1179656 | tf_op jit(solution)/shard_map/ppermute | solution.py:281
  79.7 11.3 %collective-permute-start.20 = (f32[192,512]{1,0:T(8,128)S(1)}, f32[192,512]{1,0:T(8,128)S(1)}, u32[]{:S(2)}, u32[]{:S(2)}) collective-permute-start(f32[192,512]{1,0:T(8,128)S(1)} %slice_add_fusion.1), channel_id=1, source_target_pairs={{0,2},{2,4},{4,6},{6,7},{7,5},{5,3},{3,1},{1,0},{8,9},{10,8},{12,1... | collective-permute-start | bytes 1179656 | tf_op jit(solution)/shard_map/ppermute | solution.py:377
  81.4 9.6 %collective-permute-start.27 = (f32[192,512]{1,0:T(8,128)S(1)}, f32[192,512]{1,0:T(8,128)S(1)}, u32[]{:S(2)}, u32[]{:S(2)}) collective-permute-start(f32[192,512]{1,0:T(8,128)S(1)} %get-tuple-element.88), channel_id=1, source_target_pairs={{0,1},{2,0},{4,2},{6,4},{7,6},{5,7},{3,5},{1,3},{8,10},{10,12},{12... | collective-permute-start | bytes 1179656 | tf_op jit(solution)/shard_map/ppermute | solution.py:309
  91.1 1.8 %collective-permute-start.28 = (f32[192,512]{1,0:T(8,128)S(1)}, f32[192,512]{1,0:T(8,128)S(1)}, u32[]{:S(2)}, u32[]{:S(2)}) collective-permute-start(f32[192,512]{1,0:T(8,128)S(1)} %fusion.refs_5_), channel_id=1, source_target_pairs={{0,8},{8,0},{16,24},{24,16},{1,9},{9,1},{17,25},{25,17},{2,10},{10... | collective-permute-start | bytes 1179656 | tf_op jit(solution)/shard_map/ppermute | solution.py:281
  96.0 9.2 %collective-permute-start.29 = (f32[256,256]{1,0:T(8,128)S(1)}, f32[256,256]{1,0:T(8,128)S(1)}, u32[]{:S(2)}, u32[]{:S(2)}) collective-permute-start(f32[256,256]{1,0:T(8,128)S(1)} %get-tuple-element.94), channel_id=1, source_target_pairs={{0,16},{8,24},{16,0},{24,8},{1,17},{9,25},{17,1},{25,9},{2,18},{10... | collective-permute-start | bytes 786440 | tf_op jit(solution)/shard_map/ppermute | solution.py:281
  96.6 9.4 %collective-permute-start.31 = (f32[128,512]{1,0:T(8,128)S(1)}, f32[128,512]{1,0:T(8,128)S(1)}, u32[]{:S(2)}, u32[]{:S(2)}) collective-permute-start(f32[128,512]{1,0:T(8,128)S(1)} %get-tuple-element.96), channel_id=1, source_target_pairs={{0,1},{1,0},{2,3},{3,2},{4,5},{5,4},{6,7},{7,6},{8,9},{9,8},{10,11... | collective-permute-start | bytes 786440 | tf_op jit(solution)/shard_map/ppermute | solution.py:284
  97.9 12.9 %collective-permute-start.36 = (f32[256,256]{1,0:T(8,128)S(1)}, f32[256,256]{1,0:T(8,128)S(1)}, u32[]{:S(2)}, u32[]{:S(2)}) collective-permute-start(f32[256,256]{1,0:T(8,128)S(1)} %get-tuple-element.98), channel_id=1, source_target_pairs={{0,16},{8,24},{16,0},{24,8},{1,17},{9,25},{17,1},{25,9},{2,18},{10... | collective-permute-start | bytes 786440 | tf_op jit(solution)/shard_map/ppermute | solution.py:281
  98.8 12.9 %collective-permute-start.38 = (f32[128,512]{1,0:T(8,128)S(1)}, f32[128,512]{1,0:T(8,128)S(1)}, u32[]{:S(2)}, u32[]{:S(2)}) collective-permute-start(f32[128,512]{1,0:T(8,128)S(1)} %get-tuple-element.100), channel_id=1, source_target_pairs={{0,1},{1,0},{2,3},{3,2},{4,5},{5,4},{6,7},{7,6},{8,9},{9,8},{10,11... | collective-permute-start | bytes 786440 | tf_op jit(solution)/shard_map/ppermute | solution.py:284
  105.3 8.8 %collective-permute-start.30 = (f32[128,256]{1,0:T(8,128)S(1)}, f32[128,256]{1,0:T(8,128)S(1)}, u32[]{:S(2)}, u32[]{:S(2)}) collective-permute-start(f32[128,256]{1,0:T(8,128)S(1)} %slice.147), channel_id=1, source_target_pairs={{0,1},{1,0},{2,3},{3,2},{4,5},{5,4},{6,7},{7,6},{8,9},{9,8},{10,11... | collective-permute-start | bytes 393224 | tf_op jit(solution)/shard_map/ppermute | solution.py:284
  106.1 8.0 %collective-permute-start.32 = (f32[128,256]{1,0:T(8,128)S(1)}, f32[128,256]{1,0:T(8,128)S(1)}, u32[]{:S(2)}, u32[]{:S(2)}) collective-permute-start(f32[128,256]{1,0:T(8,128)S(1)} %slice.149), channel_id=1, source_target_pairs={{0,16},{8,24},{16,0},{24,8},{1,17},{9,25},{17,1},{25,9},{2,18},{10... | collective-permute-start | bytes 393224 | tf_op jit(solution)/shard_map/ppermute | solution.py:281
  110.9 7.7 %collective-permute-start.37 = (f32[128,256]{1,0:T(8,128)S(1)}, f32[128,256]{1,0:T(8,128)S(1)}, u32[]{:S(2)}, u32[]{:S(2)}) collective-permute-start(f32[128,256]{1,0:T(8,128)S(1)} %slice.157), channel_id=1, source_target_pairs={{0,1},{1,0},{2,3},{3,2},{4,5},{5,4},{6,7},{7,6},{8,9},{9,8},{10,11... | collective-permute-start | bytes 393224 | tf_op jit(solution)/shard_map/ppermute | solution.py:284
  111.7 6.9 %collective-permute-start.39 = (f32[128,256]{1,0:T(8,128)S(1)}, f32[128,256]{1,0:T(8,128)S(1)}, u32[]{:S(2)}, u32[]{:S(2)}) collective-permute-start(f32[128,256]{1,0:T(8,128)S(1)} %slice.159), channel_id=1, source_target_pairs={{0,16},{8,24},{16,0},{24,8},{1,17},{9,25},{17,1},{25,9},{2,18},{10... | collective-permute-start | bytes 393224 | tf_op jit(solution)/shard_map/ppermute | solution.py:281
  114.2 8.1 %collective-permute-start.35 = (f32[32,512]{1,0:T(8,128)S(1)}, f32[32,512]{1,0:T(8,128)S(1)}, u32[]{:S(2)}, u32[]{:S(2)}) collective-permute-start(f32[32,512]{1,0:T(8,128)S(1)} %get-tuple-element.121), channel_id=1, source_target_pairs={{0,6},{1,7},{2,4},{3,5},{4,2},{5,3},{6,0},{7,1},{8,14},{9,15},{10,... | collective-permute-start | bytes 196616 | tf_op jit(solution)/shard_map/ppermute | solution.py:284
  117.7 6.3 %collective-permute-start.33 = (f32[32,512]{1,0:T(8,128)S(1)}, f32[32,512]{1,0:T(8,128)S(1)}, u32[]{:S(2)}, u32[]{:S(2)}) collective-permute-start(f32[32,512]{1,0:T(8,128)S(1)} %get-tuple-element.123), channel_id=1, source_target_pairs={{0,2},{1,3},{2,0},{3,1},{4,6},{5,7},{6,4},{7,5},{8,10},{9,11},{10,... | collective-permute-start | bytes 196616 | tf_op jit(solution)/shard_map/ppermute | solution.py:284
  117.7 8.3 %collective-permute-start.34 = (f32[32,512]{1,0:T(8,128)S(1)}, f32[32,512]{1,0:T(8,128)S(1)}, u32[]{:S(2)}, u32[]{:S(2)}) collective-permute-start(f32[32,512]{1,0:T(8,128)S(1)} %get-tuple-element.124), channel_id=1, source_target_pairs={{0,4},{1,5},{2,6},{3,7},{4,0},{5,1},{6,2},{7,3},{8,12},{9,13},{10,... | collective-permute-start | bytes 196616 | tf_op jit(solution)/shard_map/ppermute | solution.py:284
  118.7 7.3 %collective-permute-start.42 = (f32[32,512]{1,0:T(8,128)S(1)}, f32[32,512]{1,0:T(8,128)S(1)}, u32[]{:S(2)}, u32[]{:S(2)}) collective-permute-start(f32[32,512]{1,0:T(8,128)S(1)} %get-tuple-element.117), channel_id=1, source_target_pairs={{0,6},{1,7},{2,4},{3,5},{4,2},{5,3},{6,0},{7,1},{8,14},{9,15},{10,... | collective-permute-start | bytes 196616 | tf_op jit(solution)/shard_map/ppermute | solution.py:284
  122.2 4.9 %collective-permute-start.40 = (f32[32,512]{1,0:T(8,128)S(1)}, f32[32,512]{1,0:T(8,128)S(1)}, u32[]{:S(2)}, u32[]{:S(2)}) collective-permute-start(f32[32,512]{1,0:T(8,128)S(1)} %get-tuple-element.119), channel_id=1, source_target_pairs={{0,2},{1,3},{2,0},{3,1},{4,6},{5,7},{6,4},{7,5},{8,10},{9,11},{10,... | collective-permute-start | bytes 196616 | tf_op jit(solution)/shard_map/ppermute | solution.py:284
  122.2 5.6 %collective-permute-start.41 = (f32[32,512]{1,0:T(8,128)S(1)}, f32[32,512]{1,0:T(8,128)S(1)}, u32[]{:S(2)}, u32[]{:S(2)}) collective-permute-start(f32[32,512]{1,0:T(8,128)S(1)} %get-tuple-element.120), channel_id=1, source_target_pairs={{0,4},{1,5},{2,6},{3,7},{4,0},{5,1},{6,2},{7,3},{8,12},{9,13},{10,... | collective-permute-start | bytes 196616 | tf_op jit(solution)/shard_map/ppermute | solution.py:284
  128.4 1.3 %collective-permute-start.43 = (f32[64,256]{1,0:T(8,128)S(1)}, f32[64,256]{1,0:T(8,128)S(1)}, u32[]{:S(2)}, u32[]{:S(2)}) collective-permute-start(f32[64,256]{1,0:T(8,128)S(1)} %get-tuple-element.102), channel_id=1, source_target_pairs={{0,8},{8,0},{16,24},{24,16},{1,9},{9,1},{17,25},{25,17},{2,10},{10... | collective-permute-start | bytes 196616 | tf_op jit(solution)/shard_map/ppermute | solution.py:281
